TPU v7x, 32 devices: a whole 2x2x4 slice. The times are simulated.
32 devices in a mesh: section: 4 (over z), row: 2 (over y), col: 4 (over x, core).
Axes of the slice: x: 2, y: 2, z: 4, core: 2. Of those that a mesh axis runs over, the one named last changes fastest.
Arguments:
- x_fwd: bfloat16 [1024, 12288], P('section', 'row'), may hold values from -6 to 6
- dy_bwd: bfloat16 [1024, 12288], P(('section', 'row'), 'col'), may hold values from -6 to 6
- w_blocks: bfloat16 [4, 2, 4, 460, 128, 128], P('section', 'row', 'col'), may hold values from -0.09375 to 0.09375
- blk_row: int32 [4, 2, 4, 460], P('section', 'row', 'col'), may hold values from 0 to 47, as said below
- blk_col: int32 [4, 2, 4, 460], P('section', 'row', 'col'), may hold values from 0 to 23, as said below
- blk_count: int32 [4, 2, 4], P('section', 'row', 'col'), may hold values from 230 to 460, as said below
- tok_count: int32 [4, 2], P('section'), may hold values from 64 to 256, as said below
- owner_order: int32 [4, 16], P('section'), may hold values from 0 to 15, each once within a row
Outputs:
- y_next: bfloat16 [1024, 12288], P(('section', 'row', 'col'))
- dx_section: bfloat16 [1024, 12288], P(('section', 'row', 'col'))
Inputs may be any that keep to these rules, and one draw needn't show every extreme that they name: At each grid position the slots below blk_count name distinct block positions (blk_row, blk_col); the other slots name arbitrary positions. `blk_col`: see blk_row. `blk_count`: some grid position of every draw holds exactly 460 live slots. `tok_count`: index 0 counts the forward micro-batch, index 1 the backward one; valid tokens come first; some entry of every draw equals 256. `owner_order`: each section's row is a permutation.
All inputs are finite; a program needn't handle non-finite values.
Results may differ from a plain program's by a relative error of at most 0.015.
Values may be sent and summed in bfloat16 or wider, within the bound.
No kernel may reach another device: no remote copies, remote signals or barrier semaphores. Data moves between devices by JAX's collectives and lax.ppermute only.
A program may use at most 192 MiB of HBM per device.

v0:
```python
import jax
import jax.numpy as jnp
from jax import lax
from jax.sharding import PartitionSpec as P


def passed_along(shard, axis, by):
    length = lax.axis_size(axis)
    pairs = [(i, i + by) for i in range(length) if 0 <= i + by < length]
    return lax.ppermute(shard, axis, pairs)


def local(x_fwd, dy_bwd, w_blocks, blk_row, blk_col, blk_count, tok_count, owner_order):
    row_count = lax.axis_size("row")
    col_count = lax.axis_size("col")
    token_total, in_width = x_fwd.shape
    out_width = dy_bwd.shape[1]
    slot_total = w_blocks.shape[3]
    block_size = w_blocks.shape[5]
    block_rows = in_width // block_size
    block_cols = out_width // block_size
    owned_rows = token_total // (row_count * col_count)
    weights = w_blocks.reshape(slot_total, block_size, block_size)
    live = (jnp.arange(slot_total) < blk_count.reshape(())).astype(weights.dtype)
    dense_blocks = jnp.zeros((block_rows, block_cols, block_size, block_size), weights.dtype)
    dense_blocks = dense_blocks.at[blk_row.reshape(slot_total), blk_col.reshape(slot_total)].add(
        weights * live[:, None, None]
    )
    dense_weight = jnp.transpose(dense_blocks, (0, 2, 1, 3)).reshape(in_width, out_width)
    limits = tok_count.reshape(2)
    block_total = owner_order.shape[1]
    block_length = token_total // block_total
    token_index = (
        owner_order.reshape(block_total)[:, None] * block_length + jnp.arange(block_length)[None, :]
    ).reshape(token_total)
    ordered_rows = jnp.take(x_fwd, token_index, axis=0)
    ordered_rows = jnp.where(
        (token_index < limits[0])[:, None], ordered_rows, jnp.zeros_like(ordered_rows)
    )
    partial_value = jnp.dot(ordered_rows, dense_weight, preferred_element_type=jnp.float32).astype(
        jnp.bfloat16
    )
    outgoing = partial_value.reshape(row_count * col_count, owned_rows, out_width)
    received = lax.all_to_all(outgoing, ("row", "col"), split_axis=0, concat_axis=2, tiled=True)
    summed = received.reshape(owned_rows, row_count, col_count * out_width).astype(jnp.float32)
    forward_act = jnp.sum(summed, axis=1).astype(jnp.bfloat16)
    y_next = passed_along(forward_act, "section", 1)
    grad_rows = dy_bwd.shape[0]
    grad_index = lax.axis_index("row") * grad_rows + jnp.arange(grad_rows)
    grad_kept = jnp.where((grad_index < limits[1])[:, None], dy_bwd, jnp.zeros_like(dy_bwd))
    grad_partial = lax.dot_general(
        lax.all_gather(grad_kept, "row", axis=0, tiled=True),
        dense_weight,
        (((1,), (1,)), ((), ())),
        preferred_element_type=jnp.float32,
    ).astype(jnp.bfloat16)
    grad_outgoing = grad_partial.reshape(row_count * col_count, owned_rows, in_width)
    grad_received = lax.all_to_all(
        grad_outgoing, ("row", "col"), split_axis=0, concat_axis=2, tiled=True
    )
    grad_summed = grad_received.reshape(owned_rows, row_count, col_count, in_width).astype(
        jnp.float32
    )
    dx_section = (
        jnp.sum(grad_summed, axis=2).reshape(owned_rows, row_count * in_width).astype(jnp.bfloat16)
    )
    return (y_next, dx_section)


def solution(mesh):
    return jax.shard_map(
        local,
        mesh=mesh,
        in_specs=(
            P("section", "row"),
            P(("section", "row"), "col"),
            P("section", "row", "col", None, None, None),
            P("section", "row", "col", None),
            P("section", "row", "col", None),
            P("section", "row", "col"),
            P("section", None),
            P("section", None),
        ),
        out_specs=(P(("section", "row", "col"), None), P(("section", "row", "col"), None)),
        check_vma=False,
    )
```

profile of v0, /device:TPU:0, one launch (start us, length us, event | category | flops | bytes accessed | tf_op | source)
XLA Modules:
  0.0 281.4 jit_solution(7760835393139049051)
XLA Ops:
  7.2 1.4 fusion.22
  8.6 0.7 add_compare_fusion
  9.3 2.1 broadcast_select_fusion
  11.5 0.7 multiply_bitcast_fusion
  13.0 0.7 or_select_fusion
  13.7 14.1 %bitcast_multiply_fusion = bf16[460,128,128]{2,1,0:T(8,128)(2,1)} fusion(bf16[1,1,1,460,128,128]{5,4,3,2,1,0:T(8,128)(2,1)} %param.10, bf16[460]{0:T(512)(128)(2,1)S(1)} %fusion.19), kind=kLoop, calls=%fused_computation.8 | loop fusion | flops 7536640 | bytes 30147480 | tf_op jit(solution)/shard_map/mul | solution.py:27
  27.8 12.5 %broadcast_in_dim.45 = bf16[48,24,128,128]{3,2,1,0:T(8,128)(2,1)} broadcast(bf16[]{:T(256)} %constant.9.clone.1), dimensions={} | broadcast | bytes 37748736 | tf_op jit(solution)/shard_map/broadcast_in_dim | solution.py:25
  40.4 96.5 %scatter_fusion = bf16[48,24,128,128]{3,2,1,0:T(8,128)(2,1)} fusion(bf16[48,24,128,128]{3,2,1,0:T(8,128)(2,1)} %broadcast_in_dim.45, s32[460]{0:T(512)S(1)} %bitcast.45, bf16[460,128,128]{2,1,0:T(8,128)(2,1)} %bitcast_multiply_fusion), kind=kCustom, calls=%fused_computation.1 | custom fusion | flops 7536640 | bytes 45223520 | tf_op jit(solution)/shard_map/scatter-add | solution.py:26
  136.9 40.8 %copy.15 = bf16[48,128,24,128]{3,2,1,0:T(8,128)(2,1)} copy(bf16[48,128,24,128]{3,1,2,0:T(8,128)(2,1)} %bitcast.42) | data formatting | bytes 75497472 | tf_op jit(solution)/shard_map/transpose | solution.py:29
  177.7 4.1 %gather_fusion = bf16[256,6144]{1,0:T(8,128)(2,1)} fusion(bf16[256,6144]{1,0:T(8,128)(2,1)S(1)} %copy-done, s32[1024]{0:T(1024)S(1)} %pad_clamp_fusion), kind=kCustom, calls=%fused_computation | custom fusion | bytes 6292480 | tf_op jit(solution)/shard_map/jit(_take)/gather | solution.py:36
  182.4 18.3 %fusion.9 = bf16[256,3072]{1,0:T(8,128)(2,1)} fusion(bf16[768,8,24,128]{3,2,1,0:T(8,128)(2,1)} %bitcast.43, bf16[256,6144]{1,0:T(8,128)(2,1)} %gather_fusion, pred[256]{0:T(512)(128)(4,1)S(1)} %get-tuple-element.3, pred[256]{0:T(512)(128)(4,1)S(1)} %get-tuple-element.2), kind=kOutput, calls=%fused_computation.10 | convolution fusion | flops 9667608576 | bytes 42467840 | tf_op jit(solution)/shard_map/dot_general | solution.py:40
  200.7 5.1 %all-to-all-start = ((bf16[8,32,3072]{2,1,0:T(8,128)(2,1)}), bf16[8,32,3072]{2,1,0:T(8,128)(2,1)S(1)}, u32[]{:S(2)}, u32[]{:S(2)}) async-start(bf16[8,32,3072]{2,1,0:T(8,128)(2,1)} %bitcast.9), calls=%async_computation | async-start | bytes 3145728 | tf_op jit(solution)/shard_map/all_to_all | solution.py:44
  205.9 18.3 %fusion.6 = bf16[256,6144]{1,0:T(8,128)(2,1)} fusion(bf16[256,3072]{1,0:T(8,128)(2,1)} %all-gather.2.cloned.1.call-done, bf16[768,8,24,128]{3,2,1,0:T(8,128)(2,1)} %bitcast.44), kind=kOutput, calls=%fused_computation.9 | convolution fusion | flops 9665249280 | bytes 42467328 | tf_op jit(solution)/shard_map/dot_general | solution.py:51
  224.1 2.7 all-to-all-done
  226.9 4.5 %all-to-all-start.1 = ((bf16[8,32,6144]{2,1,0:T(8,128)(2,1)}), bf16[8,32,6144]{2,1,0:T(8,128)(2,1)}, u32[]{:S(2)}, u32[]{:S(2)}) async-start(bf16[8,32,6144]{2,1,0:T(8,128)(2,1)} %bitcast.47), calls=%async_computation.1 | async-start | bytes 6291456 | tf_op jit(solution)/shard_map/all_to_all | solution.py:58
  231.3 0.9 copy.16
  232.2 1.9 reshape.169
  234.1 6.4 %reduce_sum.21 = bf16[32,12288]{1,0:T(8,128)(2,1)} reduce(bf16[32,2,12288]{2,1,0:T(2,128)(2,1)} %reshape.169, bf16[]{:T(256)} %constant.9.clone.1), dimensions={1}, to_apply=%region_1.2 | reduce | flops 393216 | bytes 2359298 | tf_op jit(solution)/shard_map/reduce_sum | solution.py:46
  240.5 4.5 %collective-permute-start = (bf16[32,12288]{1,0:T(8,128)(2,1)}, bf16[32,12288]{1,0:T(8,128)(2,1)}, u32[]{:S(2)}, u32[]{:S(2)}) collective-permute-start(bf16[32,12288]{1,0:T(8,128)(2,1)} %reduce_sum.21), channel_id=1, source_target_pairs={{0,8},{8,16},{16,24},{1,9},{9,17},{17,25},{2,10},{10,18},{18,26},{... | collective-permute-start | bytes 2359304 | tf_op jit(solution)/shard_map/ppermute | solution.py:10
  245.0 16.7 %collective-permute-done = bf16[32,12288]{1,0:T(8,128)(2,1)} collective-permute-done((bf16[32,12288]{1,0:T(8,128)(2,1)}, bf16[32,12288]{1,0:T(8,128)(2,1)}, u32[]{:S(2)}, u32[]{:S(2)}) %collective-permute-start) | collective-permute-done | bytes 786464 | tf_op jit(solution)/shard_map/ppermute | solution.py:10
  261.7 7.5 %all-to-all-done.1 = bf16[8,32,6144]{2,1,0:T(8,128)(2,1)} async-done(((bf16[8,32,6144]{2,1,0:T(8,128)(2,1)}), bf16[8,32,6144]{2,1,0:T(8,128)(2,1)}, u32[]{:S(2)}, u32[]{:S(2)}) %all-to-all-start.1) | async-done | bytes 3145760 | tf_op jit(solution)/shard_map/all_to_all | solution.py:58
  269.2 2.3 bitcast_reduce_fusion
  271.5 0.9 copy.18
  272.5 2.1 copy.35
  (14 shorter events, 1.0 us)
Async XLA Ops:
  7.2 170.5 %copy-start = (bf16[256,6144]{1,0:T(8,128)(2,1)S(1)}, bf16[256,6144]{1,0:T(8,128)(2,1)}, u32[]{:S(2)}) copy-start(bf16[256,6144]{1,0:T(8,128)(2,1)} %param.8) | copy-start | bytes 9437188
  7.2 198.7 %all-gather.2.cloned.1.call-start = ((), (), s32[]{:S(2)}) async-start(), calls=%async_computation.2 | async-start | bytes 2359296 | tf_op jit(solution)/shard_map/all_gather | solution.py:52
  200.7 26.2 %all-to-all-start = ((bf16[8,32,3072]{2,1,0:T(8,128)(2,1)}), bf16[8,32,3072]{2,1,0:T(8,128)(2,1)S(1)}, u32[]{:S(2)}, u32[]{:S(2)}) async-start(bf16[8,32,3072]{2,1,0:T(8,128)(2,1)} %bitcast.9), calls=%async_computation | async-start | bytes 3145728 | tf_op jit(solution)/shard_map/all_to_all | solution.py:44
  226.9 42.4 %all-to-all-start.1 = ((bf16[8,32,6144]{2,1,0:T(8,128)(2,1)}), bf16[8,32,6144]{2,1,0:T(8,128)(2,1)}, u32[]{:S(2)}, u32[]{:S(2)}) async-start(bf16[8,32,6144]{2,1,0:T(8,128)(2,1)} %bitcast.47), calls=%async_computation.1 | async-start | bytes 6291456 | tf_op jit(solution)/shard_map/all_to_all | solution.py:58
  234.1 40.4 %copy-start.1 = (bf16[256,6144]{1,0:T(8,128)(2,1)S(1)}, bf16[256,6144]{1,0:T(8,128)(2,1)}, u32[]{:S(2)}) copy-start(bf16[256,6144]{1,0:T(8,128)(2,1)} %param.8) | copy-start | bytes 9437188
  240.5 21.2 %collective-permute-start = (bf16[32,12288]{1,0:T(8,128)(2,1)}, bf16[32,12288]{1,0:T(8,128)(2,1)}, u32[]{:S(2)}, u32[]{:S(2)}) collective-permute-start(bf16[32,12288]{1,0:T(8,128)(2,1)} %reduce_sum.21), channel_id=1, source_target_pairs={{0,8},{8,16},{16,24},{1,9},{9,17},{17,25},{2,10},{10,18},{18,26},{... | collective-permute-start | bytes 2359304 | tf_op jit(solution)/shard_map/ppermute | solution.py:10
Sparse Core Ops, SparseCore 0:
  11.6 29.9 all-gather.1
where the time goes:
time: 283 us; the launch traced here: 281 us
  other arithmetic  124 us (44%)
  local copies, waits for them, and re-layouts  64.7 us (23%)
  matrix products  36.6 us (13%)
  waiting for transfers between devices  27 us (10%)
  between operations  14.8 us (5%)
  starting transfers between devices  14.1 us (5%)
    scatter-add x1, other arithmetic, local(): dense_blocks.at[blk_row.reshape(slot_total), blk_col.reshape(slot_total)]  96.5 us
    transpose x1, local copies, waits for them, and re-layouts, local(): jnp.transpose(dense_blocks, (0, 2, 1, 3)).reshape(in_width, out_width)  40.8 us
    dot_general x1, matrix products, local(): jnp.dot(ordered_rows, dense_weight, preferred_element_type=jnp.float32)  18.3 us
    dot_general x1, matrix products, local(): lax.dot_general(lax.all_gather(grad_kept, 'row', axis=0, tiled=True), den...  18.3 us
    ppermute x1, waiting for transfers between devices, passed_along(): return lax.ppermute(shard, axis, pairs)  16.7 us
    mul x1, other arithmetic, local(): weights * live[:, None, None]  14.1 us
    broadcast_in_dim x1, local copies, waits for them, and re-layouts, local(): jnp.zeros((block_rows, block_cols, block_size, block_size), weights.dtype)  12.5 us
    all_to_all x1, waiting for transfers between devices, local(): lax.all_to_all(grad_outgoing, ('row', 'col'), split_axis=0, concat_axis=2...  7.47 us
  transfers between devices with their start and end apart: 4, of which 3 were waited for; matrix products, arithmetic and copies ran while one was open for 77% of the time, Pallas kernels for 0%

commit v1 on v0

--- a/solution.py
+++ b/solution.py
@@ -1,7 +1,320 @@
+import functools
+
 import jax
 import jax.numpy as jnp
 from jax import lax
+from jax.experimental import pallas as pl
+from jax.experimental.pallas import tpu as pltpu
 from jax.sharding import PartitionSpec as P
+
+F_CHUNKS = (6, 6)
+B_CHUNKS = (6, 6, 6, 6)
+
+VMEM = pl.BlockSpec(memory_space=pltpu.VMEM)
+SMEM = pl.BlockSpec(memory_space=pltpu.SMEM)
+ANY = pl.BlockSpec(memory_space=pl.ANY)
+PARAMS = pltpu.CompilerParams(vmem_limit_bytes=40 * 2**20)
+
+
+def resident(x):
+    return pltpu.with_memory_space_constraint(x, pltpu.VMEM)
+
+
+def prep_kernel(owned, count, row, col, order, w_hbm, x_hbm, w_out, x_out, slot_of, w_sem, x_sem):
+    cap = w_hbm.shape[0]
+    block_cols = slot_of.shape[1]
+    w_copy = pltpu.make_async_copy(w_hbm, w_out.at[pl.ds(0, cap)], w_sem)
+    w_copy.start()
+    r, c = lax.axis_index("row"), lax.axis_index("col")
+    block = x_hbm.shape[0] // order.shape[0]
+    per_owner = owned // block
+    copies = []
+    at = 0
+    for dr in range(2):
+        for dc in range(4):
+            first = ((r ^ dr) * 4 + (c ^ dc)) * per_owner
+            for b in range(per_owner):
+                source = pl.multiple_of(order[first + b] * block, block)
+                copies.append(
+                    pltpu.make_async_copy(
+                        x_hbm.at[pl.ds(source, block)], x_out.at[pl.ds(at, block)], x_sem.at[len(copies)]
+                    )
+                )
+                copies[-1].start()
+                at += block
+    w_out[cap] = jnp.zeros(w_out.shape[1:], w_out.dtype)
+
+    @pl.loop(0, slot_of.shape[0])
+    def _(i):
+        for j in range(block_cols):
+            slot_of[i, j] = cap
+
+    live = count[0]
+
+    @pl.loop(0, live)
+    def _(k):
+        slot_of[row[k], col[k]] = k
+
+    for copy in copies:
+        copy.wait()
+    w_copy.wait()
+
+
+def prep(owned, block_cols, count, row, col, order, weights, x):
+    cap, size, _ = weights.shape
+    block_rows = x.shape[1] // size
+    return pl.pallas_call(
+        functools.partial(prep_kernel, owned),
+        out_shape=(
+            pltpu.VMEM((cap + 1, size, size), weights.dtype),
+            pltpu.VMEM(x.shape, x.dtype),
+            jax.ShapeDtypeStruct((block_rows, block_cols), jnp.int32),
+        ),
+        in_specs=[SMEM, SMEM, SMEM, SMEM, ANY, ANY],
+        out_specs=(VMEM, VMEM, SMEM),
+        scratch_shapes=[pltpu.SemaphoreType.DMA, pltpu.SemaphoreType.DMA((order.shape[0],))],
+        compiler_params=PARAMS,
+    )(count, row, col, order, weights, x)
+
+
+def forward_kernel(first, slot_of, x, w, keep, send):
+    half = keep.shape[0]
+    for j in range(keep.shape[1] // 256):
+        rhs = jnp.concatenate(
+            [
+                jnp.concatenate(
+                    [w[slot_of[i, 2 * (first + j)]], w[slot_of[i, 2 * (first + j) + 1]]], axis=1
+                )
+                for i in range(slot_of.shape[0])
+            ],
+            axis=0,
+        )
+        part = jnp.dot(x[...], rhs, preferred_element_type=jnp.float32).astype(keep.dtype)
+        keep[:, j * 256 : (j + 1) * 256] = part[:half]
+        send[:, j * 256 : (j + 1) * 256] = part[half:]
+
+
+def forward(first, pairs, slot_of, x, w):
+    shape = jax.ShapeDtypeStruct((x.shape[0] // 2, pairs * 256), x.dtype)
+    return pl.pallas_call(
+        functools.partial(forward_kernel, first),
+        out_shape=(shape, shape),
+        in_specs=[SMEM, VMEM, VMEM],
+        out_specs=(VMEM, VMEM),
+        compiler_params=PARAMS,
+        cost_estimate=pl.CostEstimate(
+            flops=2 * x.shape[0] * x.shape[1] * pairs * 256, bytes_accessed=2**20, transcendentals=0
+        ),
+    )(slot_of, resident(x), resident(w))
+
+
+def order_grad_kernel(own, other, out, sems):
+    c = lax.axis_index("col")
+    rows = own.shape[0] // 4
+    copies = []
+    for dk in range(2):
+        for dx in range(2):
+            for source in (own, other):
+                at = pl.multiple_of((c ^ (2 * dx + dk)) * rows, rows)
+                copies.append(
+                    pltpu.make_async_copy(
+                        source.at[pl.ds(at, rows)], out.at[pl.ds(len(copies) * rows, rows)], sems.at[len(copies)]
+                    )
+                )
+                copies[-1].start()
+    for copy in copies:
+        copy.wait()
+
+
+def order_grad(own, other):
+    rows, width = own.shape
+    return pl.pallas_call(
+        order_grad_kernel,
+        out_shape=pltpu.VMEM((2 * rows, width), own.dtype),
+        in_specs=[ANY, ANY],
+        out_specs=VMEM,
+        scratch_shapes=[pltpu.SemaphoreType.DMA((8,))],
+        compiler_params=PARAMS,
+    )(own, other)
+
+
+def backward_kernel(first, slot_of, dy, w, keep, send):
+    half = keep.shape[0]
+    for i in range(keep.shape[1] // 256):
+        rhs = jnp.concatenate(
+            [
+                jnp.concatenate(
+                    [w[slot_of[2 * (first + i), j]], w[slot_of[2 * (first + i) + 1, j]]], axis=0
+                )
+                for j in range(slot_of.shape[1])
+            ],
+            axis=1,
+        )
+        part = lax.dot_general(
+            dy[...], rhs, (((1,), (1,)), ((), ())), preferred_element_type=jnp.float32
+        ).astype(keep.dtype)
+        keep[:, i * 256 : (i + 1) * 256] = part[:half]
+        send[:, i * 256 : (i + 1) * 256] = part[half:]
+
+
+def backward(first, pairs, slot_of, dy, w):
+    shape = jax.ShapeDtypeStruct((dy.shape[0] // 2, pairs * 256), dy.dtype)
+    return pl.pallas_call(
+        functools.partial(backward_kernel, first),
+        out_shape=(shape, shape),
+        in_specs=[SMEM, VMEM, VMEM],
+        out_specs=(VMEM, VMEM),
+        compiler_params=PARAMS,
+        cost_estimate=pl.CostEstimate(
+            flops=2 * dy.shape[0] * dy.shape[1] * pairs * 256, bytes_accessed=2**20, transcendentals=0
+        ),
+    )(slot_of, resident(dy), resident(w))
+
+
+def sum_forward_kernel(block, order, limits, keep, received, *outs):
+    r, c = lax.axis_index("row"), lax.axis_index("col")
+    rows = outs[0].shape[0]
+    per_owner = rows // block
+    for dc, out in enumerate(outs):
+        first = (r * 4 + (c ^ dc)) * per_owner
+        for b in range(per_owner):
+            at = dc * rows + b * block
+            total = keep[at : at + block].astype(jnp.float32) + received[at : at + block].astype(jnp.float32)
+            token = order[first + b] * block + lax.broadcasted_iota(jnp.int32, total.shape, 0)
+            out[b * block : (b + 1) * block] = jnp.where(token < limits[0], total, 0.0).astype(out.dtype)
+
+
+def sum_forward(block, order, limits, keep, received):
+    rows, width = keep.shape
+    return pl.pallas_call(
+        functools.partial(sum_forward_kernel, block),
+        out_shape=(jax.ShapeDtypeStruct((rows // 4, width), keep.dtype),) * 4,
+        in_specs=[SMEM, SMEM, VMEM, VMEM],
+        out_specs=(VMEM,) * 4,
+        compiler_params=PARAMS,
+    )(order, limits, keep, received)
+
+
+def place_forward_kernel(*refs):
+    pieces, out, sems = refs[:-2], refs[-2], refs[-1]
+    c = lax.axis_index("col")
+    width = out.shape[1] // 4
+    copies = []
+    for dc in range(4):
+        at = (c ^ dc) * width
+        for piece in pieces[dc::4]:
+            copies.append(
+                pltpu.make_async_copy(
+                    piece, out.at[:, pl.ds(pl.multiple_of(at, 128), piece.shape[1])], sems.at[len(copies)]
+                )
+            )
+            copies[-1].start()
+            at += piece.shape[1]
+    for copy in copies:
+        copy.wait()
+
+
+def place_forward(pieces):
+    rows = pieces[0].shape[0]
+    width = sum(piece.shape[1] for piece in pieces)
+    return pl.pallas_call(
+        place_forward_kernel,
+        out_shape=jax.ShapeDtypeStruct((rows, width), pieces[0].dtype),
+        in_specs=[ANY] * len(pieces),
+        out_specs=ANY,
+        scratch_shapes=[pltpu.SemaphoreType.DMA((len(pieces),))],
+        compiler_params=PARAMS,
+    )(*pieces)
+
+
+def place_backward_kernel(limits, *refs):
+    pieces, out = refs[:-1], refs[-1]
+    r, c = lax.axis_index("row"), lax.axis_index("col")
+    rows = out.shape[0]
+    width = out.shape[1] // 2
+    for dr in range(2):
+        at = (r ^ dr) * width
+        for piece in pieces[dr::2]:
+            token = (r * 4 + c) * rows + lax.broadcasted_iota(jnp.int32, piece.shape, 0)
+            value = jnp.where(token < limits[1], piece[...].astype(jnp.float32), 0.0).astype(out.dtype)
+            out[:, pl.ds(pl.multiple_of(at, 128), piece.shape[1])] = value
+            at += piece.shape[1]
+
+
+def place_backward(limits, pieces):
+    rows = pieces[0].shape[0]
+    width = sum(piece.shape[1] for piece in pieces)
+    return pl.pallas_call(
+        place_backward_kernel,
+        out_shape=jax.ShapeDtypeStruct((rows, width), pieces[0].dtype),
+        in_specs=[SMEM] + [VMEM] * len(pieces),
+        out_specs=VMEM,
+        compiler_params=PARAMS,
+    )(limits, *pieces)
+
+
+def swap(x, axis, by):
+    return lax.ppermute(x, axis, [(i, i ^ by) for i in range(lax.axis_size(axis))])
+
+
+def deliver(x, by):
+    sections, rows, cols = lax.axis_size("section"), lax.axis_size("row"), lax.axis_size("col")
+    at = lambda s, r, c: (s * rows + r) * cols + c
+    pairs = [
+        (at(s, r, c), at(s + 1, r, c ^ by))
+        for s in range(sections - 1)
+        for r in range(rows)
+        for c in range(cols)
+    ]
+    return lax.ppermute(x, ("section", "row", "col"), pairs)
+
+
+def added(a, b):
+    return (a.astype(jnp.float32) + b.astype(jnp.float32)).astype(a.dtype)
+
+
+def grid_2x4(x_fwd, dy_bwd, w_blocks, blk_row, blk_col, blk_count, tok_count, owner_order):
+    token_total = x_fwd.shape[0]
+    owned = token_total // 8
+    slots, size = w_blocks.shape[3], w_blocks.shape[5]
+    order = owner_order.reshape(-1)
+    limits = tok_count.reshape(2)
+    dy_other = swap(dy_bwd, "row", 1)
+    w, x, slot_of = prep(
+        owned,
+        dy_bwd.shape[1] // size,
+        blk_count.reshape(1),
+        blk_row.reshape(slots),
+        blk_col.reshape(slots),
+        order,
+        w_blocks.reshape(slots, size, size),
+        x_fwd,
+    )
+    pieces = []
+    first = 0
+    for pairs in F_CHUNKS:
+        keep, send = forward(first, pairs, slot_of, x, w)
+        first += pairs
+        summed = sum_forward(token_total // order.shape[0], order, limits, keep, swap(send, "row", 1))
+        pieces += [deliver(summed[by], by) for by in range(4)]
+    y_next = place_forward(pieces)
+
+    dy = order_grad(dy_bwd, dy_other)
+    pieces = []
+    first = 0
+    for pairs in B_CHUNKS:
+        keep, send = backward(first, pairs, slot_of, dy, w)
+        first += pairs
+        received = swap(send, "col", 1)
+        half = keep.shape[0] // 2
+        onward = added(keep[half:], received[half:])
+        kept = added(keep[:half], received[:half])
+        received = swap(onward, "col", 2)
+        onward = added(kept[owned:], received[owned:])
+        kept = added(kept[:owned], received[:owned])
+        pieces += [kept, swap(onward, "row", 1)]
+    dx_section = place_backward(limits, pieces)
+    return y_next, dx_section
 
 
 def passed_along(shard, axis, by):
@@ -10,7 +323,7 @@
     return lax.ppermute(shard, axis, pairs)
 
 
-def local(x_fwd, dy_bwd, w_blocks, blk_row, blk_col, blk_count, tok_count, owner_order):
+def any_grid(x_fwd, dy_bwd, w_blocks, blk_row, blk_col, blk_count, tok_count, owner_order):
     row_count = lax.axis_size("row")
     col_count = lax.axis_size("col")
     token_total, in_width = x_fwd.shape
@@ -68,8 +381,9 @@
 
 
 def solution(mesh):
+    small = mesh.shape["row"] == 2 and mesh.shape["col"] == 4
     return jax.shard_map(
-        local,
+        grid_2x4 if small else any_grid,
         mesh=mesh,
         in_specs=(
             P("section", "row"),

time: 283 us -> 137 us (0.48)
  other arithmetic: 124 us -> 0.57 us
  local copies, waits for them, and re-layouts: 64.7 us -> 6.33 us
  Pallas kernels: 0 us -> 46.5 us
  matrix products: 36.6 us -> 0 us
  starting transfers between devices: 14.1 us -> 38.1 us
  waiting for transfers between devices: 27 us -> 43.1 us
  between operations: 14.8 us -> 1.55 us
    scatter-add x1 -> x0, other arithmetic: 96.5 us -> none  [local(): dense_blocks.at[blk_row.reshape(slot_total), blk_col.reshape(slot_total)]]
    pallas_call x0 -> x12, Pallas kernels: none -> 46.5 us  [the longest x4 18.4 us: backward(): pl.pallas_call(functools.partial(backward_kernel, first), out_shape=(shap...]
    transpose x1 -> x0, local copies, waits for them, and re-layouts: 40.8 us -> none  [local(): jnp.transpose(dense_blocks, (0, 2, 1, 3)).reshape(in_width, out_width)]
    dot_general x2 -> x0, matrix products: 36.6 us -> none  [the longest x1 18.3 us: local(): jnp.dot(ordered_rows, dense_weight, preferred_element_type=jnp.float32)]
    ppermute x1 -> x23, starting transfers between devices: 4.46 us -> 38.1 us  [the longest x8 24.9 us: deliver(): return lax.ppermute(x, ('section', 'row', 'col'), pairs)]
    ppermute x1 -> x23, waiting for transfers between devices: 16.7 us -> 43.1 us  [the longest x15 43 us: swap(): lax.ppermute(x, axis, [(i, i ^ by) for i in range(lax.axis_size(axis))])]
    mul x2 -> x0, other arithmetic: 14.8 us -> none  [the longest x1 14.1 us: local(): weights * live[:, None, None]]
    broadcast_in_dim x1 -> x0, local copies, waits for them, and re-layouts: 12.5 us -> none  [local(): jnp.zeros((block_rows, block_cols, block_size, block_size), weights.dtype)]
  transfers between devices with their start and end apart: 4 -> 23, of which waited for: 3 -> 13; matrix products, arithmetic and copies ran while one was open for 77% -> 0% of each run, Pallas kernels for 0% -> 22%
where the time goes in v1:
time: 137 us; the launch traced here: 136 us
  Pallas kernels  46.5 us (34%)
  waiting for transfers between devices  43.1 us (31%)
  starting transfers between devices  38.1 us (28%)
  local copies, waits for them, and re-layouts  6.33 us (5%)
  between operations  1.55 us (1%)
    ppermute x15, waiting for transfers between devices, swap(): lax.ppermute(x, axis, [(i, i ^ by) for i in range(lax.axis_size(axis))])  43 us
    ppermute x8, starting transfers between devices, deliver(): return lax.ppermute(x, ('section', 'row', 'col'), pairs)  24.9 us
    pallas_call x4, Pallas kernels, backward(): pl.pallas_call(functools.partial(backward_kernel, first), out_shape=(shap...  18.4 us
    pallas_call x2, Pallas kernels, forward(): pl.pallas_call(functools.partial(forward_kernel, first), out_shape=(shape...  14 us
    ppermute x15, starting transfers between devices, swap(): lax.ppermute(x, axis, [(i, i ^ by) for i in range(lax.axis_size(axis))])  13.2 us
    pallas_call x1, Pallas kernels, prep(): pl.pallas_call(functools.partial(prep_kernel, owned), out_shape=(pltpu.VM...  8.08 us
    unnamed x28, local copies, waits for them, and re-layouts  6.33 us
  transfers between devices with their start and end apart: 23, of which 13 were waited for; matrix products, arithmetic and copies ran while one was open for 0% of the time, Pallas kernels for 22%

profile of v1, /device:TPU:0, one launch (start us, length us, event | category | flops | bytes accessed | tf_op | source)
XLA Modules:
  0.0 136.1 jit_solution(2423356611321066361)
XLA Ops:
  1.3 8.1 %shard_map.95 = (bf16[461,128,128]{2,1,0:T(8,128)(2,1)S(1)}, bf16[256,6144]{1,0:T(8,128)(2,1)S(1)}, s32[48,24]{1,0:T(8,128)}) custom-call(s32[1]{0:T(128)} %bitcast.6.count, s32[460]{0:T(512)} %bitcast.14, s32[460]{0:T(512)} %bitcast.15, s32[16]{0:T(128)} %bitcast.7, bf16[460,128,128]{2,1,0:T(8,128)(2,1)} %bitcast.13, bf16[256,6144]{1,0:T(8,128)(2,1)} %x_hbm.1), custom_call_target="tpu_custom_call" | custom-call | tf_op jit(solution)/shard_map/pallas_call | solution.py:66
  9.4 7.1 %shard_map.96 = (bf16[128,1536]{1,0:T(8,128)(2,1)}, bf16[128,1536]{1,0:T(8,128)(2,1)}) custom-call(s32[48,24]{1,0:T(8,128)} %get-tuple-element.25.slot_of, bf16[256,6144]{1,0:T(8,128)(2,1)S(1)} %get-tuple-element.26.x, bf16[461,128,128]{2,1,0:T(8,128)(2,1)S(1)} %get-tuple-element.27.w), custom_call_target="tpu_custom_call" | custom-call | flops 4831838208 | bytes 1048576 | tf_op jit(solution)/shard_map/pallas_call | solution.py:99
  16.5 3.0 %collective-permute-start = (bf16[128,1536]{1,0:T(8,128)(2,1)}, bf16[128,1536]{1,0:T(8,128)(2,1)S(1)}, u32[]{:S(2)}, u32[]{:S(2)}) collective-permute-start(bf16[128,1536]{1,0:T(8,128)(2,1)} %get-tuple-element.29), channel_id=1, source_target_pairs={{0,4},{4,0},{1,5},{5,1},{2,6},{6,2},{3,7},{7,3},{8,12},{12,8},{9,1... | collective-permute-start | bytes 1179656 | tf_op jit(solution)/shard_map/ppermute | solution.py:257
  19.5 7.0 %shard_map.98 = (bf16[128,1536]{1,0:T(8,128)(2,1)}, bf16[128,1536]{1,0:T(8,128)(2,1)}) custom-call(s32[48,24]{1,0:T(8,128)} %get-tuple-element.25.slot_of, bf16[256,6144]{1,0:T(8,128)(2,1)S(1)} %get-tuple-element.26.x, bf16[461,128,128]{2,1,0:T(8,128)(2,1)S(1)} %get-tuple-element.27.w), custom_call_target="tpu_custom_call" | custom-call | flops 4831838208 | bytes 1048576 | tf_op jit(solution)/shard_map/pallas_call | solution.py:99
  26.5 1.9 %collective-permute-start.5 = (bf16[128,1536]{1,0:T(8,128)(2,1)}, bf16[128,1536]{1,0:T(8,128)(2,1)S(1)}, u32[]{:S(2)}, u32[]{:S(2)}) collective-permute-start(bf16[128,1536]{1,0:T(8,128)(2,1)} %get-tuple-element.35), channel_id=1, source_target_pairs={{0,4},{4,0},{1,5},{5,1},{2,6},{6,2},{3,7},{7,3},{8,12},{12,8},{9,1... | collective-permute-start | bytes 1179656 | tf_op jit(solution)/shard_map/ppermute | solution.py:257
  30.3 4.0 %collective-permute-start.1 = (bf16[32,1536]{1,0:T(8,128)(2,1)S(1)}, bf16[32,1536]{1,0:T(8,128)(2,1)S(1)}, u32[]{:S(2)}, u32[]{:S(2)}) collective-permute-start(bf16[32,1536]{1,0:T(8,128)(2,1)S(1)} %get-tuple-element.30), channel_id=1, source_target_pairs={{0,8},{1,9},{2,10},{3,11},{4,12},{5,13},{6,14},{7,15},{8,16},{9,17... | collective-permute-start | bytes 294920 | tf_op jit(solution)/shard_map/ppermute | solution.py:269
  35.6 5.0 %collective-permute-start.3 = (bf16[32,1536]{1,0:T(8,128)(2,1)S(1)}, bf16[32,1536]{1,0:T(8,128)(2,1)S(1)}, u32[]{:S(2)}, u32[]{:S(2)}) collective-permute-start(bf16[32,1536]{1,0:T(8,128)(2,1)S(1)} %get-tuple-element.32), channel_id=1, source_target_pairs={{0,10},{1,11},{2,8},{3,9},{4,14},{5,15},{6,12},{7,13},{8,18},{9,19... | collective-permute-start | bytes 294920 | tf_op jit(solution)/shard_map/ppermute | solution.py:269
  40.7 13.4 %collective-permute-done.5.received = bf16[128,1536]{1,0:T(8,128)(2,1)S(1)} collective-permute-done((bf16[128,1536]{1,0:T(8,128)(2,1)}, bf16[128,1536]{1,0:T(8,128)(2,1)S(1)}, u32[]{:S(2)}, u32[]{:S(2)}) %collective-permute-start.5) | collective-permute-done | bytes 393248 | tf_op jit(solution)/shard_map/ppermute | solution.py:257
  54.1 3.4 %collective-permute-start.4 = (bf16[32,1536]{1,0:T(8,128)(2,1)S(1)}, bf16[32,1536]{1,0:T(8,128)(2,1)S(1)}, u32[]{:S(2)}, u32[]{:S(2)}) collective-permute-start(bf16[32,1536]{1,0:T(8,128)(2,1)S(1)} %get-tuple-element.33), channel_id=1, source_target_pairs={{0,11},{1,10},{2,9},{3,8},{4,15},{5,14},{6,13},{7,12},{8,19},{9,18... | collective-permute-start | bytes 294920 | tf_op jit(solution)/shard_map/ppermute | solution.py:269
  59.1 2.1 %shard_map.101.dy = bf16[256,3072]{1,0:T(8,128)(2,1)S(1)} custom-call(bf16[128,3072]{1,0:T(8,128)(2,1)S(1)} %copy-done.2, bf16[128,3072]{1,0:T(8,128)(2,1)S(1)} %collective-permute-done.10.other), custom_call_target="tpu_custom_call" | custom-call | tf_op jit(solution)/shard_map/pallas_call | solution.py:131
  61.3 5.3 %copy-done.1 = bf16[461,128,128]{2,1,0:T(8,128)(2,1)S(1)} copy-done((bf16[461,128,128]{2,1,0:T(8,128)(2,1)S(1)}, bf16[461,128,128]{2,1,0:T(8,128)(2,1)}, u32[]{:S(2)}) %copy-start.1) | copy-done | bytes 15106072
  66.5 4.5 %shard_map.102 = (bf16[128,1536]{1,0:T(8,128)(2,1)}, bf16[128,1536]{1,0:T(8,128)(2,1)}) custom-call(s32[48,24]{1,0:T(8,128)} %get-tuple-element.25.slot_of, bf16[256,3072]{1,0:T(8,128)(2,1)S(1)} %shard_map.101.dy, bf16[461,128,128]{2,1,0:T(8,128)(2,1)S(1)} %copy-done.1), custom_call_target="tpu_custom_call" | custom-call | flops 2415919104 | bytes 1048576 | tf_op jit(solution)/shard_map/pallas_call | solution.py:162
  71.1 4.7 %shard_map.103 = (bf16[128,1536]{1,0:T(8,128)(2,1)}, bf16[128,1536]{1,0:T(8,128)(2,1)}) custom-call(s32[48,24]{1,0:T(8,128)} %get-tuple-element.25.slot_of, bf16[256,3072]{1,0:T(8,128)(2,1)S(1)} %shard_map.101.dy, bf16[461,128,128]{2,1,0:T(8,128)(2,1)S(1)} %copy-done.1), custom_call_target="tpu_custom_call" | custom-call | flops 2415919104 | bytes 1048576 | tf_op jit(solution)/shard_map/pallas_call | solution.py:162
  77.3 4.5 %shard_map.104 = (bf16[128,1536]{1,0:T(8,128)(2,1)}, bf16[128,1536]{1,0:T(8,128)(2,1)}) custom-call(s32[48,24]{1,0:T(8,128)} %get-tuple-element.25.slot_of, bf16[256,3072]{1,0:T(8,128)(2,1)S(1)} %shard_map.101.dy, bf16[461,128,128]{2,1,0:T(8,128)(2,1)S(1)} %copy-done.1), custom_call_target="tpu_custom_call" | custom-call | flops 2415919104 | bytes 1048576 | tf_op jit(solution)/shard_map/pallas_call | solution.py:162
  81.9 4.7 %shard_map.105 = (bf16[128,1536]{1,0:T(8,128)(2,1)}, bf16[128,1536]{1,0:T(8,128)(2,1)}) custom-call(s32[48,24]{1,0:T(8,128)} %get-tuple-element.25.slot_of, bf16[256,3072]{1,0:T(8,128)(2,1)S(1)} %shard_map.101.dy, bf16[461,128,128]{2,1,0:T(8,128)(2,1)S(1)} %copy-done.1), custom_call_target="tpu_custom_call" | custom-call | flops 2415919104 | bytes 1048576 | tf_op jit(solution)/shard_map/pallas_call | solution.py:162
  90.3 1.7 %collective-permute-done.20 = bf16[128,1536]{1,0:T(8,128)(2,1)S(1)} collective-permute-done((bf16[128,1536]{1,0:T(8,128)(2,1)}, bf16[128,1536]{1,0:T(8,128)(2,1)S(1)}, u32[]{:S(2)}, u32[]{:S(2)}) %collective-permute-start.20) | collective-permute-done | bytes 393248 | tf_op jit(solution)/shard_map/ppermute | solution.py:257
  92.6 6.3 %collective-permute-done.12 = bf16[64,1536]{1,0:T(8,128)(2,1)S(1)} collective-permute-done((bf16[64,1536]{1,0:T(8,128)(2,1)S(1)}, bf16[64,1536]{1,0:T(8,128)(2,1)S(1)}, u32[]{:S(2)}, u32[]{:S(2)}) %collective-permute-start.12) | collective-permute-done | bytes 196640 | tf_op jit(solution)/shard_map/ppermute | solution.py:257
  99.5 5.5 %collective-permute-done.15 = bf16[64,1536]{1,0:T(8,128)(2,1)S(1)} collective-permute-done((bf16[64,1536]{1,0:T(8,128)(2,1)S(1)}, bf16[64,1536]{1,0:T(8,128)(2,1)S(1)}, u32[]{:S(2)}, u32[]{:S(2)}) %collective-permute-start.15) | collective-permute-done | bytes 196640 | tf_op jit(solution)/shard_map/ppermute | solution.py:257
  105.7 5.2 %collective-permute-done.18 = bf16[64,1536]{1,0:T(8,128)(2,1)S(1)} collective-permute-done((bf16[64,1536]{1,0:T(8,128)(2,1)S(1)}, bf16[64,1536]{1,0:T(8,128)(2,1)S(1)}, u32[]{:S(2)}, u32[]{:S(2)}) %collective-permute-start.18) | collective-permute-done | bytes 196640 | tf_op jit(solution)/shard_map/ppermute | solution.py:257
  111.4 3.5 %collective-permute-start.6 = (bf16[32,1536]{1,0:T(8,128)(2,1)S(1)}, bf16[32,1536]{1,0:T(8,128)(2,1)S(1)}, u32[]{:S(2)}, u32[]{:S(2)}) collective-permute-start(bf16[32,1536]{1,0:T(8,128)(2,1)S(1)} %get-tuple-element.36), channel_id=1, source_target_pairs={{0,8},{1,9},{2,10},{3,11},{4,12},{5,13},{6,14},{7,15},{8,16},{9,17... | collective-permute-start | bytes 294920 | tf_op jit(solution)/shard_map/ppermute | solution.py:269
  116.5 4.8 %collective-permute-start.8 = (bf16[32,1536]{1,0:T(8,128)(2,1)S(1)}, bf16[32,1536]{1,0:T(8,128)(2,1)S(1)}, u32[]{:S(2)}, u32[]{:S(2)}) collective-permute-start(bf16[32,1536]{1,0:T(8,128)(2,1)S(1)} %get-tuple-element.38), channel_id=1, source_target_pairs={{0,10},{1,11},{2,8},{3,9},{4,14},{5,15},{6,12},{7,13},{8,18},{9,19... | collective-permute-start | bytes 294920 | tf_op jit(solution)/shard_map/ppermute | solution.py:269
  128.2 2.1 %collective-permute-done.16.refs_3_ = bf16[32,1536]{1,0:T(8,128)(2,1)S(1)} collective-permute-done((bf16[32,1536]{1,0:T(8,128)(2,1)S(1)}, bf16[32,1536]{1,0:T(8,128)(2,1)S(1)}, u32[]{:S(2)}, u32[]{:S(2)}) %collective-permute-start.16) | collective-permute-done | bytes 98336 | tf_op jit(solution)/shard_map/ppermute | solution.py:257
  130.3 2.1 %collective-permute-done.19.refs_5_ = bf16[32,1536]{1,0:T(8,128)(2,1)S(1)} collective-permute-done((bf16[32,1536]{1,0:T(8,128)(2,1)S(1)}, bf16[32,1536]{1,0:T(8,128)(2,1)S(1)}, u32[]{:S(2)}, u32[]{:S(2)}) %collective-permute-start.19) | collective-permute-done | bytes 98336 | tf_op jit(solution)/shard_map/ppermute | solution.py:257
  132.5 2.1 %collective-permute-done.22.refs_7_ = bf16[32,1536]{1,0:T(8,128)(2,1)S(1)} collective-permute-done((bf16[32,1536]{1,0:T(8,128)(2,1)S(1)}, bf16[32,1536]{1,0:T(8,128)(2,1)S(1)}, u32[]{:S(2)}, u32[]{:S(2)}) %collective-permute-start.22) | collective-permute-done | bytes 98336 | tf_op jit(solution)/shard_map/ppermute | solution.py:257
  (70 shorter events, 22.6 us)
Async XLA Ops:
  16.4 13.2 %copy-start.6 = (s32[1,2]{1,0:T(1,128)S(1)}, s32[1,2]{1,0:T(1,128)}, u32[]{:S(2)}) copy-start(s32[1,2]{1,0:T(1,128)} %param.14) | copy-start | bytes 28
  16.5 13.1 %collective-permute-start = (bf16[128,1536]{1,0:T(8,128)(2,1)}, bf16[128,1536]{1,0:T(8,128)(2,1)S(1)}, u32[]{:S(2)}, u32[]{:S(2)}) collective-permute-start(bf16[128,1536]{1,0:T(8,128)(2,1)} %get-tuple-element.29), channel_id=1, source_target_pairs={{0,4},{4,0},{1,5},{5,1},{2,6},{6,2},{3,7},{7,3},{8,12},{12,8},{9,1... | collective-permute-start | bytes 1179656 | tf_op jit(solution)/shard_map/ppermute | solution.py:257
  19.4 39.7 %collective-permute-start.10 = (bf16[128,3072]{1,0:T(8,128)(2,1)S(1)}, bf16[128,3072]{1,0:T(8,128)(2,1)S(1)}, u32[]{:S(2)}, u32[]{:S(2)}) collective-permute-start(bf16[128,3072]{1,0:T(8,128)(2,1)S(1)} %copy-done.2), channel_id=1, source_target_pairs={{0,4},{4,0},{1,5},{5,1},{2,6},{6,2},{3,7},{7,3},{8,12},{12,8},{9,1... | collective-permute-start | bytes 2359304 | tf_op jit(solution)/shard_map/ppermute | solution.py:257
  26.5 27.5 %collective-permute-start.5 = (bf16[128,1536]{1,0:T(8,128)(2,1)}, bf16[128,1536]{1,0:T(8,128)(2,1)S(1)}, u32[]{:S(2)}, u32[]{:S(2)}) collective-permute-start(bf16[128,1536]{1,0:T(8,128)(2,1)} %get-tuple-element.35), channel_id=1, source_target_pairs={{0,4},{4,0},{1,5},{5,1},{2,6},{6,2},{3,7},{7,3},{8,12},{12,8},{9,1... | collective-permute-start | bytes 1179656 | tf_op jit(solution)/shard_map/ppermute | solution.py:257
  30.3 81.1 %collective-permute-start.1 = (bf16[32,1536]{1,0:T(8,128)(2,1)S(1)}, bf16[32,1536]{1,0:T(8,128)(2,1)S(1)}, u32[]{:S(2)}, u32[]{:S(2)}) collective-permute-start(bf16[32,1536]{1,0:T(8,128)(2,1)S(1)} %get-tuple-element.30), channel_id=1, source_target_pairs={{0,8},{1,9},{2,10},{3,11},{4,12},{5,13},{6,14},{7,15},{8,16},{9,17... | collective-permute-start | bytes 294920 | tf_op jit(solution)/shard_map/ppermute | solution.py:269
  34.3 80.6 %collective-permute-start.2 = (bf16[32,1536]{1,0:T(8,128)(2,1)S(1)}, bf16[32,1536]{1,0:T(8,128)(2,1)S(1)}, u32[]{:S(2)}, u32[]{:S(2)}) collective-permute-start(bf16[32,1536]{1,0:T(8,128)(2,1)S(1)} %get-tuple-element.31), channel_id=1, source_target_pairs={{0,9},{1,8},{2,11},{3,10},{4,13},{5,12},{6,15},{7,14},{8,17},{9,16... | collective-permute-start | bytes 294920 | tf_op jit(solution)/shard_map/ppermute | solution.py:269
  35.6 85.7 %collective-permute-start.3 = (bf16[32,1536]{1,0:T(8,128)(2,1)S(1)}, bf16[32,1536]{1,0:T(8,128)(2,1)S(1)}, u32[]{:S(2)}, u32[]{:S(2)}) collective-permute-start(bf16[32,1536]{1,0:T(8,128)(2,1)S(1)} %get-tuple-element.32), channel_id=1, source_target_pairs={{0,10},{1,11},{2,8},{3,9},{4,14},{5,15},{6,12},{7,13},{8,18},{9,19... | collective-permute-start | bytes 294920 | tf_op jit(solution)/shard_map/ppermute | solution.py:269
  54.1 69.0 %collective-permute-start.4 = (bf16[32,1536]{1,0:T(8,128)(2,1)S(1)}, bf16[32,1536]{1,0:T(8,128)(2,1)S(1)}, u32[]{:S(2)}, u32[]{:S(2)}) collective-permute-start(bf16[32,1536]{1,0:T(8,128)(2,1)S(1)} %get-tuple-element.33), channel_id=1, source_target_pairs={{0,11},{1,10},{2,9},{3,8},{4,15},{5,14},{6,13},{7,12},{8,19},{9,18... | collective-permute-start | bytes 294920 | tf_op jit(solution)/shard_map/ppermute | solution.py:269
  75.8 10.8 %collective-permute-start.11 = (bf16[128,1536]{1,0:T(8,128)(2,1)S(1)}, bf16[128,1536]{1,0:T(8,128)(2,1)S(1)}, u32[]{:S(2)}, u32[]{:S(2)}) collective-permute-start(bf16[128,1536]{1,0:T(8,128)(2,1)S(1)} %copy-done.13), channel_id=1, source_target_pairs={{0,1},{1,0},{2,3},{3,2},{4,5},{5,4},{6,7},{7,6},{8,9},{9,8},{10,11... | collective-permute-start | bytes 1179656 | tf_op jit(solution)/shard_map/ppermute | solution.py:257
  86.6 1.8 %collective-permute-start.14 = (bf16[128,1536]{1,0:T(8,128)(2,1)S(1)}, bf16[128,1536]{1,0:T(8,128)(2,1)S(1)}, u32[]{:S(2)}, u32[]{:S(2)}) collective-permute-start(bf16[128,1536]{1,0:T(8,128)(2,1)S(1)} %copy-done.12), channel_id=1, source_target_pairs={{0,1},{1,0},{2,3},{3,2},{4,5},{5,4},{6,7},{7,6},{8,9},{9,8},{10,11... | collective-permute-start | bytes 1179656 | tf_op jit(solution)/shard_map/ppermute | solution.py:257
  88.3 1.7 %collective-permute-start.17 = (bf16[128,1536]{1,0:T(8,128)(2,1)S(1)}, bf16[128,1536]{1,0:T(8,128)(2,1)S(1)}, u32[]{:S(2)}, u32[]{:S(2)}) collective-permute-start(bf16[128,1536]{1,0:T(8,128)(2,1)S(1)} %copy-done.11), channel_id=1, source_target_pairs={{0,1},{1,0},{2,3},{3,2},{4,5},{5,4},{6,7},{7,6},{8,9},{9,8},{10,11... | collective-permute-start | bytes 1179656 | tf_op jit(solution)/shard_map/ppermute | solution.py:257
  90.1 1.9 %collective-permute-start.20 = (bf16[128,1536]{1,0:T(8,128)(2,1)}, bf16[128,1536]{1,0:T(8,128)(2,1)S(1)}, u32[]{:S(2)}, u32[]{:S(2)}) collective-permute-start(bf16[128,1536]{1,0:T(8,128)(2,1)} %get-tuple-element.47), channel_id=1, source_target_pairs={{0,1},{1,0},{2,3},{3,2},{4,5},{5,4},{6,7},{7,6},{8,9},{9,8},{10,11... | collective-permute-start | bytes 1179656 | tf_op jit(solution)/shard_map/ppermute | solution.py:257
  92.0 6.9 %collective-permute-start.12 = (bf16[64,1536]{1,0:T(8,128)(2,1)S(1)}, bf16[64,1536]{1,0:T(8,128)(2,1)S(1)}, u32[]{:S(2)}, u32[]{:S(2)}) collective-permute-start(bf16[64,1536]{1,0:T(8,128)(2,1)S(1)} %get-tuple-element.55), channel_id=1, source_target_pairs={{0,2},{1,3},{2,0},{3,1},{4,6},{5,7},{6,4},{7,5},{8,10},{9,11},{10,... | collective-permute-start | bytes 589832 | tf_op jit(solution)/shard_map/ppermute | solution.py:257
  99.0 6.1 %collective-permute-start.15 = (bf16[64,1536]{1,0:T(8,128)(2,1)S(1)}, bf16[64,1536]{1,0:T(8,128)(2,1)S(1)}, u32[]{:S(2)}, u32[]{:S(2)}) collective-permute-start(bf16[64,1536]{1,0:T(8,128)(2,1)S(1)} %get-tuple-element.53), channel_id=1, source_target_pairs={{0,2},{1,3},{2,0},{3,1},{4,6},{5,7},{6,4},{7,5},{8,10},{9,11},{10,... | collective-permute-start | bytes 589832 | tf_op jit(solution)/shard_map/ppermute | solution.py:257
  105.1 5.8 %collective-permute-start.18 = (bf16[64,1536]{1,0:T(8,128)(2,1)S(1)}, bf16[64,1536]{1,0:T(8,128)(2,1)S(1)}, u32[]{:S(2)}, u32[]{:S(2)}) collective-permute-start(bf16[64,1536]{1,0:T(8,128)(2,1)S(1)} %get-tuple-element.51), channel_id=1, source_target_pairs={{0,2},{1,3},{2,0},{3,1},{4,6},{5,7},{6,4},{7,5},{8,10},{9,11},{10,... | collective-permute-start | bytes 589832 | tf_op jit(solution)/shard_map/ppermute | solution.py:257
  110.8 5.7 %collective-permute-start.21 = (bf16[64,1536]{1,0:T(8,128)(2,1)S(1)}, bf16[64,1536]{1,0:T(8,128)(2,1)S(1)}, u32[]{:S(2)}, u32[]{:S(2)}) collective-permute-start(bf16[64,1536]{1,0:T(8,128)(2,1)S(1)} %get-tuple-element.49), channel_id=1, source_target_pairs={{0,2},{1,3},{2,0},{3,1},{4,6},{5,7},{6,4},{7,5},{8,10},{9,11},{10,... | collective-permute-start | bytes 589832 | tf_op jit(solution)/shard_map/ppermute | solution.py:257
  111.4 13.2 %collective-permute-start.6 = (bf16[32,1536]{1,0:T(8,128)(2,1)S(1)}, bf16[32,1536]{1,0:T(8,128)(2,1)S(1)}, u32[]{:S(2)}, u32[]{:S(2)}) collective-permute-start(bf16[32,1536]{1,0:T(8,128)(2,1)S(1)} %get-tuple-element.36), channel_id=1, source_target_pairs={{0,8},{1,9},{2,10},{3,11},{4,12},{5,13},{6,14},{7,15},{8,16},{9,17... | collective-permute-start | bytes 294920 | tf_op jit(solution)/shard_map/ppermute | solution.py:269
  114.9 10.2 %collective-permute-start.7 = (bf16[32,1536]{1,0:T(8,128)(2,1)S(1)}, bf16[32,1536]{1,0:T(8,128)(2,1)S(1)}, u32[]{:S(2)}, u32[]{:S(2)}) collective-permute-start(bf16[32,1536]{1,0:T(8,128)(2,1)S(1)} %get-tuple-element.37), channel_id=1, source_target_pairs={{0,9},{1,8},{2,11},{3,10},{4,13},{5,12},{6,15},{7,14},{8,17},{9,16... | collective-permute-start | bytes 294920 | tf_op jit(solution)/shard_map/ppermute | solution.py:269
  116.5 10.1 %collective-permute-start.8 = (bf16[32,1536]{1,0:T(8,128)(2,1)S(1)}, bf16[32,1536]{1,0:T(8,128)(2,1)S(1)}, u32[]{:S(2)}, u32[]{:S(2)}) collective-permute-start(bf16[32,1536]{1,0:T(8,128)(2,1)S(1)} %get-tuple-element.38), channel_id=1, source_target_pairs={{0,10},{1,11},{2,8},{3,9},{4,14},{5,15},{6,12},{7,13},{8,18},{9,19... | collective-permute-start | bytes 294920 | tf_op jit(solution)/shard_map/ppermute | solution.py:269
  121.4 5.8 %collective-permute-start.9 = (bf16[32,1536]{1,0:T(8,128)(2,1)S(1)}, bf16[32,1536]{1,0:T(8,128)(2,1)S(1)}, u32[]{:S(2)}, u32[]{:S(2)}) collective-permute-start(bf16[32,1536]{1,0:T(8,128)(2,1)S(1)} %get-tuple-element.39), channel_id=1, source_target_pairs={{0,11},{1,10},{2,9},{3,8},{4,15},{5,14},{6,13},{7,12},{8,19},{9,18... | collective-permute-start | bytes 294920 | tf_op jit(solution)/shard_map/ppermute | solution.py:269
  123.0 5.2 %collective-permute-start.13 = (bf16[32,1536]{1,0:T(8,128)(2,1)S(1)}, bf16[32,1536]{1,0:T(8,128)(2,1)S(1)}, u32[]{:S(2)}, u32[]{:S(2)}) collective-permute-start(bf16[32,1536]{1,0:T(8,128)(2,1)S(1)} %get-tuple-element.62), channel_id=1, source_target_pairs={{0,4},{4,0},{1,5},{5,1},{2,6},{6,2},{3,7},{7,3},{8,12},{12,8},{9,1... | collective-permute-start | bytes 294920 | tf_op jit(solution)/shard_map/ppermute | solution.py:257
  124.6 5.7 %collective-permute-start.16 = (bf16[32,1536]{1,0:T(8,128)(2,1)S(1)}, bf16[32,1536]{1,0:T(8,128)(2,1)S(1)}, u32[]{:S(2)}, u32[]{:S(2)}) collective-permute-start(bf16[32,1536]{1,0:T(8,128)(2,1)S(1)} %get-tuple-element.60), channel_id=1, source_target_pairs={{0,4},{4,0},{1,5},{5,1},{2,6},{6,2},{3,7},{7,3},{8,12},{12,8},{9,1... | collective-permute-start | bytes 294920 | tf_op jit(solution)/shard_map/ppermute | solution.py:257
  125.1 7.3 %collective-permute-start.19 = (bf16[32,1536]{1,0:T(8,128)(2,1)S(1)}, bf16[32,1536]{1,0:T(8,128)(2,1)S(1)}, u32[]{:S(2)}, u32[]{:S(2)}) collective-permute-start(bf16[32,1536]{1,0:T(8,128)(2,1)S(1)} %get-tuple-element.58), channel_id=1, source_target_pairs={{0,4},{4,0},{1,5},{5,1},{2,6},{6,2},{3,7},{7,3},{8,12},{12,8},{9,1... | collective-permute-start | bytes 294920 | tf_op jit(solution)/shard_map/ppermute | solution.py:257
  126.6 7.9 %collective-permute-start.22 = (bf16[32,1536]{1,0:T(8,128)(2,1)S(1)}, bf16[32,1536]{1,0:T(8,128)(2,1)S(1)}, u32[]{:S(2)}, u32[]{:S(2)}) collective-permute-start(bf16[32,1536]{1,0:T(8,128)(2,1)S(1)} %get-tuple-element.56), channel_id=1, source_target_pairs={{0,4},{4,0},{1,5},{5,1},{2,6},{6,2},{3,7},{7,3},{8,12},{12,8},{9,1... | collective-permute-start | bytes 294920 | tf_op jit(solution)/shard_map/ppermute | solution.py:257
  (13 other events, 94.6 us)

commit v2 on v0

--- a/solution.py
+++ b/solution.py
@@ -1,7 +1,318 @@
+import functools
+
 import jax
 import jax.numpy as jnp
 from jax import lax
+from jax.experimental import pallas as pl
+from jax.experimental.pallas import tpu as pltpu
 from jax.sharding import PartitionSpec as P
+
+F_PARTS = 2
+B_PARTS = 4
+
+VMEM = pl.BlockSpec(memory_space=pltpu.VMEM)
+SMEM = pl.BlockSpec(memory_space=pltpu.SMEM)
+ANY = pl.BlockSpec(memory_space=pl.ANY)
+HBM = pl.BlockSpec(memory_space=pltpu.HBM)
+PARAMS = pltpu.CompilerParams(vmem_limit_bytes=16 * 2**20)
+
+
+def resident(x):
+    return pltpu.with_memory_space_constraint(x, pltpu.VMEM)
+
+
+def in_hbm(x):
+    return pltpu.with_memory_space_constraint(x, pltpu.HBM)
+
+
+def divisor(n, most):
+    return max(d for d in range(1, most + 1) if n % d == 0)
+
+
+def prep_kernel(
+    owned, block_rows, block_cols,
+    count, row_hbm, col_hbm, order_hbm, w_hbm, x_hbm,
+    w_out, x_out, slot_of,
+    row, col, order, w_sem, x_sem, list_sem,
+):
+    cap = w_hbm.shape[0]
+    positions = block_rows * block_cols
+    lists = [
+        pltpu.make_async_copy(source, target, list_sem.at[i])
+        for i, (source, target) in enumerate(
+            ((order_hbm, order), (row_hbm, row), (col_hbm, col))
+        )
+    ]
+    for copy in lists:
+        copy.start()
+    w_copy = pltpu.make_async_copy(w_hbm, w_out.at[pl.ds(0, cap)], w_sem)
+    w_copy.start()
+    w_out[cap] = jnp.zeros(w_out.shape[1:], w_out.dtype)
+
+    @pl.loop(0, positions // block_cols)
+    def _(i):
+        for j in range(block_cols):
+            slot_of[i * block_cols + j] = cap
+
+    lists[0].wait()
+    r, c = lax.axis_index("row"), lax.axis_index("col")
+    block = x_hbm.shape[0] // order.shape[1]
+    per_owner = owned // block
+    copies = []
+    at = 0
+    for dr in range(2):
+        for dc in range(4):
+            first = ((r ^ dr) * 4 + (c ^ dc)) * per_owner
+            for b in range(per_owner):
+                source = pl.multiple_of(order[0, first + b] * block, block)
+                copies.append(
+                    pltpu.make_async_copy(
+                        x_hbm.at[pl.ds(source, block)], x_out.at[pl.ds(at, block)], x_sem.at[len(copies)]
+                    )
+                )
+                copies[-1].start()
+                at += block
+    for copy in lists[1:]:
+        copy.wait()
+    live = count[0]
+    step = divisor(cap, 20)
+
+    @pl.loop(0, cap // step)
+    def _(i):
+        for j in range(step):
+            k = i * step + j
+            place = row[0, k] * block_cols + col[0, k]
+            slot_of[jnp.where(k < live, place, positions)] = k
+
+    for copy in copies:
+        copy.wait()
+    w_copy.wait()
+
+
+def prep(owned, block_cols, count, row, col, order, weights, x):
+    cap, size, _ = weights.shape
+    block_rows = x.shape[1] // size
+    lists = (row, col, order)
+    return pl.pallas_call(
+        functools.partial(prep_kernel, owned, block_rows, block_cols),
+        out_shape=(
+            pltpu.VMEM((cap + 1, size, size), weights.dtype),
+            pltpu.VMEM(x.shape, x.dtype),
+            jax.ShapeDtypeStruct((block_rows * block_cols + 1,), jnp.int32),
+        ),
+        in_specs=[SMEM] + [HBM] * 5,
+        out_specs=(VMEM, VMEM, SMEM),
+        scratch_shapes=[pltpu.SMEM(a.shape, a.dtype) for a in lists]
+        + [
+            pltpu.SemaphoreType.DMA,
+            pltpu.SemaphoreType.DMA((order.shape[1],)),
+            pltpu.SemaphoreType.DMA((len(lists),)),
+        ],
+        compiler_params=PARAMS,
+    )(count, *[in_hbm(a) for a in (*lists, weights, x)])
+
+
+def forward_kernel(block, order, limits, slot_of, x, w, *outs):
+    r, c = lax.axis_index("row"), lax.axis_index("col")
+    rows = x.shape[0]
+    half = rows // 2
+    per_owner = rows // 8 // block
+    size = w.shape[1]
+    pair = 2 * size
+    tokens = []
+    for dr in range(2):
+        for dc in range(4):
+            for b in range(per_owner):
+                first = order[((r ^ dr) * 4 + (c ^ dc)) * per_owner + b] * block
+                tokens.append(first + lax.broadcasted_iota(jnp.int32, (block, pair), 0))
+    live = jnp.concatenate(tokens, axis=0) < limits[0]
+    block_cols = sum(send.shape[1] for send in outs[1::2]) // size
+    column = 0
+    for keep, send in zip(outs[::2], outs[1::2]):
+        for j in range(keep.shape[1] // pair):
+            rhs = jnp.concatenate(
+                [
+                    jnp.concatenate([w[slot_of[i + column]], w[slot_of[i + column + 1]]], axis=1)
+                    for i in range(0, slot_of.shape[0] - 1, block_cols)
+                ],
+                axis=0,
+            )
+            part = jnp.dot(x[...], rhs, preferred_element_type=jnp.float32)
+            part = jnp.where(live, part, 0.0).astype(keep.dtype)
+            keep[:, j * pair : (j + 1) * pair] = part[:half]
+            send[:, j * pair : (j + 1) * pair] = part[half:]
+            column += 2
+
+
+def forward(block, order, limits, slot_of, x, w, width):
+    shape = pltpu.VMEM((x.shape[0] // 2, width // F_PARTS), x.dtype)
+    return pl.pallas_call(
+        functools.partial(forward_kernel, block),
+        out_shape=(shape,) * (2 * F_PARTS),
+        in_specs=[SMEM, SMEM, SMEM, VMEM, VMEM],
+        out_specs=(VMEM,) * (2 * F_PARTS),
+        compiler_params=PARAMS,
+        cost_estimate=pl.CostEstimate(flops=1000, bytes_accessed=1000, transcendentals=0),
+    )(order, limits, slot_of, resident(x), resident(w))
+
+
+def backward_kernel(first, slot_of, own, other, w, *refs):
+    keep, send, dy = refs[-3:]
+    c = lax.axis_index("col")
+    owned = own.shape[0] // 4
+    size = w.shape[1]
+    block_cols = own.shape[1] // size
+    at = 0
+    for dk in range(2):
+        for dx in range(2):
+            rows = pl.ds(pl.multiple_of((c ^ (2 * dx + dk)) * owned, owned), owned)
+            for source in (own, other):
+                dy[at : at + owned] = source[rows]
+                at += owned
+    half = keep.shape[0]
+    pair = 2 * size
+    for i in range(keep.shape[1] // pair):
+        at = (first + 2 * i) * block_cols
+        rhs = jnp.concatenate(
+            [
+                jnp.concatenate([w[slot_of[at + j]], w[slot_of[at + block_cols + j]]], axis=0)
+                for j in range(block_cols)
+            ],
+            axis=1,
+        )
+        part = lax.dot_general(
+            dy[...], rhs, (((1,), (1,)), ((), ())), preferred_element_type=jnp.float32
+        ).astype(keep.dtype)
+        keep[:, i * pair : (i + 1) * pair] = part[:half]
+        send[:, i * pair : (i + 1) * pair] = part[half:]
+
+
+def backward(part, slot_of, own, other, w, after):
+    block_cols = own.shape[1] // w.shape[1]
+    block_rows = slot_of.shape[0] // block_cols
+    shape = pltpu.VMEM((own.shape[0], block_rows * w.shape[1] // B_PARTS), own.dtype)
+    return pl.pallas_call(
+        functools.partial(backward_kernel, part * (block_rows // B_PARTS)),
+        out_shape=(shape, shape),
+        in_specs=[SMEM, VMEM, VMEM, VMEM] + [ANY] * len(after),
+        out_specs=(VMEM, VMEM),
+        scratch_shapes=[pltpu.VMEM((2 * own.shape[0], own.shape[1]), own.dtype)],
+        compiler_params=PARAMS,
+        cost_estimate=pl.CostEstimate(flops=1000, bytes_accessed=1000, transcendentals=0),
+    )(slot_of, own, other, resident(w), *after)
+
+
+def place_forward_kernel(*refs):
+    pieces, out, sems = refs[:-2], refs[-2], refs[-1]
+    c = lax.axis_index("col")
+    width = out.shape[1] // 4
+    copies = []
+    for dc in range(4):
+        at = (c ^ dc) * width
+        for piece in pieces[dc::4]:
+            copies.append(
+                pltpu.make_async_copy(
+                    piece, out.at[:, pl.ds(pl.multiple_of(at, 128), piece.shape[1])], sems.at[len(copies)]
+                )
+            )
+            copies[-1].start()
+            at += piece.shape[1]
+    for copy in copies:
+        copy.wait()
+
+
+def place_forward(pieces):
+    rows = pieces[0].shape[0]
+    width = sum(piece.shape[1] for piece in pieces)
+    return pl.pallas_call(
+        place_forward_kernel,
+        out_shape=jax.ShapeDtypeStruct((rows, width), pieces[0].dtype),
+        in_specs=[ANY] * len(pieces),
+        out_specs=ANY,
+        scratch_shapes=[pltpu.SemaphoreType.DMA((len(pieces),))],
+        compiler_params=PARAMS,
+    )(*pieces)
+
+
+def place_backward_kernel(limits, *refs):
+    pieces, out = refs[:-1], refs[-1]
+    r, c = lax.axis_index("row"), lax.axis_index("col")
+    rows = out.shape[0]
+    width = out.shape[1] // 2
+    for dr in range(2):
+        at = (r ^ dr) * width
+        for piece in pieces[dr::2]:
+            token = (r * 4 + c) * rows + lax.broadcasted_iota(jnp.int32, piece.shape, 0)
+            value = jnp.where(token < limits[1], piece[...].astype(jnp.float32), 0.0).astype(out.dtype)
+            out[:, pl.ds(pl.multiple_of(at, 128), piece.shape[1])] = value
+            at += piece.shape[1]
+
+
+def place_backward(limits, pieces):
+    rows = pieces[0].shape[0]
+    width = sum(piece.shape[1] for piece in pieces)
+    return pl.pallas_call(
+        place_backward_kernel,
+        out_shape=jax.ShapeDtypeStruct((rows, width), pieces[0].dtype),
+        in_specs=[SMEM] + [VMEM] * len(pieces),
+        out_specs=VMEM,
+        compiler_params=PARAMS,
+    )(limits, *pieces)
+
+
+def swap(x, axis, by):
+    return lax.ppermute(x, axis, [(i, i ^ by) for i in range(lax.axis_size(axis))])
+
+
+def added(a, b):
+    return (a.astype(jnp.float32) + b.astype(jnp.float32)).astype(a.dtype)
+
+
+def grid_2x4(x_fwd, dy_bwd, w_blocks, blk_row, blk_col, blk_count, tok_count, owner_order):
+    token_total = x_fwd.shape[0]
+    owned = token_total // 8
+    slots, size = w_blocks.shape[3], w_blocks.shape[5]
+    order = owner_order.reshape(-1)
+    limits = tok_count.reshape(2)
+    block = token_total // order.shape[0]
+    dy_other = swap(dy_bwd, "row", 1)
+    w, x, slot_of = prep(
+        owned,
+        dy_bwd.shape[1] // size,
+        blk_count.reshape(1),
+        blk_row.reshape(1, slots),
+        blk_col.reshape(1, slots),
+        owner_order,
+        w_blocks.reshape(slots, size, size),
+        x_fwd,
+    )
+    parts = forward(block, order, limits, slot_of, x, w, dy_bwd.shape[1])
+    keeps, sends = parts[::2], parts[1::2]
+    *sends, dy_other = lax.optimization_barrier((*sends, dy_other))
+
+    y_pieces, dx_pieces = [], []
+    forward_sums, backward_sums = [], []
+    for part in range(B_PARTS):
+        after = backward_sums[part - 2 : part - 1] if part >= 2 else []
+        if part == B_PARTS - 1:
+            after = after + forward_sums[:1]
+        keep, send = backward(part, slot_of, dy_bwd, dy_other, w, after)
+        if part < F_PARTS:
+            summed = added(keeps[part], swap(sends[part], "row", 1))
+            forward_sums.append(summed)
+            shifted = passed_along(summed, "section", 1)
+            here, there = shifted[: 2 * owned], swap(shifted[2 * owned :], "col", 2)
+            y_pieces += [here[:owned], swap(here[owned:], "col", 1), there[:owned], swap(there[owned:], "col", 1)]
+        received = swap(send, "col", 1)
+        half = keep.shape[0] // 2
+        onward = added(keep[half:], received[half:])
+        backward_sums.append(onward)
+        kept = added(keep[:half], received[:half])
+        received = swap(onward, "col", 2)
+        onward = added(kept[owned:], received[owned:])
+        kept = added(kept[:owned], received[:owned])
+        dx_pieces += [kept, swap(onward, "row", 1)]
+    return place_forward(y_pieces), place_backward(limits, dx_pieces)
 
 
 def passed_along(shard, axis, by):
@@ -10,7 +321,7 @@
     return lax.ppermute(shard, axis, pairs)
 
 
-def local(x_fwd, dy_bwd, w_blocks, blk_row, blk_col, blk_count, tok_count, owner_order):
+def any_grid(x_fwd, dy_bwd, w_blocks, blk_row, blk_col, blk_count, tok_count, owner_order):
     row_count = lax.axis_size("row")
     col_count = lax.axis_size("col")
     token_total, in_width = x_fwd.shape
@@ -68,8 +379,9 @@
 
 
 def solution(mesh):
+    small = mesh.shape["row"] == 2 and mesh.shape["col"] == 4
     return jax.shard_map(
-        local,
+        grid_2x4 if small else any_grid,
         mesh=mesh,
         in_specs=(
             P("section", "row"),

time: 283 us -> 82.9 us (0.29)
  other arithmetic: 124 us -> 0.77 us
  local copies, waits for them, and re-layouts: 64.7 us -> 0.1 us
  matrix products: 36.6 us -> 0 us
  Pallas kernels: 0 us -> 33.7 us
  between operations: 14.8 us -> 1.76 us
  starting transfers between devices: 14.1 us -> 23 us
  waiting for transfers between devices: 27 us -> 23.4 us
    scatter-add x1 -> x0, other arithmetic: 96.5 us -> none  [local(): dense_blocks.at[blk_row.reshape(slot_total), blk_col.reshape(slot_total)]]
    transpose x1 -> x0, local copies, waits for them, and re-layouts: 40.8 us -> none  [local(): jnp.transpose(dense_blocks, (0, 2, 1, 3)).reshape(in_width, out_width)]
    dot_general x2 -> x0, matrix products: 36.6 us -> none  [the longest x1 18.3 us: local(): jnp.dot(ordered_rows, dense_weight, preferred_element_type=jnp.float32)]
    pallas_call x0 -> x8, Pallas kernels: none -> 33.7 us  [the longest x4 13.2 us: backward(): pl.pallas_call(functools.partial(backward_kernel, part * (block_rows // B...]
    ppermute x0 -> x21, waiting for transfers between devices: none -> 16.2 us  [swap(): lax.ppermute(x, axis, [(i, i ^ by) for i in range(lax.axis_size(axis))])]
    ppermute x0 -> x21, starting transfers between devices: none -> 16 us  [swap(): lax.ppermute(x, axis, [(i, i ^ by) for i in range(lax.axis_size(axis))])]
    mul x2 -> x0, other arithmetic: 14.8 us -> none  [the longest x1 14.1 us: local(): weights * live[:, None, None]]
    broadcast_in_dim x1 -> x0, local copies, waits for them, and re-layouts: 12.5 us -> none  [local(): jnp.zeros((block_rows, block_cols, block_size, block_size), weights.dtype)]
  transfers between devices with their start and end apart: 4 -> 23, of which waited for: 3 -> 8; matrix products, arithmetic and copies ran while one was open for 77% -> 1% of each run, Pallas kernels for 0% -> 36%
where the time goes in v2:
time: 82.9 us; the launch traced here: 82.7 us
  Pallas kernels  33.7 us (41%)
  waiting for transfers between devices  23.4 us (28%)
  starting transfers between devices  23 us (28%)
  between operations  1.76 us (2%)
    ppermute x21, waiting for transfers between devices, swap(): lax.ppermute(x, axis, [(i, i ^ by) for i in range(lax.axis_size(axis))])  16.2 us
    ppermute x21, starting transfers between devices, swap(): lax.ppermute(x, axis, [(i, i ^ by) for i in range(lax.axis_size(axis))])  16 us
    pallas_call x4, Pallas kernels, backward(): pl.pallas_call(functools.partial(backward_kernel, part * (block_rows // B...  13.2 us
    pallas_call x1, Pallas kernels, forward(): pl.pallas_call(functools.partial(forward_kernel, block), out_shape=(shape...  10.8 us
    ppermute x2, waiting for transfers between devices, passed_along(): return lax.ppermute(shard, axis, pairs)  7.18 us
    pallas_call x1, Pallas kernels, prep(): pl.pallas_call(functools.partial(prep_kernel, owned, block_rows, block_co...  7.15 us
    ppermute x2, starting transfers between devices, passed_along(): return lax.ppermute(shard, axis, pairs)  6.99 us
  transfers between devices with their start and end apart: 23, of which 8 were waited for; matrix products, arithmetic and copies ran while one was open for 1% of the time, Pallas kernels for 36%

profile of v2, /device:TPU:0, one launch (start us, length us, event | category | flops | bytes accessed | tf_op | source)
XLA Modules:
  0.0 82.7 jit_solution(2716441452928436974)
XLA Ops:
  0.7 3.0 %collective-permute-start = (bf16[128,3072]{1,0:T(8,128)(2,1)}, bf16[128,3072]{1,0:T(8,128)(2,1)S(1)}, u32[]{:S(2)}, u32[]{:S(2)}) collective-permute-start(bf16[128,3072]{1,0:T(8,128)(2,1)} %own.7), channel_id=1, source_target_pairs={{0,4},{4,0},{1,5},{5,1},{2,6},{6,2},{3,7},{7,3},{8,12},{12,8},{9,1... | collective-permute-start | bytes 2359304 | tf_op jit(solution)/shard_map/ppermute | solution.py:264
  4.3 7.2 %shard_map.95 = (bf16[461,128,128]{2,1,0:T(8,128)(2,1)S(1)}, bf16[256,6144]{1,0:T(8,128)(2,1)S(1)}, s32[1153]{0:T(1024)S(1)}) custom-call(s32[1]{0:T(128)} %bitcast.6.count, s32[1,460]{1,0:T(1,128)} %bitcast.11, s32[1,460]{1,0:T(1,128)} %bitcast.12, s32[1,16]{1,0:T(1,128)} %order_hbm.1, bf16[460,128,128]{2,1,0:T(8,128)(2,1)} %bitcast.10, bf16[256,6144]{1,0:T(8,128)(2,1)} %x_hbm.1), custom_call_target="tpu_custom_call" | custom-call | tf_op jit(solution)/shard_map/pallas_call | solution.py:96
  11.5 10.8 %shard_map.96 = (bf16[128,1536]{1,0:T(8,128)(2,1)S(1)}, bf16[128,1536]{1,0:T(8,128)(2,1)S(1)}, bf16[128,1536]{1,0:T(8,128)(2,1)S(1)}, bf16[128,1536]{1,0:T(8,128)(2,1)S(1)}) custom-call(s32[16]{0:T(128)S(1)} %bitcast.7, s32[2]{0:T(128)S(1)} %bitcast.8, s32[1153]{0:T(1024)S(1)} %get-tuple-element.20.slot_of, bf16[256,6144]{1,0:T(8,128)(2,1)S(1)} %get-tuple-element.21.x, ...), custom_call_target="tpu_custom_call" | custom-call | flops 1000 | bytes 1000 | tf_op jit(solution)/shard_map/pallas_call | solution.py:149
  22.3 3.3 %shard_map.98 = (bf16[128,1536]{1,0:T(8,128)(2,1)S(1)}, bf16[128,1536]{1,0:T(8,128)(2,1)S(1)}) custom-call(s32[1153]{0:T(1024)S(1)} %get-tuple-element.20.slot_of, bf16[128,3072]{1,0:T(8,128)(2,1)S(1)} %copy-done, bf16[128,3072]{1,0:T(8,128)(2,1)S(1)} %collective-permute-done.other, bf16[461,128,128]{2,1,0:T(8,128)(2,1)S(1)} %get-tuple-element.22.w), custom_call_target="tpu_custom_call" | custom-call | flops 1000 | bytes 1000 | tf_op jit(solution)/shard_map/pallas_call | solution.py:194
  25.7 3.3 %shard_map.99 = (bf16[128,1536]{1,0:T(8,128)(2,1)S(1)}, bf16[128,1536]{1,0:T(8,128)(2,1)S(1)}) custom-call(s32[1153]{0:T(1024)S(1)} %get-tuple-element.20.slot_of, bf16[128,3072]{1,0:T(8,128)(2,1)S(1)} %copy-done, bf16[128,3072]{1,0:T(8,128)(2,1)S(1)} %collective-permute-done.other, bf16[461,128,128]{2,1,0:T(8,128)(2,1)S(1)} %get-tuple-element.22.w), custom_call_target="tpu_custom_call" | custom-call | flops 1000 | bytes 1000 | tf_op jit(solution)/shard_map/pallas_call | solution.py:194
  30.4 1.2 %collective-permute-start.6 = (bf16[128,1536]{1,0:T(8,128)(2,1)S(1)}, bf16[128,1536]{1,0:T(8,128)(2,1)S(1)}, u32[]{:S(2)}, u32[]{:S(2)}) collective-permute-start(bf16[128,1536]{1,0:T(8,128)(2,1)S(1)} %get-tuple-element.28), channel_id=1, source_target_pairs={{0,4},{4,0},{1,5},{5,1},{2,6},{6,2},{3,7},{7,3},{8,12},{12,8},{9,1... | collective-permute-start | bytes 1179656 | tf_op jit(solution)/shard_map/ppermute | solution.py:264
  31.7 3.5 %shard_map.100 = (bf16[128,1536]{1,0:T(8,128)(2,1)S(1)}, bf16[128,1536]{1,0:T(8,128)(2,1)S(1)}) custom-call(s32[1153]{0:T(1024)S(1)} %get-tuple-element.20.slot_of, bf16[128,3072]{1,0:T(8,128)(2,1)S(1)} %copy-done, bf16[128,3072]{1,0:T(8,128)(2,1)S(1)} %collective-permute-done.other, bf16[461,128,128]{2,1,0:T(8,128)(2,1)S(1)} %get-tuple-element.22.w, ...), custom_call_target="tpu_custom_call" | custom-call | flops 1000 | bytes 1000 | tf_op jit(solution)/shard_map/pallas_call | solution.py:194
  35.1 1.6 %collective-permute-start.12 = (bf16[64,1536]{1,0:T(8,128)(2,1)S(1)}, bf16[64,1536]{1,0:T(8,128)(2,1)S(1)}, u32[]{:S(2)}, u32[]{:S(2)}) collective-permute-start(bf16[64,1536]{1,0:T(8,128)(2,1)S(1)} %get-tuple-element.45.refs_0_), channel_id=1, source_target_pairs={{0,2},{1,3},{2,0},{3,1},{4,6},{5,7},{6,4},{7,5},{8,10},{9,11},{10,... | collective-permute-start | bytes 589832 | tf_op jit(solution)/shard_map/ppermute | solution.py:264
  36.7 4.8 %collective-permute-done.1 = bf16[128,1536]{1,0:T(8,128)(2,1)S(1)} collective-permute-done((bf16[128,1536]{1,0:T(8,128)(2,1)S(1)}, bf16[128,1536]{1,0:T(8,128)(2,1)S(1)}, u32[]{:S(2)}, u32[]{:S(2)}) %collective-permute-start.1) | collective-permute-done | bytes 393248 | tf_op jit(solution)/shard_map/ppermute | solution.py:264
  41.7 1.6 %collective-permute-start.15 = (bf16[64,1536]{1,0:T(8,128)(2,1)S(1)}, bf16[64,1536]{1,0:T(8,128)(2,1)S(1)}, u32[]{:S(2)}, u32[]{:S(2)}) collective-permute-start(bf16[64,1536]{1,0:T(8,128)(2,1)S(1)} %get-tuple-element.43.refs_0_), channel_id=1, source_target_pairs={{0,2},{1,3},{2,0},{3,1},{4,6},{5,7},{6,4},{7,5},{8,10},{9,11},{10,... | collective-permute-start | bytes 589832 | tf_op jit(solution)/shard_map/ppermute | solution.py:264
  43.3 3.3 %shard_map.101 = (bf16[128,1536]{1,0:T(8,128)(2,1)S(1)}, bf16[128,1536]{1,0:T(8,128)(2,1)S(1)}) custom-call(s32[1153]{0:T(1024)S(1)} %get-tuple-element.20.slot_of, bf16[128,3072]{1,0:T(8,128)(2,1)S(1)} %copy-done, bf16[128,3072]{1,0:T(8,128)(2,1)S(1)} %collective-permute-done.other, bf16[461,128,128]{2,1,0:T(8,128)(2,1)S(1)} %get-tuple-element.22.w, ...), custom_call_target="tpu_custom_call" | custom-call | flops 1000 | bytes 1000 | tf_op jit(solution)/shard_map/pallas_call | solution.py:194
  46.5 3.5 %collective-permute-start.2 = (bf16[128,1536]{1,0:T(8,128)(2,1)S(1)}, bf16[128,1536]{1,0:T(8,128)(2,1)S(1)}, u32[]{:S(2)}, u32[]{:S(2)}) collective-permute-start(bf16[128,1536]{1,0:T(8,128)(2,1)S(1)} %add_convert_fusion.1.refs_1_), channel_id=1, source_target_pairs={{0,8},{8,16},{16,24},{1,9},{9,17},{17,25},{2,10},{10,18},{18,26},{... | collective-permute-start | bytes 1179656 | tf_op jit(solution)/shard_map/ppermute | solution.py:321
  50.7 3.5 %collective-permute-start.7 = (bf16[128,1536]{1,0:T(8,128)(2,1)S(1)}, bf16[128,1536]{1,0:T(8,128)(2,1)S(1)}, u32[]{:S(2)}, u32[]{:S(2)}) collective-permute-start(bf16[128,1536]{1,0:T(8,128)(2,1)S(1)} %add_convert_fusion), channel_id=1, source_target_pairs={{0,8},{8,16},{16,24},{1,9},{9,17},{17,25},{2,10},{10,18},{18,26},{... | collective-permute-start | bytes 1179656 | tf_op jit(solution)/shard_map/ppermute | solution.py:321
  54.3 0.9 %collective-permute-start.16 = (bf16[32,1536]{1,0:T(8,128)(2,1)S(1)}, bf16[32,1536]{1,0:T(8,128)(2,1)S(1)}, u32[]{:S(2)}, u32[]{:S(2)}) collective-permute-start(bf16[32,1536]{1,0:T(8,128)(2,1)S(1)} %get-tuple-element.50), channel_id=1, source_target_pairs={{0,4},{4,0},{1,5},{5,1},{2,6},{6,2},{3,7},{7,3},{8,12},{12,8},{9,1... | collective-permute-start | bytes 294920 | tf_op jit(solution)/shard_map/ppermute | solution.py:264
  55.2 1.3 %collective-permute-start.13 = (bf16[32,1536]{1,0:T(8,128)(2,1)S(1)}, bf16[32,1536]{1,0:T(8,128)(2,1)S(1)}, u32[]{:S(2)}, u32[]{:S(2)}) collective-permute-start(bf16[32,1536]{1,0:T(8,128)(2,1)S(1)} %get-tuple-element.52), channel_id=1, source_target_pairs={{0,4},{4,0},{1,5},{5,1},{2,6},{6,2},{3,7},{7,3},{8,12},{12,8},{9,1... | collective-permute-start | bytes 294920 | tf_op jit(solution)/shard_map/ppermute | solution.py:264
  57.3 1.5 %collective-permute-done.2 = bf16[128,1536]{1,0:T(8,128)(2,1)S(1)} collective-permute-done((bf16[128,1536]{1,0:T(8,128)(2,1)S(1)}, bf16[128,1536]{1,0:T(8,128)(2,1)S(1)}, u32[]{:S(2)}, u32[]{:S(2)}) %collective-permute-start.2) | collective-permute-done | bytes 393248 | tf_op jit(solution)/shard_map/ppermute | solution.py:321
  59.4 5.7 %collective-permute-done.7 = bf16[128,1536]{1,0:T(8,128)(2,1)S(1)} collective-permute-done((bf16[128,1536]{1,0:T(8,128)(2,1)S(1)}, bf16[128,1536]{1,0:T(8,128)(2,1)S(1)}, u32[]{:S(2)}, u32[]{:S(2)}) %collective-permute-start.7) | collective-permute-done | bytes 393248 | tf_op jit(solution)/shard_map/ppermute | solution.py:321
  65.8 2.5 %collective-permute-done.18 = bf16[64,1536]{1,0:T(8,128)(2,1)S(1)} collective-permute-done((bf16[64,1536]{1,0:T(8,128)(2,1)S(1)}, bf16[64,1536]{1,0:T(8,128)(2,1)S(1)}, u32[]{:S(2)}, u32[]{:S(2)}) %collective-permute-start.18) | collective-permute-done | bytes 196640 | tf_op jit(solution)/shard_map/ppermute | solution.py:264
  68.8 4.1 %collective-permute-done.4 = bf16[64,1536]{1,0:T(8,128)(2,1)S(1)} collective-permute-done((bf16[64,1536]{1,0:T(8,128)(2,1)S(1)}, bf16[64,1536]{1,0:T(8,128)(2,1)S(1)}, u32[]{:S(2)}, u32[]{:S(2)}) %collective-permute-start.4) | collective-permute-done | bytes 196640 | tf_op jit(solution)/shard_map/ppermute | solution.py:264
  73.7 1.6 %collective-permute-done.9 = bf16[64,1536]{1,0:T(8,128)(2,1)S(1)} collective-permute-done((bf16[64,1536]{1,0:T(8,128)(2,1)S(1)}, bf16[64,1536]{1,0:T(8,128)(2,1)S(1)}, u32[]{:S(2)}, u32[]{:S(2)}) %collective-permute-start.9) | collective-permute-done | bytes 196640 | tf_op jit(solution)/shard_map/ppermute | solution.py:264
  76.8 1.6 %collective-permute-done.22.refs_7_ = bf16[32,1536]{1,0:T(8,128)(2,1)S(1)} collective-permute-done((bf16[32,1536]{1,0:T(8,128)(2,1)S(1)}, bf16[32,1536]{1,0:T(8,128)(2,1)S(1)}, u32[]{:S(2)}, u32[]{:S(2)}) %collective-permute-start.22) | collective-permute-done | bytes 98336 | tf_op jit(solution)/shard_map/ppermute | solution.py:264
  78.4 1.5 %collective-permute-done.19.refs_5_ = bf16[32,1536]{1,0:T(8,128)(2,1)S(1)} collective-permute-done((bf16[32,1536]{1,0:T(8,128)(2,1)S(1)}, bf16[32,1536]{1,0:T(8,128)(2,1)S(1)}, u32[]{:S(2)}, u32[]{:S(2)}) %collective-permute-start.19) | collective-permute-done | bytes 98336 | tf_op jit(solution)/shard_map/ppermute | solution.py:264
  80.0 1.6 %shard_map.102 = bf16[32,12288]{1,0:T(8,128)(2,1)} custom-call(s32[2]{0:T(128)S(1)} %bitcast.9, bf16[32,1536]{1,0:T(8,128)(2,1)S(1)} %get-tuple-element.53.refs_0_, bf16[32,1536]{1,0:T(8,128)(2,1)S(1)} %collective-permute-done.13.refs_1_, bf16[32,1536]{1,0:T(8,128)(2,1)S(1)} %get-tuple-element.51.refs_2_, ...), custom_call_target="tpu_custom_call" | custom-call | tf_op jit(solution)/shard_map/pallas_call | solution.py:254
  81.6 0.9 %shard_map.97 = bf16[32,12288]{1,0:T(8,128)(2,1)} custom-call(bf16[32,1536]{1,0:T(8,128)(2,1)S(1)} %get-tuple-element.57.refs_0_, bf16[32,1536]{1,0:T(8,128)(2,1)S(1)} %collective-permute-done.3.refs_1_, bf16[32,1536]{1,0:T(8,128)(2,1)S(1)} %get-tuple-element.61.refs_2_, bf16[32,1536]{1,0:T(8,128)(2,1)S(1)} %collective-permute-done.5.refs_3_, ...), custom_call_target="tpu_custom_call" | custom-call | tf_op jit(solution)/shard_map/pallas_call | solution.py:227
  (52 shorter events, 7.4 us)
Async XLA Ops:
  0.7 21.7 %collective-permute-start = (bf16[128,3072]{1,0:T(8,128)(2,1)}, bf16[128,3072]{1,0:T(8,128)(2,1)S(1)}, u32[]{:S(2)}, u32[]{:S(2)}) collective-permute-start(bf16[128,3072]{1,0:T(8,128)(2,1)} %own.7), channel_id=1, source_target_pairs={{0,4},{4,0},{1,5},{5,1},{2,6},{6,2},{3,7},{7,3},{8,12},{12,8},{9,1... | collective-permute-start | bytes 2359304 | tf_op jit(solution)/shard_map/ppermute | solution.py:264
  4.3 18.0 %copy-start = (bf16[128,3072]{1,0:T(8,128)(2,1)S(1)}, bf16[128,3072]{1,0:T(8,128)(2,1)}, u32[]{:S(2)}) copy-start(bf16[128,3072]{1,0:T(8,128)(2,1)} %own.7) | copy-start | bytes 2359300
  25.6 5.9 %collective-permute-start.11 = (bf16[128,1536]{1,0:T(8,128)(2,1)S(1)}, bf16[128,1536]{1,0:T(8,128)(2,1)S(1)}, u32[]{:S(2)}, u32[]{:S(2)}) collective-permute-start(bf16[128,1536]{1,0:T(8,128)(2,1)S(1)} %get-tuple-element.31), channel_id=1, source_target_pairs={{0,1},{1,0},{2,3},{3,2},{4,5},{5,4},{6,7},{7,6},{8,9},{9,8},{10,11... | collective-permute-start | bytes 1179656 | tf_op jit(solution)/shard_map/ppermute | solution.py:264
  29.0 12.6 %collective-permute-start.14 = (bf16[128,1536]{1,0:T(8,128)(2,1)S(1)}, bf16[128,1536]{1,0:T(8,128)(2,1)S(1)}, u32[]{:S(2)}, u32[]{:S(2)}) collective-permute-start(bf16[128,1536]{1,0:T(8,128)(2,1)S(1)} %get-tuple-element.33), channel_id=1, source_target_pairs={{0,1},{1,0},{2,3},{3,2},{4,5},{5,4},{6,7},{7,6},{8,9},{9,8},{10,11... | collective-permute-start | bytes 1179656 | tf_op jit(solution)/shard_map/ppermute | solution.py:264
  29.5 12.0 %collective-permute-start.1 = (bf16[128,1536]{1,0:T(8,128)(2,1)S(1)}, bf16[128,1536]{1,0:T(8,128)(2,1)S(1)}, u32[]{:S(2)}, u32[]{:S(2)}) collective-permute-start(bf16[128,1536]{1,0:T(8,128)(2,1)S(1)} %get-tuple-element.26), channel_id=1, source_target_pairs={{0,4},{4,0},{1,5},{5,1},{2,6},{6,2},{3,7},{7,3},{8,12},{12,8},{9,1... | collective-permute-start | bytes 1179656 | tf_op jit(solution)/shard_map/ppermute | solution.py:264
  30.4 19.8 %collective-permute-start.6 = (bf16[128,1536]{1,0:T(8,128)(2,1)S(1)}, bf16[128,1536]{1,0:T(8,128)(2,1)S(1)}, u32[]{:S(2)}, u32[]{:S(2)}) collective-permute-start(bf16[128,1536]{1,0:T(8,128)(2,1)S(1)} %get-tuple-element.28), channel_id=1, source_target_pairs={{0,4},{4,0},{1,5},{5,1},{2,6},{6,2},{3,7},{7,3},{8,12},{12,8},{9,1... | collective-permute-start | bytes 1179656 | tf_op jit(solution)/shard_map/ppermute | solution.py:264
  35.1 19.1 %collective-permute-start.12 = (bf16[64,1536]{1,0:T(8,128)(2,1)S(1)}, bf16[64,1536]{1,0:T(8,128)(2,1)S(1)}, u32[]{:S(2)}, u32[]{:S(2)}) collective-permute-start(bf16[64,1536]{1,0:T(8,128)(2,1)S(1)} %get-tuple-element.45.refs_0_), channel_id=1, source_target_pairs={{0,2},{1,3},{2,0},{3,1},{4,6},{5,7},{6,4},{7,5},{8,10},{9,11},{10,... | collective-permute-start | bytes 589832 | tf_op jit(solution)/shard_map/ppermute | solution.py:264
  41.7 9.0 %collective-permute-start.15 = (bf16[64,1536]{1,0:T(8,128)(2,1)S(1)}, bf16[64,1536]{1,0:T(8,128)(2,1)S(1)}, u32[]{:S(2)}, u32[]{:S(2)}) collective-permute-start(bf16[64,1536]{1,0:T(8,128)(2,1)S(1)} %get-tuple-element.43.refs_0_), channel_id=1, source_target_pairs={{0,2},{1,3},{2,0},{3,1},{4,6},{5,7},{6,4},{7,5},{8,10},{9,11},{10,... | collective-permute-start | bytes 589832 | tf_op jit(solution)/shard_map/ppermute | solution.py:264
  46.5 12.3 %collective-permute-start.2 = (bf16[128,1536]{1,0:T(8,128)(2,1)S(1)}, bf16[128,1536]{1,0:T(8,128)(2,1)S(1)}, u32[]{:S(2)}, u32[]{:S(2)}) collective-permute-start(bf16[128,1536]{1,0:T(8,128)(2,1)S(1)} %add_convert_fusion.1.refs_1_), channel_id=1, source_target_pairs={{0,8},{8,16},{16,24},{1,9},{9,17},{17,25},{2,10},{10,18},{18,26},{... | collective-permute-start | bytes 1179656 | tf_op jit(solution)/shard_map/ppermute | solution.py:321
  50.0 5.2 %collective-permute-start.20 = (bf16[128,1536]{1,0:T(8,128)(2,1)S(1)}, bf16[128,1536]{1,0:T(8,128)(2,1)S(1)}, u32[]{:S(2)}, u32[]{:S(2)}) collective-permute-start(bf16[128,1536]{1,0:T(8,128)(2,1)S(1)} %get-tuple-element.37), channel_id=1, source_target_pairs={{0,1},{1,0},{2,3},{3,2},{4,5},{5,4},{6,7},{7,6},{8,9},{9,8},{10,11... | collective-permute-start | bytes 1179656 | tf_op jit(solution)/shard_map/ppermute | solution.py:264
  50.1 6.5 %collective-permute-start.17 = (bf16[128,1536]{1,0:T(8,128)(2,1)S(1)}, bf16[128,1536]{1,0:T(8,128)(2,1)S(1)}, u32[]{:S(2)}, u32[]{:S(2)}) collective-permute-start(bf16[128,1536]{1,0:T(8,128)(2,1)S(1)} %get-tuple-element.35), channel_id=1, source_target_pairs={{0,1},{1,0},{2,3},{3,2},{4,5},{5,4},{6,7},{7,6},{8,9},{9,8},{10,11... | collective-permute-start | bytes 1179656 | tf_op jit(solution)/shard_map/ppermute | solution.py:264
  50.7 14.3 %collective-permute-start.7 = (bf16[128,1536]{1,0:T(8,128)(2,1)S(1)}, bf16[128,1536]{1,0:T(8,128)(2,1)S(1)}, u32[]{:S(2)}, u32[]{:S(2)}) collective-permute-start(bf16[128,1536]{1,0:T(8,128)(2,1)S(1)} %add_convert_fusion), channel_id=1, source_target_pairs={{0,8},{8,16},{16,24},{1,9},{9,17},{17,25},{2,10},{10,18},{18,26},{... | collective-permute-start | bytes 1179656 | tf_op jit(solution)/shard_map/ppermute | solution.py:321
  54.3 21.9 %collective-permute-start.16 = (bf16[32,1536]{1,0:T(8,128)(2,1)S(1)}, bf16[32,1536]{1,0:T(8,128)(2,1)S(1)}, u32[]{:S(2)}, u32[]{:S(2)}) collective-permute-start(bf16[32,1536]{1,0:T(8,128)(2,1)S(1)} %get-tuple-element.50), channel_id=1, source_target_pairs={{0,4},{4,0},{1,5},{5,1},{2,6},{6,2},{3,7},{7,3},{8,12},{12,8},{9,1... | collective-permute-start | bytes 294920 | tf_op jit(solution)/shard_map/ppermute | solution.py:264
  55.2 21.1 %collective-permute-start.13 = (bf16[32,1536]{1,0:T(8,128)(2,1)S(1)}, bf16[32,1536]{1,0:T(8,128)(2,1)S(1)}, u32[]{:S(2)}, u32[]{:S(2)}) collective-permute-start(bf16[32,1536]{1,0:T(8,128)(2,1)S(1)} %get-tuple-element.52), channel_id=1, source_target_pairs={{0,4},{4,0},{1,5},{5,1},{2,6},{6,2},{3,7},{7,3},{8,12},{12,8},{9,1... | collective-permute-start | bytes 294920 | tf_op jit(solution)/shard_map/ppermute | solution.py:264
  56.6 9.0 %collective-permute-start.21 = (bf16[64,1536]{1,0:T(8,128)(2,1)S(1)}, bf16[64,1536]{1,0:T(8,128)(2,1)S(1)}, u32[]{:S(2)}, u32[]{:S(2)}) collective-permute-start(bf16[64,1536]{1,0:T(8,128)(2,1)S(1)} %get-tuple-element.39), channel_id=1, source_target_pairs={{0,2},{1,3},{2,0},{3,1},{4,6},{5,7},{6,4},{7,5},{8,10},{9,11},{10,... | collective-permute-start | bytes 589832 | tf_op jit(solution)/shard_map/ppermute | solution.py:264
  58.8 9.4 %collective-permute-start.18 = (bf16[64,1536]{1,0:T(8,128)(2,1)S(1)}, bf16[64,1536]{1,0:T(8,128)(2,1)S(1)}, u32[]{:S(2)}, u32[]{:S(2)}) collective-permute-start(bf16[64,1536]{1,0:T(8,128)(2,1)S(1)} %get-tuple-element.41), channel_id=1, source_target_pairs={{0,2},{1,3},{2,0},{3,1},{4,6},{5,7},{6,4},{7,5},{8,10},{9,11},{10,... | collective-permute-start | bytes 589832 | tf_op jit(solution)/shard_map/ppermute | solution.py:264
  65.0 7.8 %collective-permute-start.4 = (bf16[64,1536]{1,0:T(8,128)(2,1)S(1)}, bf16[64,1536]{1,0:T(8,128)(2,1)S(1)}, u32[]{:S(2)}, u32[]{:S(2)}) collective-permute-start(bf16[64,1536]{1,0:T(8,128)(2,1)S(1)} %slice.176), channel_id=1, source_target_pairs={{0,2},{1,3},{2,0},{3,1},{4,6},{5,7},{6,4},{7,5},{8,10},{9,11},{10,... | collective-permute-start | bytes 589832 | tf_op jit(solution)/shard_map/ppermute | solution.py:264
  65.6 15.9 %collective-permute-start.3 = (bf16[32,1536]{1,0:T(8,128)(2,1)S(1)}, bf16[32,1536]{1,0:T(8,128)(2,1)S(1)}, u32[]{:S(2)}, u32[]{:S(2)}) collective-permute-start(bf16[32,1536]{1,0:T(8,128)(2,1)S(1)} %get-tuple-element.56), channel_id=1, source_target_pairs={{0,1},{1,0},{2,3},{3,2},{4,5},{5,4},{6,7},{7,6},{8,9},{9,8},{10,11... | collective-permute-start | bytes 294920 | tf_op jit(solution)/shard_map/ppermute | solution.py:264
  68.2 7.1 %collective-permute-start.9 = (bf16[64,1536]{1,0:T(8,128)(2,1)S(1)}, bf16[64,1536]{1,0:T(8,128)(2,1)S(1)}, u32[]{:S(2)}, u32[]{:S(2)}) collective-permute-start(bf16[64,1536]{1,0:T(8,128)(2,1)S(1)} %slice.181), channel_id=1, source_target_pairs={{0,2},{1,3},{2,0},{3,1},{4,6},{5,7},{6,4},{7,5},{8,10},{9,11},{10,... | collective-permute-start | bytes 589832 | tf_op jit(solution)/shard_map/ppermute | solution.py:264
  72.9 5.6 %collective-permute-start.22 = (bf16[32,1536]{1,0:T(8,128)(2,1)S(1)}, bf16[32,1536]{1,0:T(8,128)(2,1)S(1)}, u32[]{:S(2)}, u32[]{:S(2)}) collective-permute-start(bf16[32,1536]{1,0:T(8,128)(2,1)S(1)} %get-tuple-element.46), channel_id=1, source_target_pairs={{0,4},{4,0},{1,5},{5,1},{2,6},{6,2},{3,7},{7,3},{8,12},{12,8},{9,1... | collective-permute-start | bytes 294920 | tf_op jit(solution)/shard_map/ppermute | solution.py:264
  75.4 4.6 %collective-permute-start.19 = (bf16[32,1536]{1,0:T(8,128)(2,1)S(1)}, bf16[32,1536]{1,0:T(8,128)(2,1)S(1)}, u32[]{:S(2)}, u32[]{:S(2)}) collective-permute-start(bf16[32,1536]{1,0:T(8,128)(2,1)S(1)} %get-tuple-element.48), channel_id=1, source_target_pairs={{0,4},{4,0},{1,5},{5,1},{2,6},{6,2},{3,7},{7,3},{8,12},{12,8},{9,1... | collective-permute-start | bytes 294920 | tf_op jit(solution)/shard_map/ppermute | solution.py:264
  76.2 5.3 %collective-permute-start.8 = (bf16[32,1536]{1,0:T(8,128)(2,1)S(1)}, bf16[32,1536]{1,0:T(8,128)(2,1)S(1)}, u32[]{:S(2)}, u32[]{:S(2)}) collective-permute-start(bf16[32,1536]{1,0:T(8,128)(2,1)S(1)} %get-tuple-element.54), channel_id=1, source_target_pairs={{0,1},{1,0},{2,3},{3,2},{4,5},{5,4},{6,7},{7,6},{8,9},{9,8},{10,11... | collective-permute-start | bytes 294920 | tf_op jit(solution)/shard_map/ppermute | solution.py:264
  76.3 5.3 %collective-permute-start.5 = (bf16[32,1536]{1,0:T(8,128)(2,1)S(1)}, bf16[32,1536]{1,0:T(8,128)(2,1)S(1)}, u32[]{:S(2)}, u32[]{:S(2)}) collective-permute-start(bf16[32,1536]{1,0:T(8,128)(2,1)S(1)} %get-tuple-element.60), channel_id=1, source_target_pairs={{0,1},{1,0},{2,3},{3,2},{4,5},{5,4},{6,7},{7,6},{8,9},{9,8},{10,11... | collective-permute-start | bytes 294920 | tf_op jit(solution)/shard_map/ppermute | solution.py:264
  78.4 3.1 %collective-permute-start.10 = (bf16[32,1536]{1,0:T(8,128)(2,1)S(1)}, bf16[32,1536]{1,0:T(8,128)(2,1)S(1)}, u32[]{:S(2)}, u32[]{:S(2)}) collective-permute-start(bf16[32,1536]{1,0:T(8,128)(2,1)S(1)} %get-tuple-element.58), channel_id=1, source_target_pairs={{0,1},{1,0},{2,3},{3,2},{4,5},{5,4},{6,7},{7,6},{8,9},{9,8},{10,11... | collective-permute-start | bytes 294920 | tf_op jit(solution)/shard_map/ppermute | solution.py:264
  (2 other events, 21.7 us)

commit v3 on v2

--- a/solution.py
+++ b/solution.py
@@ -7,6 +7,7 @@
 from jax.experimental.pallas import tpu as pltpu
 from jax.sharding import PartitionSpec as P
 
+AFTER = ((), (), ('c0','y0'), ('k2','c1'))
 F_PARTS = 2
 B_PARTS = 4
 
@@ -203,22 +204,16 @@
 
 
 def place_forward_kernel(*refs):
-    pieces, out, sems = refs[:-2], refs[-2], refs[-1]
+    pieces, out = refs[:-1], refs[-1]
     c = lax.axis_index("col")
     width = out.shape[1] // 4
-    copies = []
+    first_section = lax.axis_index("section") == 0
     for dc in range(4):
         at = (c ^ dc) * width
         for piece in pieces[dc::4]:
-            copies.append(
-                pltpu.make_async_copy(
-                    piece, out.at[:, pl.ds(pl.multiple_of(at, 128), piece.shape[1])], sems.at[len(copies)]
-                )
-            )
-            copies[-1].start()
+            value = jnp.where(first_section, 0.0, piece[...].astype(jnp.float32)).astype(out.dtype)
+            out[:, pl.ds(pl.multiple_of(at, 128), piece.shape[1])] = value
             at += piece.shape[1]
-    for copy in copies:
-        copy.wait()
 
 
 def place_forward(pieces):
@@ -227,9 +222,8 @@
     return pl.pallas_call(
         place_forward_kernel,
         out_shape=jax.ShapeDtypeStruct((rows, width), pieces[0].dtype),
-        in_specs=[ANY] * len(pieces),
-        out_specs=ANY,
-        scratch_shapes=[pltpu.SemaphoreType.DMA((len(pieces),))],
+        in_specs=[VMEM] * len(pieces),
+        out_specs=VMEM,
         compiler_params=PARAMS,
     )(*pieces)
 
@@ -262,6 +256,11 @@
 
 def swap(x, axis, by):
     return lax.ppermute(x, axis, [(i, i ^ by) for i in range(lax.axis_size(axis))])
+
+
+def around(x, axis, by):
+    length = lax.axis_size(axis)
+    return lax.ppermute(x, axis, [(i, (i + by) % length) for i in range(length)])
 
 
 def added(a, b):
@@ -290,23 +289,26 @@
     keeps, sends = parts[::2], parts[1::2]
     *sends, dy_other = lax.optimization_barrier((*sends, dy_other))
 
+    y_received = [swap(send, "row", 1) for send in sends]
     y_pieces, dx_pieces = [], []
     forward_sums, backward_sums = [], []
+    marks = {}
     for part in range(B_PARTS):
-        after = backward_sums[part - 2 : part - 1] if part >= 2 else []
-        if part == B_PARTS - 1:
-            after = after + forward_sums[:1]
+        after = [marks[name] for name in AFTER[part]]
         keep, send = backward(part, slot_of, dy_bwd, dy_other, w, after)
+        marks[f"k{part}"] = keep
         if part < F_PARTS:
-            summed = added(keeps[part], swap(sends[part], "row", 1))
+            summed = added(keeps[part], y_received[part])
             forward_sums.append(summed)
-            shifted = passed_along(summed, "section", 1)
+            marks[f'y{part}'] = summed
+            shifted = around(summed, "section", 1)
             here, there = shifted[: 2 * owned], swap(shifted[2 * owned :], "col", 2)
             y_pieces += [here[:owned], swap(here[owned:], "col", 1), there[:owned], swap(there[owned:], "col", 1)]
         received = swap(send, "col", 1)
         half = keep.shape[0] // 2
         onward = added(keep[half:], received[half:])
         backward_sums.append(onward)
+        marks[f'c{part}'] = onward
         kept = added(keep[:half], received[:half])
         received = swap(onward, "col", 2)
         onward = added(kept[owned:], received[owned:])

time: 82.9 us -> 75.2 us (0.907)
  waiting for transfers between devices: 23.4 us -> 16.7 us
  starting transfers between devices: 23 us -> 22.1 us
    ppermute x21, waiting for transfers between devices: 16.2 us -> 10.7 us  [swap(): lax.ppermute(x, axis, [(i, i ^ by) for i in range(lax.axis_size(axis))])]
    ppermute x2, starting transfers between devices: 6.99 us -> 3.21 us  [around(): lax.ppermute(x, axis, [(i, (i + by) % length) for i in range(length)])]
    ppermute x21, starting transfers between devices: 16 us -> 18.9 us  [swap(): lax.ppermute(x, axis, [(i, i ^ by) for i in range(lax.axis_size(axis))])]
    ppermute x2, waiting for transfers between devices: 7.18 us -> 5.99 us  [around(): lax.ppermute(x, axis, [(i, (i + by) % length) for i in range(length)])]
  transfers between devices with their start and end apart: 23 -> 23, of which waited for: 8 -> 7; matrix products, arithmetic and copies ran while one was open for 1% -> 1% of each run, Pallas kernels for 36% -> 44%
where the time goes in v3:
time: 75.2 us; the launch traced here: 75.1 us
  Pallas kernels  33.8 us (45%)
  starting transfers between devices  22.1 us (29%)
  waiting for transfers between devices  16.7 us (22%)
  between operations  1.59 us (2%)
  other arithmetic  0.78 us (1%)
    ppermute x21, starting transfers between devices, swap(): lax.ppermute(x, axis, [(i, i ^ by) for i in range(lax.axis_size(axis))])  18.9 us
    pallas_call x4, Pallas kernels, backward(): pl.pallas_call(functools.partial(backward_kernel, part * (block_rows // B...  13.2 us
    pallas_call x1, Pallas kernels, forward(): pl.pallas_call(functools.partial(forward_kernel, block), out_shape=(shape...  10.8 us
    ppermute x21, waiting for transfers between devices, swap(): lax.ppermute(x, axis, [(i, i ^ by) for i in range(lax.axis_size(axis))])  10.7 us
    pallas_call x1, Pallas kernels, prep(): pl.pallas_call(functools.partial(prep_kernel, owned, block_rows, block_co...  7.15 us
    ppermute x2, waiting for transfers between devices, around(): lax.ppermute(x, axis, [(i, (i + by) % length) for i in range(length)])  5.99 us
    ppermute x2, starting transfers between devices, around(): lax.ppermute(x, axis, [(i, (i + by) % length) for i in range(length)])  3.21 us
    pallas_call x1, Pallas kernels, place_backward(): pl.pallas_call(place_backward_kernel, out_shape=jax.ShapeDtypeStruct((row...  1.58 us
  transfers between devices with their start and end apart: 23, of which 7 were waited for; matrix products, arithmetic and copies ran while one was open for 1% of the time, Pallas kernels for 44%

profile of v3, /device:TPU:0, one launch (start us, length us, event | category | flops | bytes accessed | tf_op | source)
XLA Modules:
  0.0 75.1 jit_solution(2875718400649953129)
XLA Ops:
  0.7 3.0 %collective-permute-start = (bf16[128,3072]{1,0:T(8,128)(2,1)}, bf16[128,3072]{1,0:T(8,128)(2,1)S(1)}, u32[]{:S(2)}, u32[]{:S(2)}) collective-permute-start(bf16[128,3072]{1,0:T(8,128)(2,1)} %own.7), channel_id=1, source_target_pairs={{0,4},{4,0},{1,5},{5,1},{2,6},{6,2},{3,7},{7,3},{8,12},{12,8},{9,1... | collective-permute-start | bytes 2359304 | tf_op jit(solution)/shard_map/ppermute | solution.py:258
  4.3 7.2 %shard_map.95 = (bf16[461,128,128]{2,1,0:T(8,128)(2,1)S(1)}, bf16[256,6144]{1,0:T(8,128)(2,1)S(1)}, s32[1153]{0:T(1024)S(1)}) custom-call(s32[1]{0:T(128)} %bitcast.6.count, s32[1,460]{1,0:T(1,128)} %bitcast.11, s32[1,460]{1,0:T(1,128)} %bitcast.12, s32[1,16]{1,0:T(1,128)} %order_hbm.1, bf16[460,128,128]{2,1,0:T(8,128)(2,1)} %bitcast.10, bf16[256,6144]{1,0:T(8,128)(2,1)} %x_hbm.1), custom_call_target="tpu_custom_call" | custom-call | tf_op jit(solution)/shard_map/pallas_call | solution.py:97
  11.5 10.8 %shard_map.96 = (bf16[128,1536]{1,0:T(8,128)(2,1)S(1)}, bf16[128,1536]{1,0:T(8,128)(2,1)S(1)}, bf16[128,1536]{1,0:T(8,128)(2,1)S(1)}, bf16[128,1536]{1,0:T(8,128)(2,1)S(1)}) custom-call(s32[16]{0:T(128)S(1)} %bitcast.7, s32[2]{0:T(128)S(1)} %bitcast.8, s32[1153]{0:T(1024)S(1)} %get-tuple-element.20.slot_of, bf16[256,6144]{1,0:T(8,128)(2,1)S(1)} %get-tuple-element.21.x, ...), custom_call_target="tpu_custom_call" | custom-call | flops 1000 | bytes 1000 | tf_op jit(solution)/shard_map/pallas_call | solution.py:150
  23.2 3.3 %shard_map.98 = (bf16[128,1536]{1,0:T(8,128)(2,1)S(1)}, bf16[128,1536]{1,0:T(8,128)(2,1)S(1)}) custom-call(s32[1153]{0:T(1024)S(1)} %get-tuple-element.20.slot_of, bf16[128,3072]{1,0:T(8,128)(2,1)S(1)} %copy-done, bf16[128,3072]{1,0:T(8,128)(2,1)S(1)} %collective-permute-done.other, bf16[461,128,128]{2,1,0:T(8,128)(2,1)S(1)} %get-tuple-element.22.w), custom_call_target="tpu_custom_call" | custom-call | flops 1000 | bytes 1000 | tf_op jit(solution)/shard_map/pallas_call | solution.py:195
  26.4 3.3 %shard_map.99 = (bf16[128,1536]{1,0:T(8,128)(2,1)S(1)}, bf16[128,1536]{1,0:T(8,128)(2,1)S(1)}) custom-call(s32[1153]{0:T(1024)S(1)} %get-tuple-element.20.slot_of, bf16[128,3072]{1,0:T(8,128)(2,1)S(1)} %copy-done, bf16[128,3072]{1,0:T(8,128)(2,1)S(1)} %collective-permute-done.other, bf16[461,128,128]{2,1,0:T(8,128)(2,1)S(1)} %get-tuple-element.22.w), custom_call_target="tpu_custom_call" | custom-call | flops 1000 | bytes 1000 | tf_op jit(solution)/shard_map/pallas_call | solution.py:195
  30.3 1.3 %collective-permute-start.6 = (bf16[128,1536]{1,0:T(8,128)(2,1)S(1)}, bf16[128,1536]{1,0:T(8,128)(2,1)S(1)}, u32[]{:S(2)}, u32[]{:S(2)}) collective-permute-start(bf16[128,1536]{1,0:T(8,128)(2,1)S(1)} %get-tuple-element.28), channel_id=1, source_target_pairs={{0,4},{4,0},{1,5},{5,1},{2,6},{6,2},{3,7},{7,3},{8,12},{12,8},{9,1... | collective-permute-start | bytes 1179656 | tf_op jit(solution)/shard_map/ppermute | solution.py:258
  31.5 1.4 %collective-permute-done.1 = bf16[128,1536]{1,0:T(8,128)(2,1)S(1)} collective-permute-done((bf16[128,1536]{1,0:T(8,128)(2,1)S(1)}, bf16[128,1536]{1,0:T(8,128)(2,1)S(1)}, u32[]{:S(2)}, u32[]{:S(2)}) %collective-permute-start.1) | collective-permute-done | bytes 393248 | tf_op jit(solution)/shard_map/ppermute | solution.py:258
  33.2 1.6 %collective-permute-start.12 = (bf16[64,1536]{1,0:T(8,128)(2,1)S(1)}, bf16[64,1536]{1,0:T(8,128)(2,1)S(1)}, u32[]{:S(2)}, u32[]{:S(2)}) collective-permute-start(bf16[64,1536]{1,0:T(8,128)(2,1)S(1)} %get-tuple-element.45.refs_0_), channel_id=1, source_target_pairs={{0,2},{1,3},{2,0},{3,1},{4,6},{5,7},{6,4},{7,5},{8,10},{9,11},{10,... | collective-permute-start | bytes 589832 | tf_op jit(solution)/shard_map/ppermute | solution.py:258
  34.8 3.5 %shard_map.100 = (bf16[128,1536]{1,0:T(8,128)(2,1)S(1)}, bf16[128,1536]{1,0:T(8,128)(2,1)S(1)}) custom-call(s32[1153]{0:T(1024)S(1)} %get-tuple-element.20.slot_of, bf16[128,3072]{1,0:T(8,128)(2,1)S(1)} %copy-done, bf16[128,3072]{1,0:T(8,128)(2,1)S(1)} %collective-permute-done.other, bf16[461,128,128]{2,1,0:T(8,128)(2,1)S(1)} %get-tuple-element.22.w, ...), custom_call_target="tpu_custom_call" | custom-call | flops 1000 | bytes 1000 | tf_op jit(solution)/shard_map/pallas_call | solution.py:195
  38.2 1.6 %collective-permute-start.2 = (bf16[128,1536]{1,0:T(8,128)(2,1)S(1)}, bf16[128,1536]{1,0:T(8,128)(2,1)S(1)}, u32[]{:S(2)}, u32[]{:S(2)}) collective-permute-start(bf16[128,1536]{1,0:T(8,128)(2,1)S(1)} %add_convert_fusion.1.refs_1_), channel_id=1, source_target_pairs={{0,8},{8,16},{16,24},{24,0},{1,9},{9,17},{17,25},{25,1},{2,10},{10... | collective-permute-start | bytes 1179656 | tf_op jit(solution)/shard_map/ppermute | solution.py:263
  40.6 3.3 %shard_map.101 = (bf16[128,1536]{1,0:T(8,128)(2,1)S(1)}, bf16[128,1536]{1,0:T(8,128)(2,1)S(1)}) custom-call(s32[1153]{0:T(1024)S(1)} %get-tuple-element.20.slot_of, bf16[128,3072]{1,0:T(8,128)(2,1)S(1)} %copy-done, bf16[128,3072]{1,0:T(8,128)(2,1)S(1)} %collective-permute-done.other, bf16[461,128,128]{2,1,0:T(8,128)(2,1)S(1)} %get-tuple-element.22.w, ...), custom_call_target="tpu_custom_call" | custom-call | flops 1000 | bytes 1000 | tf_op jit(solution)/shard_map/pallas_call | solution.py:195
  44.5 1.2 %collective-permute-done.15 = bf16[64,1536]{1,0:T(8,128)(2,1)S(1)} collective-permute-done((bf16[64,1536]{1,0:T(8,128)(2,1)S(1)}, bf16[64,1536]{1,0:T(8,128)(2,1)S(1)}, u32[]{:S(2)}, u32[]{:S(2)}) %collective-permute-start.15) | collective-permute-done | bytes 196640 | tf_op jit(solution)/shard_map/ppermute | solution.py:258
  45.7 1.6 %collective-permute-start.7 = (bf16[128,1536]{1,0:T(8,128)(2,1)S(1)}, bf16[128,1536]{1,0:T(8,128)(2,1)S(1)}, u32[]{:S(2)}, u32[]{:S(2)}) collective-permute-start(bf16[128,1536]{1,0:T(8,128)(2,1)S(1)} %add_convert_fusion), channel_id=1, source_target_pairs={{0,8},{8,16},{16,24},{24,0},{1,9},{9,17},{17,25},{25,1},{2,10},{10... | collective-permute-start | bytes 1179656 | tf_op jit(solution)/shard_map/ppermute | solution.py:263
  48.0 1.6 %collective-permute-start.13 = (bf16[32,1536]{1,0:T(8,128)(2,1)S(1)}, bf16[32,1536]{1,0:T(8,128)(2,1)S(1)}, u32[]{:S(2)}, u32[]{:S(2)}) collective-permute-start(bf16[32,1536]{1,0:T(8,128)(2,1)S(1)} %get-tuple-element.52), channel_id=1, source_target_pairs={{0,4},{4,0},{1,5},{5,1},{2,6},{6,2},{3,7},{7,3},{8,12},{12,8},{9,1... | collective-permute-start | bytes 294920 | tf_op jit(solution)/shard_map/ppermute | solution.py:258
  50.4 1.6 %collective-permute-start.18 = (bf16[64,1536]{1,0:T(8,128)(2,1)S(1)}, bf16[64,1536]{1,0:T(8,128)(2,1)S(1)}, u32[]{:S(2)}, u32[]{:S(2)}) collective-permute-start(bf16[64,1536]{1,0:T(8,128)(2,1)S(1)} %get-tuple-element.41), channel_id=1, source_target_pairs={{0,2},{1,3},{2,0},{3,1},{4,6},{5,7},{6,4},{7,5},{8,10},{9,11},{10,... | collective-permute-start | bytes 589832 | tf_op jit(solution)/shard_map/ppermute | solution.py:258
  52.0 6.0 %collective-permute-done.7 = bf16[128,1536]{1,0:T(8,128)(2,1)S(1)} collective-permute-done((bf16[128,1536]{1,0:T(8,128)(2,1)S(1)}, bf16[128,1536]{1,0:T(8,128)(2,1)S(1)}, u32[]{:S(2)}, u32[]{:S(2)}) %collective-permute-start.7) | collective-permute-done | bytes 393248 | tf_op jit(solution)/shard_map/ppermute | solution.py:263
  57.9 1.0 %collective-permute-start.4 = (bf16[64,1536]{1,0:T(8,128)(2,1)S(1)}, bf16[64,1536]{1,0:T(8,128)(2,1)S(1)}, u32[]{:S(2)}, u32[]{:S(2)}) collective-permute-start(bf16[64,1536]{1,0:T(8,128)(2,1)S(1)} %slice.176), channel_id=1, source_target_pairs={{0,2},{1,3},{2,0},{3,1},{4,6},{5,7},{6,4},{7,5},{8,10},{9,11},{10,... | collective-permute-start | bytes 589832 | tf_op jit(solution)/shard_map/ppermute | solution.py:258
  59.2 1.2 %collective-permute-start.9 = (bf16[64,1536]{1,0:T(8,128)(2,1)S(1)}, bf16[64,1536]{1,0:T(8,128)(2,1)S(1)}, u32[]{:S(2)}, u32[]{:S(2)}) collective-permute-start(bf16[64,1536]{1,0:T(8,128)(2,1)S(1)} %slice.181), channel_id=1, source_target_pairs={{0,2},{1,3},{2,0},{3,1},{4,6},{5,7},{6,4},{7,5},{8,10},{9,11},{10,... | collective-permute-start | bytes 589832 | tf_op jit(solution)/shard_map/ppermute | solution.py:258
  60.4 4.5 %collective-permute-done.4 = bf16[64,1536]{1,0:T(8,128)(2,1)S(1)} collective-permute-done((bf16[64,1536]{1,0:T(8,128)(2,1)S(1)}, bf16[64,1536]{1,0:T(8,128)(2,1)S(1)}, u32[]{:S(2)}, u32[]{:S(2)}) %collective-permute-start.4) | collective-permute-done | bytes 196640 | tf_op jit(solution)/shard_map/ppermute | solution.py:258
  65.0 2.0 %collective-permute-start.22 = (bf16[32,1536]{1,0:T(8,128)(2,1)S(1)}, bf16[32,1536]{1,0:T(8,128)(2,1)S(1)}, u32[]{:S(2)}, u32[]{:S(2)}) collective-permute-start(bf16[32,1536]{1,0:T(8,128)(2,1)S(1)} %get-tuple-element.46), channel_id=1, source_target_pairs={{0,4},{4,0},{1,5},{5,1},{2,6},{6,2},{3,7},{7,3},{8,12},{12,8},{9,1... | collective-permute-start | bytes 294920 | tf_op jit(solution)/shard_map/ppermute | solution.py:258
  67.8 1.3 %collective-permute-start.19 = (bf16[32,1536]{1,0:T(8,128)(2,1)S(1)}, bf16[32,1536]{1,0:T(8,128)(2,1)S(1)}, u32[]{:S(2)}, u32[]{:S(2)}) collective-permute-start(bf16[32,1536]{1,0:T(8,128)(2,1)S(1)} %get-tuple-element.48), channel_id=1, source_target_pairs={{0,4},{4,0},{1,5},{5,1},{2,6},{6,2},{3,7},{7,3},{8,12},{12,8},{9,1... | collective-permute-start | bytes 294920 | tf_op jit(solution)/shard_map/ppermute | solution.py:258
  70.0 2.4 %collective-permute-done.19.refs_5_ = bf16[32,1536]{1,0:T(8,128)(2,1)S(1)} collective-permute-done((bf16[32,1536]{1,0:T(8,128)(2,1)S(1)}, bf16[32,1536]{1,0:T(8,128)(2,1)S(1)}, u32[]{:S(2)}, u32[]{:S(2)}) %collective-permute-start.19) | collective-permute-done | bytes 98336 | tf_op jit(solution)/shard_map/ppermute | solution.py:258
  72.4 1.6 %shard_map.102 = bf16[32,12288]{1,0:T(8,128)(2,1)} custom-call(s32[2]{0:T(128)S(1)} %bitcast.9, bf16[32,1536]{1,0:T(8,128)(2,1)S(1)} %get-tuple-element.53.refs_0_, bf16[32,1536]{1,0:T(8,128)(2,1)S(1)} %collective-permute-done.13.refs_1_, bf16[32,1536]{1,0:T(8,128)(2,1)S(1)} %get-tuple-element.51.refs_2_, ...), custom_call_target="tpu_custom_call" | custom-call | tf_op jit(solution)/shard_map/pallas_call | solution.py:248
  74.1 1.0 %shard_map.97 = bf16[32,12288]{1,0:T(8,128)(2,1)} custom-call(bf16[32,1536]{1,0:T(8,128)(2,1)S(1)} %get-tuple-element.57.refs_0_, bf16[32,1536]{1,0:T(8,128)(2,1)S(1)} %collective-permute-done.3.refs_1_, bf16[32,1536]{1,0:T(8,128)(2,1)S(1)} %get-tuple-element.61.refs_2_, bf16[32,1536]{1,0:T(8,128)(2,1)S(1)} %collective-permute-done.5.refs_3_, ...), custom_call_target="tpu_custom_call" | custom-call | tf_op jit(solution)/shard_map/pallas_call | solution.py:222
  (52 shorter events, 6.4 us)
Async XLA Ops:
  0.7 21.7 %collective-permute-start = (bf16[128,3072]{1,0:T(8,128)(2,1)}, bf16[128,3072]{1,0:T(8,128)(2,1)S(1)}, u32[]{:S(2)}, u32[]{:S(2)}) collective-permute-start(bf16[128,3072]{1,0:T(8,128)(2,1)} %own.7), channel_id=1, source_target_pairs={{0,4},{4,0},{1,5},{5,1},{2,6},{6,2},{3,7},{7,3},{8,12},{12,8},{9,1... | collective-permute-start | bytes 2359304 | tf_op jit(solution)/shard_map/ppermute | solution.py:258
  4.3 18.8 %copy-start = (bf16[128,3072]{1,0:T(8,128)(2,1)S(1)}, bf16[128,3072]{1,0:T(8,128)(2,1)}, u32[]{:S(2)}) copy-start(bf16[128,3072]{1,0:T(8,128)(2,1)} %own.7) | copy-start | bytes 2359300
  22.3 10.6 %collective-permute-start.1 = (bf16[128,1536]{1,0:T(8,128)(2,1)S(1)}, bf16[128,1536]{1,0:T(8,128)(2,1)S(1)}, u32[]{:S(2)}, u32[]{:S(2)}) collective-permute-start(bf16[128,1536]{1,0:T(8,128)(2,1)S(1)} %get-tuple-element.26), channel_id=1, source_target_pairs={{0,4},{4,0},{1,5},{5,1},{2,6},{6,2},{3,7},{7,3},{8,12},{12,8},{9,1... | collective-permute-start | bytes 1179656 | tf_op jit(solution)/shard_map/ppermute | solution.py:258
  29.7 3.4 %collective-permute-start.11 = (bf16[128,1536]{1,0:T(8,128)(2,1)S(1)}, bf16[128,1536]{1,0:T(8,128)(2,1)S(1)}, u32[]{:S(2)}, u32[]{:S(2)}) collective-permute-start(bf16[128,1536]{1,0:T(8,128)(2,1)S(1)} %get-tuple-element.31), channel_id=1, source_target_pairs={{0,1},{1,0},{2,3},{3,2},{4,5},{5,4},{6,7},{7,6},{8,9},{9,8},{10,11... | collective-permute-start | bytes 1179656 | tf_op jit(solution)/shard_map/ppermute | solution.py:258
  29.8 10.1 %collective-permute-start.14 = (bf16[128,1536]{1,0:T(8,128)(2,1)S(1)}, bf16[128,1536]{1,0:T(8,128)(2,1)S(1)}, u32[]{:S(2)}, u32[]{:S(2)}) collective-permute-start(bf16[128,1536]{1,0:T(8,128)(2,1)S(1)} %get-tuple-element.33), channel_id=1, source_target_pairs={{0,1},{1,0},{2,3},{3,2},{4,5},{5,4},{6,7},{7,6},{8,9},{9,8},{10,11... | collective-permute-start | bytes 1179656 | tf_op jit(solution)/shard_map/ppermute | solution.py:258
  30.3 13.6 %collective-permute-start.6 = (bf16[128,1536]{1,0:T(8,128)(2,1)S(1)}, bf16[128,1536]{1,0:T(8,128)(2,1)S(1)}, u32[]{:S(2)}, u32[]{:S(2)}) collective-permute-start(bf16[128,1536]{1,0:T(8,128)(2,1)S(1)} %get-tuple-element.28), channel_id=1, source_target_pairs={{0,4},{4,0},{1,5},{5,1},{2,6},{6,2},{3,7},{7,3},{8,12},{12,8},{9,1... | collective-permute-start | bytes 1179656 | tf_op jit(solution)/shard_map/ppermute | solution.py:258
  33.2 14.1 %collective-permute-start.12 = (bf16[64,1536]{1,0:T(8,128)(2,1)S(1)}, bf16[64,1536]{1,0:T(8,128)(2,1)S(1)}, u32[]{:S(2)}, u32[]{:S(2)}) collective-permute-start(bf16[64,1536]{1,0:T(8,128)(2,1)S(1)} %get-tuple-element.45.refs_0_), channel_id=1, source_target_pairs={{0,2},{1,3},{2,0},{3,1},{4,6},{5,7},{6,4},{7,5},{8,10},{9,11},{10,... | collective-permute-start | bytes 589832 | tf_op jit(solution)/shard_map/ppermute | solution.py:258
  38.2 12.1 %collective-permute-start.2 = (bf16[128,1536]{1,0:T(8,128)(2,1)S(1)}, bf16[128,1536]{1,0:T(8,128)(2,1)S(1)}, u32[]{:S(2)}, u32[]{:S(2)}) collective-permute-start(bf16[128,1536]{1,0:T(8,128)(2,1)S(1)} %add_convert_fusion.1.refs_1_), channel_id=1, source_target_pairs={{0,8},{8,16},{16,24},{24,0},{1,9},{9,17},{17,25},{25,1},{2,10},{10... | collective-permute-start | bytes 1179656 | tf_op jit(solution)/shard_map/ppermute | solution.py:263
  40.0 5.7 %collective-permute-start.15 = (bf16[64,1536]{1,0:T(8,128)(2,1)S(1)}, bf16[64,1536]{1,0:T(8,128)(2,1)S(1)}, u32[]{:S(2)}, u32[]{:S(2)}) collective-permute-start(bf16[64,1536]{1,0:T(8,128)(2,1)S(1)} %get-tuple-element.43.refs_1_), channel_id=1, source_target_pairs={{0,2},{1,3},{2,0},{3,1},{4,6},{5,7},{6,4},{7,5},{8,10},{9,11},{10,... | collective-permute-start | bytes 589832 | tf_op jit(solution)/shard_map/ppermute | solution.py:258
  43.8 4.1 %collective-permute-start.20 = (bf16[128,1536]{1,0:T(8,128)(2,1)S(1)}, bf16[128,1536]{1,0:T(8,128)(2,1)S(1)}, u32[]{:S(2)}, u32[]{:S(2)}) collective-permute-start(bf16[128,1536]{1,0:T(8,128)(2,1)S(1)} %get-tuple-element.37), channel_id=1, source_target_pairs={{0,1},{1,0},{2,3},{3,2},{4,5},{5,4},{6,7},{7,6},{8,9},{9,8},{10,11... | collective-permute-start | bytes 1179656 | tf_op jit(solution)/shard_map/ppermute | solution.py:258
  43.9 5.7 %collective-permute-start.17 = (bf16[128,1536]{1,0:T(8,128)(2,1)S(1)}, bf16[128,1536]{1,0:T(8,128)(2,1)S(1)}, u32[]{:S(2)}, u32[]{:S(2)}) collective-permute-start(bf16[128,1536]{1,0:T(8,128)(2,1)S(1)} %get-tuple-element.35), channel_id=1, source_target_pairs={{0,1},{1,0},{2,3},{3,2},{4,5},{5,4},{6,7},{7,6},{8,9},{9,8},{10,11... | collective-permute-start | bytes 1179656 | tf_op jit(solution)/shard_map/ppermute | solution.py:258
  45.7 12.3 %collective-permute-start.7 = (bf16[128,1536]{1,0:T(8,128)(2,1)S(1)}, bf16[128,1536]{1,0:T(8,128)(2,1)S(1)}, u32[]{:S(2)}, u32[]{:S(2)}) collective-permute-start(bf16[128,1536]{1,0:T(8,128)(2,1)S(1)} %add_convert_fusion), channel_id=1, source_target_pairs={{0,8},{8,16},{16,24},{24,0},{1,9},{9,17},{17,25},{25,1},{2,10},{10... | collective-permute-start | bytes 1179656 | tf_op jit(solution)/shard_map/ppermute | solution.py:263
  47.3 21.9 %collective-permute-start.16 = (bf16[32,1536]{1,0:T(8,128)(2,1)S(1)}, bf16[32,1536]{1,0:T(8,128)(2,1)S(1)}, u32[]{:S(2)}, u32[]{:S(2)}) collective-permute-start(bf16[32,1536]{1,0:T(8,128)(2,1)S(1)} %get-tuple-element.50), channel_id=1, source_target_pairs={{0,4},{4,0},{1,5},{5,1},{2,6},{6,2},{3,7},{7,3},{8,12},{12,8},{9,1... | collective-permute-start | bytes 294920 | tf_op jit(solution)/shard_map/ppermute | solution.py:258
  48.0 21.3 %collective-permute-start.13 = (bf16[32,1536]{1,0:T(8,128)(2,1)S(1)}, bf16[32,1536]{1,0:T(8,128)(2,1)S(1)}, u32[]{:S(2)}, u32[]{:S(2)}) collective-permute-start(bf16[32,1536]{1,0:T(8,128)(2,1)S(1)} %get-tuple-element.52), channel_id=1, source_target_pairs={{0,4},{4,0},{1,5},{5,1},{2,6},{6,2},{3,7},{7,3},{8,12},{12,8},{9,1... | collective-permute-start | bytes 294920 | tf_op jit(solution)/shard_map/ppermute | solution.py:258
  49.7 9.3 %collective-permute-start.21 = (bf16[64,1536]{1,0:T(8,128)(2,1)S(1)}, bf16[64,1536]{1,0:T(8,128)(2,1)S(1)}, u32[]{:S(2)}, u32[]{:S(2)}) collective-permute-start(bf16[64,1536]{1,0:T(8,128)(2,1)S(1)} %get-tuple-element.39), channel_id=1, source_target_pairs={{0,2},{1,3},{2,0},{3,1},{4,6},{5,7},{6,4},{7,5},{8,10},{9,11},{10,... | collective-permute-start | bytes 589832 | tf_op jit(solution)/shard_map/ppermute | solution.py:258
  50.4 8.8 %collective-permute-start.18 = (bf16[64,1536]{1,0:T(8,128)(2,1)S(1)}, bf16[64,1536]{1,0:T(8,128)(2,1)S(1)}, u32[]{:S(2)}, u32[]{:S(2)}) collective-permute-start(bf16[64,1536]{1,0:T(8,128)(2,1)S(1)} %get-tuple-element.41), channel_id=1, source_target_pairs={{0,2},{1,3},{2,0},{3,1},{4,6},{5,7},{6,4},{7,5},{8,10},{9,11},{10,... | collective-permute-start | bytes 589832 | tf_op jit(solution)/shard_map/ppermute | solution.py:258
  57.9 7.0 %collective-permute-start.4 = (bf16[64,1536]{1,0:T(8,128)(2,1)S(1)}, bf16[64,1536]{1,0:T(8,128)(2,1)S(1)}, u32[]{:S(2)}, u32[]{:S(2)}) collective-permute-start(bf16[64,1536]{1,0:T(8,128)(2,1)S(1)} %slice.176), channel_id=1, source_target_pairs={{0,2},{1,3},{2,0},{3,1},{4,6},{5,7},{6,4},{7,5},{8,10},{9,11},{10,... | collective-permute-start | bytes 589832 | tf_op jit(solution)/shard_map/ppermute | solution.py:258
  59.0 15.0 %collective-permute-start.3 = (bf16[32,1536]{1,0:T(8,128)(2,1)S(1)}, bf16[32,1536]{1,0:T(8,128)(2,1)S(1)}, u32[]{:S(2)}, u32[]{:S(2)}) collective-permute-start(bf16[32,1536]{1,0:T(8,128)(2,1)S(1)} %get-tuple-element.56), channel_id=1, source_target_pairs={{0,1},{1,0},{2,3},{3,2},{4,5},{5,4},{6,7},{7,6},{8,9},{9,8},{10,11... | collective-permute-start | bytes 294920 | tf_op jit(solution)/shard_map/ppermute | solution.py:258
  59.2 8.7 %collective-permute-start.9 = (bf16[64,1536]{1,0:T(8,128)(2,1)S(1)}, bf16[64,1536]{1,0:T(8,128)(2,1)S(1)}, u32[]{:S(2)}, u32[]{:S(2)}) collective-permute-start(bf16[64,1536]{1,0:T(8,128)(2,1)S(1)} %slice.181), channel_id=1, source_target_pairs={{0,2},{1,3},{2,0},{3,1},{4,6},{5,7},{6,4},{7,5},{8,10},{9,11},{10,... | collective-permute-start | bytes 589832 | tf_op jit(solution)/shard_map/ppermute | solution.py:258
  65.0 5.0 %collective-permute-start.22 = (bf16[32,1536]{1,0:T(8,128)(2,1)S(1)}, bf16[32,1536]{1,0:T(8,128)(2,1)S(1)}, u32[]{:S(2)}, u32[]{:S(2)}) collective-permute-start(bf16[32,1536]{1,0:T(8,128)(2,1)S(1)} %get-tuple-element.46), channel_id=1, source_target_pairs={{0,4},{4,0},{1,5},{5,1},{2,6},{6,2},{3,7},{7,3},{8,12},{12,8},{9,1... | collective-permute-start | bytes 294920 | tf_op jit(solution)/shard_map/ppermute | solution.py:258
  67.8 4.6 %collective-permute-start.19 = (bf16[32,1536]{1,0:T(8,128)(2,1)S(1)}, bf16[32,1536]{1,0:T(8,128)(2,1)S(1)}, u32[]{:S(2)}, u32[]{:S(2)}) collective-permute-start(bf16[32,1536]{1,0:T(8,128)(2,1)S(1)} %get-tuple-element.48), channel_id=1, source_target_pairs={{0,4},{4,0},{1,5},{5,1},{2,6},{6,2},{3,7},{7,3},{8,12},{12,8},{9,1... | collective-permute-start | bytes 294920 | tf_op jit(solution)/shard_map/ppermute | solution.py:258
  69.2 4.8 %collective-permute-start.8 = (bf16[32,1536]{1,0:T(8,128)(2,1)S(1)}, bf16[32,1536]{1,0:T(8,128)(2,1)S(1)}, u32[]{:S(2)}, u32[]{:S(2)}) collective-permute-start(bf16[32,1536]{1,0:T(8,128)(2,1)S(1)} %get-tuple-element.54), channel_id=1, source_target_pairs={{0,1},{1,0},{2,3},{3,2},{4,5},{5,4},{6,7},{7,6},{8,9},{9,8},{10,11... | collective-permute-start | bytes 294920 | tf_op jit(solution)/shard_map/ppermute | solution.py:258
  69.3 4.8 %collective-permute-start.5 = (bf16[32,1536]{1,0:T(8,128)(2,1)S(1)}, bf16[32,1536]{1,0:T(8,128)(2,1)S(1)}, u32[]{:S(2)}, u32[]{:S(2)}) collective-permute-start(bf16[32,1536]{1,0:T(8,128)(2,1)S(1)} %get-tuple-element.60), channel_id=1, source_target_pairs={{0,1},{1,0},{2,3},{3,2},{4,5},{5,4},{6,7},{7,6},{8,9},{9,8},{10,11... | collective-permute-start | bytes 294920 | tf_op jit(solution)/shard_map/ppermute | solution.py:258
  70.0 4.0 %collective-permute-start.10 = (bf16[32,1536]{1,0:T(8,128)(2,1)S(1)}, bf16[32,1536]{1,0:T(8,128)(2,1)S(1)}, u32[]{:S(2)}, u32[]{:S(2)}) collective-permute-start(bf16[32,1536]{1,0:T(8,128)(2,1)S(1)} %get-tuple-element.58), channel_id=1, source_target_pairs={{0,1},{1,0},{2,3},{3,2},{4,5},{5,4},{6,7},{7,6},{8,9},{9,8},{10,11... | collective-permute-start | bytes 294920 | tf_op jit(solution)/shard_map/ppermute | solution.py:258
  (2 other events, 21.7 us)

commit v4 on v3

--- a/solution.py
+++ b/solution.py
@@ -7,9 +7,20 @@
 from jax.experimental.pallas import tpu as pltpu
 from jax.sharding import PartitionSpec as P
 
-AFTER = ((), (), ('c0','y0'), ('k2','c1'))
-F_PARTS = 2
-B_PARTS = 4
+
+F_PAIRS = (4, 8)
+B_PAIRS = (7, 9, 8)
+F_FAR_FIRST = (False, True)
+TIES = {
+    "b0": ("z0", "x1",),
+    "fa0": ("z1",),
+    "fb0": ("x0", "b0",),
+    "k2": ("c0",),
+    "u1": ("d0",),
+    "y0": ("d0",),
+    "y1": ("d0",),
+    "z1": ("z0",),
+}
 
 VMEM = pl.BlockSpec(memory_space=pltpu.VMEM)
 SMEM = pl.BlockSpec(memory_space=pltpu.SMEM)
@@ -113,7 +124,7 @@
     )(count, *[in_hbm(a) for a in (*lists, weights, x)])
 
 
-def forward_kernel(block, order, limits, slot_of, x, w, *outs):
+def forward_kernel(block, block_cols, order, limits, slot_of, x, w, *outs):
     r, c = lax.axis_index("row"), lax.axis_index("col")
     rows = x.shape[0]
     half = rows // 2
@@ -127,10 +138,21 @@
                 first = order[((r ^ dr) * 4 + (c ^ dc)) * per_owner + b] * block
                 tokens.append(first + lax.broadcasted_iota(jnp.int32, (block, pair), 0))
     live = jnp.concatenate(tokens, axis=0) < limits[0]
-    block_cols = sum(send.shape[1] for send in outs[1::2]) // size
+    quarter = half // 2
     column = 0
-    for keep, send in zip(outs[::2], outs[1::2]):
-        for j in range(keep.shape[1] // pair):
+    for far_first in F_FAR_FIRST:
+        if far_first:
+            (near, near_send, far), outs = outs[:3], outs[3:]
+            places = (
+                (near, 0, 0),
+                (far, 0, quarter),
+                (near_send, 0, half),
+                (far, quarter, half + quarter),
+            )
+        else:
+            (keep, send), outs = outs[:2], outs[2:]
+            places = ((keep, 0, 0), (keep, quarter, quarter), (send, 0, half), (send, quarter, half + quarter))
+        for j in range(places[0][0].shape[1] // pair):
             rhs = jnp.concatenate(
                 [
                     jnp.concatenate([w[slot_of[i + column]], w[slot_of[i + column + 1]]], axis=1)
@@ -139,19 +161,23 @@
                 axis=0,
             )
             part = jnp.dot(x[...], rhs, preferred_element_type=jnp.float32)
-            part = jnp.where(live, part, 0.0).astype(keep.dtype)
-            keep[:, j * pair : (j + 1) * pair] = part[:half]
-            send[:, j * pair : (j + 1) * pair] = part[half:]
+            part = jnp.where(live, part, 0.0).astype(x.dtype)
+            for out, to, at in places:
+                out[to : to + quarter, j * pair : (j + 1) * pair] = part[at : at + quarter]
             column += 2
 
 
-def forward(block, order, limits, slot_of, x, w, width):
-    shape = pltpu.VMEM((x.shape[0] // 2, width // F_PARTS), x.dtype)
+def forward(block, order, limits, slot_of, x, w, widths):
+    half = x.shape[0] // 2
+    shapes = []
+    for width, far_first in zip(widths, F_FAR_FIRST):
+        for rows in (half // 2, half // 2, half) if far_first else (half, half):
+            shapes.append(pltpu.VMEM((rows, width), x.dtype))
     return pl.pallas_call(
-        functools.partial(forward_kernel, block),
-        out_shape=(shape,) * (2 * F_PARTS),
+        functools.partial(forward_kernel, block, sum(widths) // w.shape[1]),
+        out_shape=shapes,
         in_specs=[SMEM, SMEM, SMEM, VMEM, VMEM],
-        out_specs=(VMEM,) * (2 * F_PARTS),
+        out_specs=[VMEM] * len(shapes),
         compiler_params=PARAMS,
         cost_estimate=pl.CostEstimate(flops=1000, bytes_accessed=1000, transcendentals=0),
     )(order, limits, slot_of, resident(x), resident(w))
@@ -188,12 +214,10 @@
         send[:, i * pair : (i + 1) * pair] = part[half:]
 
 
-def backward(part, slot_of, own, other, w, after):
-    block_cols = own.shape[1] // w.shape[1]
-    block_rows = slot_of.shape[0] // block_cols
-    shape = pltpu.VMEM((own.shape[0], block_rows * w.shape[1] // B_PARTS), own.dtype)
+def backward(first, pairs, slot_of, own, other, w, after):
+    shape = pltpu.VMEM((own.shape[0], pairs * 2 * w.shape[1]), own.dtype)
     return pl.pallas_call(
-        functools.partial(backward_kernel, part * (block_rows // B_PARTS)),
+        functools.partial(backward_kernel, 2 * first),
         out_shape=(shape, shape),
         in_specs=[SMEM, VMEM, VMEM, VMEM] + [ANY] * len(after),
         out_specs=(VMEM, VMEM),
@@ -263,6 +287,10 @@
     return lax.ppermute(x, axis, [(i, (i + by) % length) for i in range(length)])
 
 
+def tied(x, *others):
+    return lax.optimization_barrier((x, *others))[0]
+
+
 def added(a, b):
     return (a.astype(jnp.float32) + b.astype(jnp.float32)).astype(a.dtype)
 
@@ -274,7 +302,6 @@
     order = owner_order.reshape(-1)
     limits = tok_count.reshape(2)
     block = token_total // order.shape[0]
-    dy_other = swap(dy_bwd, "row", 1)
     w, x, slot_of = prep(
         owned,
         dy_bwd.shape[1] // size,
@@ -285,35 +312,69 @@
         w_blocks.reshape(slots, size, size),
         x_fwd,
     )
-    parts = forward(block, order, limits, slot_of, x, w, dy_bwd.shape[1])
-    keeps, sends = parts[::2], parts[1::2]
-    *sends, dy_other = lax.optimization_barrier((*sends, dy_other))
-
-    y_received = [swap(send, "row", 1) for send in sends]
+    widths = [size * 2 * share for share in F_PAIRS]
+    parts = forward(block, order, limits, slot_of, x, w, widths)
+    grouped = []
+    for far_first in F_FAR_FIRST:
+        count = 3 if far_first else 2
+        grouped.append(parts[:count])
+        parts = parts[count:]
+    half, quarter = dy_bwd.shape[0], dy_bwd.shape[0] // 2
+    made = {}
+
+    def get(name):
+        if name not in made:
+            made[name] = make(name)
+        return made[name]
+
+    def make(name):
+        kind, at = name[:-1], int(name[-1])
+        after = [get(other)[0] for other in TIES.get(name, ())]
+        if kind == "d":
+            return (swap(dy_bwd, "row", 1),)
+        if kind == "y":
+            return (added(grouped[at][0], swap(tied(grouped[at][1], *after), "row", 1)),)
+        if kind == "u":
+            return (swap(tied(grouped[at][2], *after), "col", 2),)
+        if kind == "v":
+            far = get(f"u{at}")[0]
+            return (added(far[:quarter], swap(tied(far[quarter:], *after), "row", 1)),)
+        if kind == "z":
+            total = get(f"y{at}")[0]
+            if F_FAR_FIRST[at]:
+                far = get(f"v{at}")[0]
+                total = jnp.concatenate([total[:owned], far[:owned], total[owned:], far[owned:]])
+            return (around(tied(total, *after), "section", 1),)
+        if kind == "fx":
+            return (swap(tied(get(f"z{at}")[0][quarter:], *after), "col", 2),)
+        if kind == "fa":
+            if F_FAR_FIRST[at]:
+                return (swap(tied(get(f"z{at}")[0][quarter:], *after), "col", 1),)
+            return (swap(tied(get(f"z{at}")[0][owned:quarter], *after), "col", 1),)
+        if kind == "fb":
+            return (swap(tied(get(f"fx{at}")[0][owned:], *after), "col", 1),)
+        if kind == "k":
+            return backward(sum(B_PAIRS[:at]), B_PAIRS[at], slot_of, dy_bwd, get("d0")[0], w, after)
+        if kind == "c":
+            keep, send = get(f"k{at}")
+            received = swap(tied(send, *after), "col", 1)
+            return added(keep[quarter:], received[quarter:]), added(keep[:quarter], received[:quarter])
+        if kind == "x":
+            onward, kept = get(f"c{at}")
+            received = swap(tied(onward, *after), "col", 2)
+            return added(kept[owned:], received[owned:]), added(kept[:owned], received[:owned])
+        if kind == "b":
+            return (swap(tied(get(f"x{at}")[0], *after), "row", 1),)
+
     y_pieces, dx_pieces = [], []
-    forward_sums, backward_sums = [], []
-    marks = {}
-    for part in range(B_PARTS):
-        after = [marks[name] for name in AFTER[part]]
-        keep, send = backward(part, slot_of, dy_bwd, dy_other, w, after)
-        marks[f"k{part}"] = keep
-        if part < F_PARTS:
-            summed = added(keeps[part], y_received[part])
-            forward_sums.append(summed)
-            marks[f'y{part}'] = summed
-            shifted = around(summed, "section", 1)
-            here, there = shifted[: 2 * owned], swap(shifted[2 * owned :], "col", 2)
-            y_pieces += [here[:owned], swap(here[owned:], "col", 1), there[:owned], swap(there[owned:], "col", 1)]
-        received = swap(send, "col", 1)
-        half = keep.shape[0] // 2
-        onward = added(keep[half:], received[half:])
-        backward_sums.append(onward)
-        marks[f'c{part}'] = onward
-        kept = added(keep[:half], received[:half])
-        received = swap(onward, "col", 2)
-        onward = added(kept[owned:], received[owned:])
-        kept = added(kept[:owned], received[:owned])
-        dx_pieces += [kept, swap(onward, "row", 1)]
+    for at in range(len(F_PAIRS)):
+        here, beside = get(f"z{at}")[0], get(f"fa{at}")[0]
+        if F_FAR_FIRST[at]:
+            y_pieces += [here[:owned], beside[:owned], here[owned:quarter], beside[owned:]]
+        else:
+            y_pieces += [here[:owned], beside, get(f"fx{at}")[0][:owned], get(f"fb{at}")[0]]
+    for at in range(len(B_PAIRS)):
+        dx_pieces += [get(f"x{at}")[1], get(f"b{at}")[0]]
     return place_forward(y_pieces), place_backward(limits, dx_pieces)
 
 

time: 75.2 us -> 71.6 us (0.952)
  starting transfers between devices: 22.1 us -> 19.3 us
  Pallas kernels: 33.8 us -> 33 us
    ppermute x21 -> x18, starting transfers between devices: 18.9 us -> 16.1 us  [swap(): lax.ppermute(x, axis, [(i, i ^ by) for i in range(lax.axis_size(axis))])]
    ppermute x2, waiting for transfers between devices: 5.99 us -> 4.95 us  [around(): lax.ppermute(x, axis, [(i, (i + by) % length) for i in range(length)])]
    ppermute x21 -> x18, waiting for transfers between devices: 10.7 us -> 11.7 us  [swap(): lax.ppermute(x, axis, [(i, i ^ by) for i in range(lax.axis_size(axis))])]
    pallas_call x5 -> x4, Pallas kernels: 24 us -> 23.2 us  [the longest x3 12.4 us: backward(): pl.pallas_call(functools.partial(backward_kernel, 2 * first), out_shape=(...]
  transfers between devices with their start and end apart: 23 -> 20, of which waited for: 7 -> 6; matrix products, arithmetic and copies ran while one was open for 1% -> 1% of each run, Pallas kernels for 44% -> 45%
where the time goes in v4:
time: 71.6 us; the launch traced here: 71.4 us
  Pallas kernels  33 us (46%)
  starting transfers between devices  19.3 us (27%)
  waiting for transfers between devices  16.6 us (23%)
  between operations  1.55 us (2%)
  other arithmetic  0.82 us (1%)
    ppermute x18, starting transfers between devices, swap(): lax.ppermute(x, axis, [(i, i ^ by) for i in range(lax.axis_size(axis))])  16.1 us
    pallas_call x3, Pallas kernels, backward(): pl.pallas_call(functools.partial(backward_kernel, 2 * first), out_shape=(...  12.4 us
    ppermute x18, waiting for transfers between devices, swap(): lax.ppermute(x, axis, [(i, i ^ by) for i in range(lax.axis_size(axis))])  11.7 us
    pallas_call x1, Pallas kernels, forward(): pl.pallas_call(functools.partial(forward_kernel, block, sum(widths) // w....  10.8 us
    pallas_call x1, Pallas kernels, prep(): pl.pallas_call(functools.partial(prep_kernel, owned, block_rows, block_co...  7.15 us
    ppermute x2, waiting for transfers between devices, around(): lax.ppermute(x, axis, [(i, (i + by) % length) for i in range(length)])  4.95 us
    ppermute x2, starting transfers between devices, around(): lax.ppermute(x, axis, [(i, (i + by) % length) for i in range(length)])  3.25 us
    pallas_call x1, Pallas kernels, place_backward(): pl.pallas_call(place_backward_kernel, out_shape=jax.ShapeDtypeStruct((row...  1.58 us
  transfers between devices with their start and end apart: 20, of which 6 were waited for; matrix products, arithmetic and copies ran while one was open for 1% of the time, Pallas kernels for 45%

profile of v4, /device:TPU:0, one launch (start us, length us, event | category | flops | bytes accessed | tf_op | source)
XLA Modules:
  0.0 71.4 jit_solution(9473763234397289528)
XLA Ops:
  0.7 3.0 %collective-permute-start = (bf16[128,3072]{1,0:T(8,128)(2,1)}, bf16[128,3072]{1,0:T(8,128)(2,1)S(1)}, u32[]{:S(2)}, u32[]{:S(2)}) collective-permute-start(bf16[128,3072]{1,0:T(8,128)(2,1)} %own.5), channel_id=1, source_target_pairs={{0,4},{4,0},{1,5},{5,1},{2,6},{6,2},{3,7},{7,3},{8,12},{12,8},{9,1... | collective-permute-start | bytes 2359304 | tf_op jit(solution)/shard_map/ppermute | solution.py:282
  4.3 7.2 %shard_map.95 = (bf16[461,128,128]{2,1,0:T(8,128)(2,1)S(1)}, bf16[256,6144]{1,0:T(8,128)(2,1)S(1)}, s32[1153]{0:T(1024)S(1)}) custom-call(s32[1]{0:T(128)} %bitcast.6.count, s32[1,460]{1,0:T(1,128)} %bitcast.11, s32[1,460]{1,0:T(1,128)} %bitcast.12, s32[1,16]{1,0:T(1,128)} %order_hbm.1, bf16[460,128,128]{2,1,0:T(8,128)(2,1)} %bitcast.10, bf16[256,6144]{1,0:T(8,128)(2,1)} %x_hbm.1), custom_call_target="tpu_custom_call" | custom-call | tf_op jit(solution)/shard_map/pallas_call | solution.py:108
  11.5 10.8 %shard_map.96 = (bf16[128,1024]{1,0:T(8,128)(2,1)S(1)}, bf16[128,1024]{1,0:T(8,128)(2,1)S(1)}, bf16[64,2048]{1,0:T(8,128)(2,1)S(1)}, bf16[64,2048]{1,0:T(8,128)(2,1)S(1)}, bf16[128,2048]{1,0:T(8,128)(2,1)S(1)}) custom-call(s32[16]{0:T(128)S(1)} %bitcast.7, s32[2]{0:T(128)S(1)} %bitcast.8, s32[1153]{0:T(1024)S(1)} %get-tuple-element.23.slot_of, ...), custom_call_target="tpu_custom_call" | custom-call | flops 1000 | bytes 1000 | tf_op jit(solution)/shard_map/pallas_call | solution.py:176
  22.3 0.8 %collective-permute-start.1 = (bf16[128,1024]{1,0:T(8,128)(2,1)S(1)}, bf16[128,1024]{1,0:T(8,128)(2,1)S(1)}, u32[]{:S(2)}, u32[]{:S(2)}) collective-permute-start(bf16[128,1024]{1,0:T(8,128)(2,1)S(1)} %get-tuple-element.28), channel_id=1, source_target_pairs={{0,4},{4,0},{1,5},{5,1},{2,6},{6,2},{3,7},{7,3},{8,12},{12,8},{9,1... | collective-permute-start | bytes 786440 | tf_op jit(solution)/shard_map/ppermute | solution.py:282
  23.2 1.3 %collective-permute-start.3 = (bf16[64,2048]{1,0:T(8,128)(2,1)S(1)}, bf16[64,2048]{1,0:T(8,128)(2,1)S(1)}, u32[]{:S(2)}, u32[]{:S(2)}) collective-permute-start(bf16[64,2048]{1,0:T(8,128)(2,1)S(1)} %get-tuple-element.31), channel_id=1, source_target_pairs={{0,4},{4,0},{1,5},{5,1},{2,6},{6,2},{3,7},{7,3},{8,12},{12,8},{9,1... | collective-permute-start | bytes 786440 | tf_op jit(solution)/shard_map/ppermute | solution.py:282
  24.4 1.5 %collective-permute-start.4 = (bf16[128,2048]{1,0:T(8,128)(2,1)S(1)}, bf16[128,2048]{1,0:T(8,128)(2,1)S(1)}, u32[]{:S(2)}, u32[]{:S(2)}) collective-permute-start(bf16[128,2048]{1,0:T(8,128)(2,1)S(1)} %get-tuple-element.33), channel_id=1, source_target_pairs={{0,2},{1,3},{2,0},{3,1},{4,6},{5,7},{6,4},{7,5},{8,10},{9,11},{10,... | collective-permute-start | bytes 1572872 | tf_op jit(solution)/shard_map/ppermute | solution.py:282
  25.9 3.7 %shard_map.97 = (bf16[128,1792]{1,0:T(8,128)(2,1)S(1)}, bf16[128,1792]{1,0:T(8,128)(2,1)S(1)}) custom-call(s32[1153]{0:T(1024)S(1)} %get-tuple-element.23.slot_of, bf16[128,3072]{1,0:T(8,128)(2,1)S(1)} %copy-done, bf16[128,3072]{1,0:T(8,128)(2,1)S(1)} %collective-permute-done.other, bf16[461,128,128]{2,1,0:T(8,128)(2,1)S(1)} %get-tuple-element.25.w), custom_call_target="tpu_custom_call" | custom-call | flops 1000 | bytes 1000 | tf_op jit(solution)/shard_map/pallas_call | solution.py:219
  29.7 4.7 %shard_map.98 = (bf16[128,2304]{1,0:T(8,128)(2,1)S(1)}, bf16[128,2304]{1,0:T(8,128)(2,1)S(1)}) custom-call(s32[1153]{0:T(1024)S(1)} %get-tuple-element.23.slot_of, bf16[128,3072]{1,0:T(8,128)(2,1)S(1)} %copy-done, bf16[128,3072]{1,0:T(8,128)(2,1)S(1)} %collective-permute-done.other, bf16[461,128,128]{2,1,0:T(8,128)(2,1)S(1)} %get-tuple-element.25.w), custom_call_target="tpu_custom_call" | custom-call | flops 1000 | bytes 1000 | tf_op jit(solution)/shard_map/pallas_call | solution.py:219
  35.0 1.6 %collective-permute-start.2 = (bf16[128,1024]{1,0:T(8,128)(2,1)S(1)}, bf16[128,1024]{1,0:T(8,128)(2,1)S(1)}, u32[]{:S(2)}, u32[]{:S(2)}) collective-permute-start(bf16[128,1024]{1,0:T(8,128)(2,1)S(1)} %add_convert_fusion.6), channel_id=1, source_target_pairs={{0,8},{8,16},{16,24},{24,0},{1,9},{9,17},{17,25},{25,1},{2,10},{10... | collective-permute-start | bytes 786440 | tf_op jit(solution)/shard_map/ppermute | solution.py:287
  37.6 4.1 %shard_map.100 = (bf16[128,2048]{1,0:T(8,128)(2,1)S(1)}, bf16[128,2048]{1,0:T(8,128)(2,1)S(1)}) custom-call(s32[1153]{0:T(1024)S(1)} %get-tuple-element.23.slot_of, bf16[128,3072]{1,0:T(8,128)(2,1)S(1)} %copy-done, bf16[128,3072]{1,0:T(8,128)(2,1)S(1)} %collective-permute-done.other, bf16[461,128,128]{2,1,0:T(8,128)(2,1)S(1)} %get-tuple-element.25.w, ...), custom_call_target="tpu_custom_call" | custom-call | flops 1000 | bytes 1000 | tf_op jit(solution)/shard_map/pallas_call | solution.py:219
  42.5 2.7 %collective-permute-done.2 = bf16[128,1024]{1,0:T(8,128)(2,1)S(1)} collective-permute-done((bf16[128,1024]{1,0:T(8,128)(2,1)S(1)}, bf16[128,1024]{1,0:T(8,128)(2,1)S(1)}, u32[]{:S(2)}, u32[]{:S(2)}) %collective-permute-start.2) | collective-permute-done | bytes 262176 | tf_op jit(solution)/shard_map/ppermute | solution.py:287
  45.9 1.6 %collective-permute-start.12 = (bf16[64,2304]{1,0:T(8,128)(2,1)S(1)}, bf16[64,2304]{1,0:T(8,128)(2,1)S(1)}, u32[]{:S(2)}, u32[]{:S(2)}) collective-permute-start(bf16[64,2304]{1,0:T(8,128)(2,1)S(1)} %get-tuple-element.45), channel_id=1, source_target_pairs={{0,2},{1,3},{2,0},{3,1},{4,6},{5,7},{6,4},{7,5},{8,10},{9,11},{10,... | collective-permute-start | bytes 884744 | tf_op jit(solution)/shard_map/ppermute | solution.py:282
  47.5 3.0 %collective-permute-done.5 = bf16[64,2048]{1,0:T(8,128)(2,1)S(1)} collective-permute-done((bf16[64,2048]{1,0:T(8,128)(2,1)S(1)}, bf16[64,2048]{1,0:T(8,128)(2,1)S(1)}, u32[]{:S(2)}, u32[]{:S(2)}) %collective-permute-start.5) | collective-permute-done | bytes 262176 | tf_op jit(solution)/shard_map/ppermute | solution.py:282
  50.7 1.6 %collective-permute-start.6 = (bf16[128,2048]{1,0:T(8,128)(2,1)S(1)}, bf16[128,2048]{1,0:T(8,128)(2,1)S(1)}, u32[]{:S(2)}, u32[]{:S(2)}) collective-permute-start(bf16[128,2048]{1,0:T(8,128)(2,1)S(1)} %pad_maximum_fusion), channel_id=1, source_target_pairs={{0,8},{8,16},{16,24},{24,0},{1,9},{9,17},{17,25},{25,1},{2,10},{10... | collective-permute-start | bytes 1572872 | tf_op jit(solution)/shard_map/ppermute | solution.py:287
  52.4 1.4 %collective-permute-start.18 = (bf16[64,2048]{1,0:T(8,128)(2,1)S(1)}, bf16[64,2048]{1,0:T(8,128)(2,1)S(1)}, u32[]{:S(2)}, u32[]{:S(2)}) collective-permute-start(bf16[64,2048]{1,0:T(8,128)(2,1)S(1)} %get-tuple-element.47), channel_id=1, source_target_pairs={{0,2},{1,3},{2,0},{3,1},{4,6},{5,7},{6,4},{7,5},{8,10},{9,11},{10,... | collective-permute-start | bytes 786440 | tf_op jit(solution)/shard_map/ppermute | solution.py:282
  53.9 3.9 %collective-permute-done.12 = bf16[64,2304]{1,0:T(8,128)(2,1)S(1)} collective-permute-done((bf16[64,2304]{1,0:T(8,128)(2,1)S(1)}, bf16[64,2304]{1,0:T(8,128)(2,1)S(1)}, u32[]{:S(2)}, u32[]{:S(2)}) %collective-permute-start.12) | collective-permute-done | bytes 294944 | tf_op jit(solution)/shard_map/ppermute | solution.py:282
  57.9 1.0 %collective-permute-start.13 = (bf16[32,1792]{1,0:T(8,128)(2,1)S(1)}, bf16[32,1792]{1,0:T(8,128)(2,1)S(1)}, u32[]{:S(2)}, u32[]{:S(2)}) collective-permute-start(bf16[32,1792]{1,0:T(8,128)(2,1)S(1)} %get-tuple-element.40), channel_id=1, source_target_pairs={{0,4},{4,0},{1,5},{5,1},{2,6},{6,2},{3,7},{7,3},{8,12},{12,8},{9,1... | collective-permute-start | bytes 344072 | tf_op jit(solution)/shard_map/ppermute | solution.py:282
  58.9 1.1 %collective-permute-start.16 = (bf16[32,2304]{1,0:T(8,128)(2,1)S(1)}, bf16[32,2304]{1,0:T(8,128)(2,1)S(1)}, u32[]{:S(2)}, u32[]{:S(2)}) collective-permute-start(bf16[32,2304]{1,0:T(8,128)(2,1)S(1)} %get-tuple-element.51), channel_id=1, source_target_pairs={{0,4},{4,0},{1,5},{5,1},{2,6},{6,2},{3,7},{7,3},{8,12},{12,8},{9,1... | collective-permute-start | bytes 442376 | tf_op jit(solution)/shard_map/ppermute | solution.py:282
  60.0 2.7 %collective-permute-done.13.refs_1_ = bf16[32,1792]{1,0:T(8,128)(2,1)S(1)} collective-permute-done((bf16[32,1792]{1,0:T(8,128)(2,1)S(1)}, bf16[32,1792]{1,0:T(8,128)(2,1)S(1)}, u32[]{:S(2)}, u32[]{:S(2)}) %collective-permute-start.13) | collective-permute-done | bytes 114720 | tf_op jit(solution)/shard_map/ppermute | solution.py:282
  62.8 1.0 %collective-permute-start.19 = (bf16[32,2048]{1,0:T(8,128)(2,1)S(1)}, bf16[32,2048]{1,0:T(8,128)(2,1)S(1)}, u32[]{:S(2)}, u32[]{:S(2)}) collective-permute-start(bf16[32,2048]{1,0:T(8,128)(2,1)S(1)} %get-tuple-element.52), channel_id=1, source_target_pairs={{0,4},{4,0},{1,5},{5,1},{2,6},{6,2},{3,7},{7,3},{8,12},{12,8},{9,1... | collective-permute-start | bytes 393224 | tf_op jit(solution)/shard_map/ppermute | solution.py:282
  63.8 2.3 %collective-permute-done.6 = bf16[128,2048]{1,0:T(8,128)(2,1)S(1)} collective-permute-done((bf16[128,2048]{1,0:T(8,128)(2,1)S(1)}, bf16[128,2048]{1,0:T(8,128)(2,1)S(1)}, u32[]{:S(2)}, u32[]{:S(2)}) %collective-permute-start.6) | collective-permute-done | bytes 524320 | tf_op jit(solution)/shard_map/ppermute | solution.py:287
  66.7 2.0 %collective-permute-done.19.refs_5_ = bf16[32,2048]{1,0:T(8,128)(2,1)S(1)} collective-permute-done((bf16[32,2048]{1,0:T(8,128)(2,1)S(1)}, bf16[32,2048]{1,0:T(8,128)(2,1)S(1)}, u32[]{:S(2)}, u32[]{:S(2)}) %collective-permute-start.19) | collective-permute-done | bytes 131104 | tf_op jit(solution)/shard_map/ppermute | solution.py:282
  68.8 1.6 %shard_map.101 = bf16[32,12288]{1,0:T(8,128)(2,1)} custom-call(s32[2]{0:T(128)S(1)} %bitcast.9, bf16[32,1792]{1,0:T(8,128)(2,1)S(1)} %get-tuple-element.56.refs_0_, bf16[32,1792]{1,0:T(8,128)(2,1)S(1)} %collective-permute-done.13.refs_1_, bf16[32,2304]{1,0:T(8,128)(2,1)S(1)} %get-tuple-element.50.refs_2_, ...), custom_call_target="tpu_custom_call" | custom-call | tf_op jit(solution)/shard_map/pallas_call | solution.py:272
  70.4 1.0 %shard_map.99 = bf16[32,12288]{1,0:T(8,128)(2,1)} custom-call(bf16[32,1024]{1,0:T(8,128)(2,1)S(1)} %get-tuple-element.65.refs_0_, bf16[32,1024]{1,0:T(8,128)(2,1)S(1)} %collective-permute-done.7.refs_1_, bf16[32,1024]{1,0:T(8,128)(2,1)S(1)} %get-tuple-element.67.refs_2_, bf16[32,1024]{1,0:T(8,128)(2,1)S(1)} %collective-permute-done.14.refs_3_, ...), custom_call_target="tpu_custom_call" | custom-call | tf_op jit(solution)/shard_map/pallas_call | solution.py:246
  (48 shorter events, 4.3 us)
Async XLA Ops:
  0.6 10.9 %copy-start.1 = (s32[1,16]{1,0:T(1,128)S(1)}, s32[1,16]{1,0:T(1,128)}, u32[]{:S(2)}) copy-start(s32[1,16]{1,0:T(1,128)} %order_hbm.1) | copy-start | bytes 196
  0.6 10.9 %copy-start.2 = (s32[1,2]{1,0:T(1,128)S(1)}, s32[1,2]{1,0:T(1,128)}, u32[]{:S(2)}) copy-start(s32[1,2]{1,0:T(1,128)} %param.14) | copy-start | bytes 28
  0.7 21.7 %collective-permute-start = (bf16[128,3072]{1,0:T(8,128)(2,1)}, bf16[128,3072]{1,0:T(8,128)(2,1)S(1)}, u32[]{:S(2)}, u32[]{:S(2)}) collective-permute-start(bf16[128,3072]{1,0:T(8,128)(2,1)} %own.5), channel_id=1, source_target_pairs={{0,4},{4,0},{1,5},{5,1},{2,6},{6,2},{3,7},{7,3},{8,12},{12,8},{9,1... | collective-permute-start | bytes 2359304 | tf_op jit(solution)/shard_map/ppermute | solution.py:282
  4.3 21.6 %copy-start = (bf16[128,3072]{1,0:T(8,128)(2,1)S(1)}, bf16[128,3072]{1,0:T(8,128)(2,1)}, u32[]{:S(2)}) copy-start(bf16[128,3072]{1,0:T(8,128)(2,1)} %own.5) | copy-start | bytes 2359300
  22.3 12.6 %collective-permute-start.1 = (bf16[128,1024]{1,0:T(8,128)(2,1)S(1)}, bf16[128,1024]{1,0:T(8,128)(2,1)S(1)}, u32[]{:S(2)}, u32[]{:S(2)}) collective-permute-start(bf16[128,1024]{1,0:T(8,128)(2,1)S(1)} %get-tuple-element.28), channel_id=1, source_target_pairs={{0,4},{4,0},{1,5},{5,1},{2,6},{6,2},{3,7},{7,3},{8,12},{12,8},{9,1... | collective-permute-start | bytes 786440 | tf_op jit(solution)/shard_map/ppermute | solution.py:282
  23.2 13.4 %collective-permute-start.3 = (bf16[64,2048]{1,0:T(8,128)(2,1)S(1)}, bf16[64,2048]{1,0:T(8,128)(2,1)S(1)}, u32[]{:S(2)}, u32[]{:S(2)}) collective-permute-start(bf16[64,2048]{1,0:T(8,128)(2,1)S(1)} %get-tuple-element.31), channel_id=1, source_target_pairs={{0,4},{4,0},{1,5},{5,1},{2,6},{6,2},{3,7},{7,3},{8,12},{12,8},{9,1... | collective-permute-start | bytes 786440 | tf_op jit(solution)/shard_map/ppermute | solution.py:282
  24.4 17.3 %collective-permute-start.4 = (bf16[128,2048]{1,0:T(8,128)(2,1)S(1)}, bf16[128,2048]{1,0:T(8,128)(2,1)S(1)}, u32[]{:S(2)}, u32[]{:S(2)}) collective-permute-start(bf16[128,2048]{1,0:T(8,128)(2,1)S(1)} %get-tuple-element.33), channel_id=1, source_target_pairs={{0,2},{1,3},{2,0},{3,1},{4,6},{5,7},{6,4},{7,5},{8,10},{9,11},{10,... | collective-permute-start | bytes 1572872 | tf_op jit(solution)/shard_map/ppermute | solution.py:282
  29.6 7.1 %collective-permute-start.9 = (bf16[128,1792]{1,0:T(8,128)(2,1)S(1)}, bf16[128,1792]{1,0:T(8,128)(2,1)S(1)}, u32[]{:S(2)}, u32[]{:S(2)}) collective-permute-start(bf16[128,1792]{1,0:T(8,128)(2,1)S(1)} %get-tuple-element.37), channel_id=1, source_target_pairs={{0,1},{1,0},{2,3},{3,2},{4,5},{5,4},{6,7},{7,6},{8,9},{9,8},{10,11... | collective-permute-start | bytes 1376264 | tf_op jit(solution)/shard_map/ppermute | solution.py:282
  34.4 11.4 %collective-permute-start.11 = (bf16[128,2304]{1,0:T(8,128)(2,1)S(1)}, bf16[128,2304]{1,0:T(8,128)(2,1)S(1)}, u32[]{:S(2)}, u32[]{:S(2)}) collective-permute-start(bf16[128,2304]{1,0:T(8,128)(2,1)S(1)} %get-tuple-element.39), channel_id=1, source_target_pairs={{0,1},{1,0},{2,3},{3,2},{4,5},{5,4},{6,7},{7,6},{8,9},{9,8},{10,11... | collective-permute-start | bytes 1769480 | tf_op jit(solution)/shard_map/ppermute | solution.py:282
  35.0 10.2 %collective-permute-start.2 = (bf16[128,1024]{1,0:T(8,128)(2,1)S(1)}, bf16[128,1024]{1,0:T(8,128)(2,1)S(1)}, u32[]{:S(2)}, u32[]{:S(2)}) collective-permute-start(bf16[128,1024]{1,0:T(8,128)(2,1)S(1)} %add_convert_fusion.6), channel_id=1, source_target_pairs={{0,8},{8,16},{16,24},{24,0},{1,9},{9,17},{17,25},{25,1},{2,10},{10... | collective-permute-start | bytes 786440 | tf_op jit(solution)/shard_map/ppermute | solution.py:287
  36.9 10.6 %collective-permute-start.10 = (bf16[64,1792]{1,0:T(8,128)(2,1)S(1)}, bf16[64,1792]{1,0:T(8,128)(2,1)S(1)}, u32[]{:S(2)}, u32[]{:S(2)}) collective-permute-start(bf16[64,1792]{1,0:T(8,128)(2,1)S(1)} %get-tuple-element.49.refs_0_), channel_id=1, source_target_pairs={{0,2},{1,3},{2,0},{3,1},{4,6},{5,7},{6,4},{7,5},{8,10},{9,11},{10,... | collective-permute-start | bytes 688136 | tf_op jit(solution)/shard_map/ppermute | solution.py:282
  41.6 10.7 %collective-permute-start.17 = (bf16[128,2048]{1,0:T(8,128)(2,1)S(1)}, bf16[128,2048]{1,0:T(8,128)(2,1)S(1)}, u32[]{:S(2)}, u32[]{:S(2)}) collective-permute-start(bf16[128,2048]{1,0:T(8,128)(2,1)S(1)} %get-tuple-element.43), channel_id=1, source_target_pairs={{0,1},{1,0},{2,3},{3,2},{4,5},{5,4},{6,7},{7,6},{8,9},{9,8},{10,11... | collective-permute-start | bytes 1572872 | tf_op jit(solution)/shard_map/ppermute | solution.py:282
  41.8 8.8 %collective-permute-start.5 = (bf16[64,2048]{1,0:T(8,128)(2,1)S(1)}, bf16[64,2048]{1,0:T(8,128)(2,1)S(1)}, u32[]{:S(2)}, u32[]{:S(2)}) collective-permute-start(bf16[64,2048]{1,0:T(8,128)(2,1)S(1)} %slice.164), channel_id=1, source_target_pairs={{0,4},{4,0},{1,5},{5,1},{2,6},{6,2},{3,7},{7,3},{8,12},{12,8},{9,1... | collective-permute-start | bytes 786440 | tf_op jit(solution)/shard_map/ppermute | solution.py:282
  45.2 13.7 %collective-permute-start.8 = (bf16[64,1024]{1,0:T(8,128)(2,1)S(1)}, bf16[64,1024]{1,0:T(8,128)(2,1)S(1)}, u32[]{:S(2)}, u32[]{:S(2)}) collective-permute-start(bf16[64,1024]{1,0:T(8,128)(2,1)S(1)} %slice.168), channel_id=1, source_target_pairs={{0,2},{1,3},{2,0},{3,1},{4,6},{5,7},{6,4},{7,5},{8,10},{9,11},{10,... | collective-permute-start | bytes 393224 | tf_op jit(solution)/shard_map/ppermute | solution.py:282
  45.9 11.9 %collective-permute-start.12 = (bf16[64,2304]{1,0:T(8,128)(2,1)S(1)}, bf16[64,2304]{1,0:T(8,128)(2,1)S(1)}, u32[]{:S(2)}, u32[]{:S(2)}) collective-permute-start(bf16[64,2304]{1,0:T(8,128)(2,1)S(1)} %get-tuple-element.45), channel_id=1, source_target_pairs={{0,2},{1,3},{2,0},{3,1},{4,6},{5,7},{6,4},{7,5},{8,10},{9,11},{10,... | collective-permute-start | bytes 884744 | tf_op jit(solution)/shard_map/ppermute | solution.py:282
  50.7 15.4 %collective-permute-start.6 = (bf16[128,2048]{1,0:T(8,128)(2,1)S(1)}, bf16[128,2048]{1,0:T(8,128)(2,1)S(1)}, u32[]{:S(2)}, u32[]{:S(2)}) collective-permute-start(bf16[128,2048]{1,0:T(8,128)(2,1)S(1)} %pad_maximum_fusion), channel_id=1, source_target_pairs={{0,8},{8,16},{16,24},{24,0},{1,9},{9,17},{17,25},{25,1},{2,10},{10... | collective-permute-start | bytes 1572872 | tf_op jit(solution)/shard_map/ppermute | solution.py:287
  52.4 10.3 %collective-permute-start.18 = (bf16[64,2048]{1,0:T(8,128)(2,1)S(1)}, bf16[64,2048]{1,0:T(8,128)(2,1)S(1)}, u32[]{:S(2)}, u32[]{:S(2)}) collective-permute-start(bf16[64,2048]{1,0:T(8,128)(2,1)S(1)} %get-tuple-element.47), channel_id=1, source_target_pairs={{0,2},{1,3},{2,0},{3,1},{4,6},{5,7},{6,4},{7,5},{8,10},{9,11},{10,... | collective-permute-start | bytes 786440 | tf_op jit(solution)/shard_map/ppermute | solution.py:282
  57.9 4.9 %collective-permute-start.13 = (bf16[32,1792]{1,0:T(8,128)(2,1)S(1)}, bf16[32,1792]{1,0:T(8,128)(2,1)S(1)}, u32[]{:S(2)}, u32[]{:S(2)}) collective-permute-start(bf16[32,1792]{1,0:T(8,128)(2,1)S(1)} %get-tuple-element.40), channel_id=1, source_target_pairs={{0,4},{4,0},{1,5},{5,1},{2,6},{6,2},{3,7},{7,3},{8,12},{12,8},{9,1... | collective-permute-start | bytes 344072 | tf_op jit(solution)/shard_map/ppermute | solution.py:282
  58.9 7.8 %collective-permute-start.16 = (bf16[32,2304]{1,0:T(8,128)(2,1)S(1)}, bf16[32,2304]{1,0:T(8,128)(2,1)S(1)}, u32[]{:S(2)}, u32[]{:S(2)}) collective-permute-start(bf16[32,2304]{1,0:T(8,128)(2,1)S(1)} %get-tuple-element.51), channel_id=1, source_target_pairs={{0,4},{4,0},{1,5},{5,1},{2,6},{6,2},{3,7},{7,3},{8,12},{12,8},{9,1... | collective-permute-start | bytes 442376 | tf_op jit(solution)/shard_map/ppermute | solution.py:282
  62.7 7.7 %collective-permute-start.14 = (bf16[32,1024]{1,0:T(8,128)(2,1)S(1)}, bf16[32,1024]{1,0:T(8,128)(2,1)S(1)}, u32[]{:S(2)}, u32[]{:S(2)}) collective-permute-start(bf16[32,1024]{1,0:T(8,128)(2,1)S(1)} %get-tuple-element.41), channel_id=1, source_target_pairs={{0,1},{1,0},{2,3},{3,2},{4,5},{5,4},{6,7},{7,6},{8,9},{9,8},{10,11... | collective-permute-start | bytes 196616 | tf_op jit(solution)/shard_map/ppermute | solution.py:282
  62.8 6.0 %collective-permute-start.19 = (bf16[32,2048]{1,0:T(8,128)(2,1)S(1)}, bf16[32,2048]{1,0:T(8,128)(2,1)S(1)}, u32[]{:S(2)}, u32[]{:S(2)}) collective-permute-start(bf16[32,2048]{1,0:T(8,128)(2,1)S(1)} %get-tuple-element.52), channel_id=1, source_target_pairs={{0,4},{4,0},{1,5},{5,1},{2,6},{6,2},{3,7},{7,3},{8,12},{12,8},{9,1... | collective-permute-start | bytes 393224 | tf_op jit(solution)/shard_map/ppermute | solution.py:282
  66.1 4.3 %collective-permute-start.7 = (bf16[32,1024]{1,0:T(8,128)(2,1)S(1)}, bf16[32,1024]{1,0:T(8,128)(2,1)S(1)}, u32[]{:S(2)}, u32[]{:S(2)}) collective-permute-start(bf16[32,1024]{1,0:T(8,128)(2,1)S(1)} %get-tuple-element.35), channel_id=1, source_target_pairs={{0,1},{1,0},{2,3},{3,2},{4,5},{5,4},{6,7},{7,6},{8,9},{9,8},{10,11... | collective-permute-start | bytes 196616 | tf_op jit(solution)/shard_map/ppermute | solution.py:282
  66.1 4.2 %collective-permute-start.15 = (bf16[64,2048]{1,0:T(8,128)(2,1)S(1)}, bf16[64,2048]{1,0:T(8,128)(2,1)S(1)}, u32[]{:S(2)}, u32[]{:S(2)}) collective-permute-start(bf16[64,2048]{1,0:T(8,128)(2,1)S(1)} %slice.180), channel_id=1, source_target_pairs={{0,1},{1,0},{2,3},{3,2},{4,5},{5,4},{6,7},{7,6},{8,9},{9,8},{10,11... | collective-permute-start | bytes 786440 | tf_op jit(solution)/shard_map/ppermute | solution.py:282

commit v5 on v4

--- a/solution.py
+++ b/solution.py
@@ -8,18 +8,20 @@
 from jax.sharding import PartitionSpec as P
 
 
-F_PAIRS = (4, 8)
-B_PAIRS = (7, 9, 8)
-F_FAR_FIRST = (False, True)
+F_PAIRS = (6, 6)
+B_PAIRS = (8, 9, 7)
+JOINT = 1
+F_FAR_FIRST = (0, 1)
+TRACE_FIRST = ()
+B_JOINED = 1
+C_SPLIT = 1
 TIES = {
-    "b0": ("z0", "x1",),
-    "fa0": ("z1",),
-    "fb0": ("x0", "b0",),
+    "b0": ("x1", "z1",),
     "k2": ("c0",),
     "u1": ("d0",),
+    "x1": ("y0",),
     "y0": ("d0",),
-    "y1": ("d0",),
-    "z1": ("z0",),
+    "y1": ("c0",),
 }
 
 VMEM = pl.BlockSpec(memory_space=pltpu.VMEM)
@@ -227,53 +229,40 @@
     )(slot_of, own, other, resident(w), *after)
 
 
-def place_forward_kernel(*refs):
-    pieces, out = refs[:-1], refs[-1]
-    c = lax.axis_index("col")
-    width = out.shape[1] // 4
+def place_kernel(counts, limits, *refs):
+    y_out, dx_out = refs[-2:]
+    lists = []
+    for count in counts:
+        lists.append(refs[:count])
+        refs = refs[count:]
+    r, c = lax.axis_index("row"), lax.axis_index("col")
+    rows = y_out.shape[0]
     first_section = lax.axis_index("section") == 0
-    for dc in range(4):
+    for dr, pieces in enumerate(lists[:2]):
+        at = (r ^ dr) * (dx_out.shape[1] // 2)
+        for piece in pieces:
+            token = (r * 4 + c) * rows + lax.broadcasted_iota(jnp.int32, piece.shape, 0)
+            value = jnp.where(token < limits[1], piece[...].astype(jnp.float32), 0.0)
+            dx_out[:, pl.ds(pl.multiple_of(at, 128), piece.shape[1])] = value.astype(dx_out.dtype)
+            at += piece.shape[1]
+    width = y_out.shape[1] // 4
+    for dc, pieces in zip((0, 2, 1, 3), lists[2:4] + [lists[4], lists[4]]):
         at = (c ^ dc) * width
-        for piece in pieces[dc::4]:
-            value = jnp.where(first_section, 0.0, piece[...].astype(jnp.float32)).astype(out.dtype)
-            out[:, pl.ds(pl.multiple_of(at, 128), piece.shape[1])] = value
-            at += piece.shape[1]
-
-
-def place_forward(pieces):
-    rows = pieces[0].shape[0]
-    width = sum(piece.shape[1] for piece in pieces)
+        for piece in pieces:
+            value = piece[...] if dc % 2 == 0 else piece[:, dc // 2 * width : (dc // 2 + 1) * width]
+            value = jnp.where(first_section, 0.0, value.astype(jnp.float32)).astype(y_out.dtype)
+            y_out[:, pl.ds(pl.multiple_of(at, 128), value.shape[1])] = value
+            at += value.shape[1]
+
+
+def place(limits, width, lists):
+    pieces = [piece for each in lists for piece in each]
+    shape = jax.ShapeDtypeStruct((pieces[0].shape[0], width), pieces[0].dtype)
     return pl.pallas_call(
-        place_forward_kernel,
-        out_shape=jax.ShapeDtypeStruct((rows, width), pieces[0].dtype),
-        in_specs=[VMEM] * len(pieces),
-        out_specs=VMEM,
-        compiler_params=PARAMS,
-    )(*pieces)
-
-
-def place_backward_kernel(limits, *refs):
-    pieces, out = refs[:-1], refs[-1]
-    r, c = lax.axis_index("row"), lax.axis_index("col")
-    rows = out.shape[0]
-    width = out.shape[1] // 2
-    for dr in range(2):
-        at = (r ^ dr) * width
-        for piece in pieces[dr::2]:
-            token = (r * 4 + c) * rows + lax.broadcasted_iota(jnp.int32, piece.shape, 0)
-            value = jnp.where(token < limits[1], piece[...].astype(jnp.float32), 0.0).astype(out.dtype)
-            out[:, pl.ds(pl.multiple_of(at, 128), piece.shape[1])] = value
-            at += piece.shape[1]
-
-
-def place_backward(limits, pieces):
-    rows = pieces[0].shape[0]
-    width = sum(piece.shape[1] for piece in pieces)
-    return pl.pallas_call(
-        place_backward_kernel,
-        out_shape=jax.ShapeDtypeStruct((rows, width), pieces[0].dtype),
+        functools.partial(place_kernel, [len(each) for each in lists]),
+        out_shape=[shape] * 2,
         in_specs=[SMEM] + [VMEM] * len(pieces),
-        out_specs=VMEM,
+        out_specs=[VMEM] * 2,
         compiler_params=PARAMS,
     )(limits, *pieces)
 
@@ -341,41 +330,58 @@
             return (added(far[:quarter], swap(tied(far[quarter:], *after), "row", 1)),)
         if kind == "z":
             total = get(f"y{at}")[0]
-            if F_FAR_FIRST[at]:
+            if F_FAR_FIRST[at] == JOINT:
                 far = get(f"v{at}")[0]
                 total = jnp.concatenate([total[:owned], far[:owned], total[owned:], far[owned:]])
             return (around(tied(total, *after), "section", 1),)
+        if kind == "w":
+            return (around(tied(get(f"v{at}")[0], *after), "section", 1),)
         if kind == "fx":
             return (swap(tied(get(f"z{at}")[0][quarter:], *after), "col", 2),)
-        if kind == "fa":
-            if F_FAR_FIRST[at]:
-                return (swap(tied(get(f"z{at}")[0][quarter:], *after), "col", 1),)
-            return (swap(tied(get(f"z{at}")[0][owned:quarter], *after), "col", 1),)
-        if kind == "fb":
-            return (swap(tied(get(f"fx{at}")[0][owned:], *after), "col", 1),)
+        if kind == "fc":
+            near, beyond = [], []
+            for part, far_first in enumerate(F_FAR_FIRST):
+                here = get(f"z{part}")[0]
+                if far_first == JOINT:
+                    near.append(here[quarter : quarter + owned])
+                    beyond.append(here[quarter + owned :])
+                else:
+                    near.append(here[owned:quarter])
+                    beyond.append(get(f"w{part}" if far_first else f"fx{part}")[0][owned:])
+            return (swap(tied(jnp.concatenate(near + beyond, axis=1), *after), "col", 1),)
         if kind == "k":
             return backward(sum(B_PAIRS[:at]), B_PAIRS[at], slot_of, dy_bwd, get("d0")[0], w, after)
         if kind == "c":
             keep, send = get(f"k{at}")
-            received = swap(tied(send, *after), "col", 1)
+            send = tied(send, *after)
+            step = send.shape[0] // C_SPLIT
+            received = jnp.concatenate(
+                [swap(send[i * step : (i + 1) * step], "col", 1) for i in range(C_SPLIT)]
+            )
             return added(keep[quarter:], received[quarter:]), added(keep[:quarter], received[:quarter])
         if kind == "x":
             onward, kept = get(f"c{at}")
             received = swap(tied(onward, *after), "col", 2)
             return added(kept[owned:], received[owned:]), added(kept[:owned], received[:owned])
         if kind == "b":
-            return (swap(tied(get(f"x{at}")[0], *after), "row", 1),)
-
-    y_pieces, dx_pieces = [], []
-    for at in range(len(F_PAIRS)):
-        here, beside = get(f"z{at}")[0], get(f"fa{at}")[0]
-        if F_FAR_FIRST[at]:
-            y_pieces += [here[:owned], beside[:owned], here[owned:quarter], beside[owned:]]
+            onward = [get(f"x{part}")[0] for part in (range(B_JOINED) if at < B_JOINED else (at,))]
+            return (swap(tied(jnp.concatenate(onward, axis=1), *after), "row", 1),)
+
+    for name in TRACE_FIRST:
+        get(name)
+    own, beyond = [], []
+    for part, far_first in enumerate(F_FAR_FIRST):
+        here = get(f"z{part}")[0]
+        own.append(here[:owned])
+        if far_first == JOINT:
+            beyond.append(here[owned:quarter])
         else:
-            y_pieces += [here[:owned], beside, get(f"fx{at}")[0][:owned], get(f"fb{at}")[0]]
-    for at in range(len(B_PAIRS)):
-        dx_pieces += [get(f"x{at}")[1], get(f"b{at}")[0]]
-    return place_forward(y_pieces), place_backward(limits, dx_pieces)
+            beyond.append(get(f"w{part}" if far_first else f"fx{part}")[0][:owned])
+    parts = range(len(B_PAIRS))
+    kept = [get(f"x{part}")[1] for part in parts]
+    received = [get(f"b{part}")[0] for part in parts if part == 0 or part >= B_JOINED]
+    y_next, dx_section = place(limits, 4 * dy_bwd.shape[1], [kept, received, own, beyond, [get("fc0")[0]]])
+    return y_next, dx_section
 
 
 def passed_along(shard, axis, by):

time: 71.6 us -> 68.2 us (0.953)
  waiting for transfers between devices: 16.6 us -> 13.6 us
  Pallas kernels: 33 us -> 32.2 us
    ppermute x2, waiting for transfers between devices: 4.95 us -> 1.93 us  [around(): lax.ppermute(x, axis, [(i, (i + by) % length) for i in range(length)])]
    pallas_call x2 -> x1, Pallas kernels: 2.6 us -> 1.9 us  [place(): pl.pallas_call(functools.partial(place_kernel, [len(each) for each in lis...]
    ppermute x18 -> x16, starting transfers between devices: 16.1 us -> 16.5 us  [swap(): lax.ppermute(x, axis, [(i, i ^ by) for i in range(lax.axis_size(axis))])]
    ppermute x18 -> x16, waiting for transfers between devices: 11.7 us -> 11.7 us  [swap(): lax.ppermute(x, axis, [(i, i ^ by) for i in range(lax.axis_size(axis))])]
  transfers between devices with their start and end apart: 20 -> 18, of which waited for: 6 -> 8; matrix products, arithmetic and copies ran while one was open for 1% -> 1% of each run, Pallas kernels for 45% -> 45%
where the time goes in v5:
time: 68.2 us; the launch traced here: 68.1 us
  Pallas kernels  32.2 us (47%)
  starting transfers between devices  19.7 us (29%)
  waiting for transfers between devices  13.6 us (20%)
  between operations  1.53 us (2%)
  other arithmetic  0.83 us (1%)
    ppermute x16, starting transfers between devices, swap(): lax.ppermute(x, axis, [(i, i ^ by) for i in range(lax.axis_size(axis))])  16.5 us
    pallas_call x3, Pallas kernels, backward(): pl.pallas_call(functools.partial(backward_kernel, 2 * first), out_shape=(...  12.4 us
    ppermute x16, waiting for transfers between devices, swap(): lax.ppermute(x, axis, [(i, i ^ by) for i in range(lax.axis_size(axis))])  11.7 us
    pallas_call x1, Pallas kernels, forward(): pl.pallas_call(functools.partial(forward_kernel, block, sum(widths) // w....  10.8 us
    pallas_call x1, Pallas kernels, prep(): pl.pallas_call(functools.partial(prep_kernel, owned, block_rows, block_co...  7.15 us
    ppermute x2, starting transfers between devices, around(): lax.ppermute(x, axis, [(i, (i + by) % length) for i in range(length)])  3.26 us
    ppermute x2, waiting for transfers between devices, around(): lax.ppermute(x, axis, [(i, (i + by) % length) for i in range(length)])  1.93 us
    pallas_call x1, Pallas kernels, place(): pl.pallas_call(functools.partial(place_kernel, [len(each) for each in lis...  1.9 us
  transfers between devices with their start and end apart: 18, of which 8 were waited for; matrix products, arithmetic and copies ran while one was open for 1% of the time, Pallas kernels for 45%

profile of v5, /device:TPU:0, one launch (start us, length us, event | category | flops | bytes accessed | tf_op | source)
XLA Modules:
  0.0 68.1 jit_solution(15214359641646486588)
XLA Ops:
  0.7 3.0 %collective-permute-start = (bf16[128,3072]{1,0:T(8,128)(2,1)}, bf16[128,3072]{1,0:T(8,128)(2,1)S(1)}, u32[]{:S(2)}, u32[]{:S(2)}) collective-permute-start(bf16[128,3072]{1,0:T(8,128)(2,1)} %own.5), channel_id=1, source_target_pairs={{0,4},{4,0},{1,5},{5,1},{2,6},{6,2},{3,7},{7,3},{8,12},{12,8},{9,1... | collective-permute-start | bytes 2359304 | tf_op jit(solution)/shard_map/ppermute | solution.py:271
  4.3 7.2 %shard_map.95 = (bf16[461,128,128]{2,1,0:T(8,128)(2,1)S(1)}, bf16[256,6144]{1,0:T(8,128)(2,1)S(1)}, s32[1153]{0:T(1024)S(1)}) custom-call(s32[1]{0:T(128)} %bitcast.6.count, s32[1,460]{1,0:T(1,128)} %bitcast.11, s32[1,460]{1,0:T(1,128)} %bitcast.12, s32[1,16]{1,0:T(1,128)} %order_hbm.1, bf16[460,128,128]{2,1,0:T(8,128)(2,1)} %bitcast.10, bf16[256,6144]{1,0:T(8,128)(2,1)} %x_hbm.1), custom_call_target="tpu_custom_call" | custom-call | tf_op jit(solution)/shard_map/pallas_call | solution.py:110
  11.5 10.8 %shard_map.98 = (bf16[128,1536]{1,0:T(8,128)(2,1)S(1)}, bf16[128,1536]{1,0:T(8,128)(2,1)S(1)}, bf16[64,1536]{1,0:T(8,128)(2,1)S(1)}, bf16[64,1536]{1,0:T(8,128)(2,1)S(1)}, bf16[128,1536]{1,0:T(8,128)(2,1)S(1)}) custom-call(s32[16]{0:T(128)S(1)} %bitcast.7, s32[2]{0:T(128)S(1)} %bitcast.8, s32[1153]{0:T(1024)S(1)} %get-tuple-element.21.slot_of, ...), custom_call_target="tpu_custom_call" | custom-call | flops 1000 | bytes 1000 | tf_op jit(solution)/shard_map/pallas_call | solution.py:178
  22.3 1.5 %collective-permute-start.9 = (bf16[128,1536]{1,0:T(8,128)(2,1)S(1)}, bf16[128,1536]{1,0:T(8,128)(2,1)S(1)}, u32[]{:S(2)}, u32[]{:S(2)}) collective-permute-start(bf16[128,1536]{1,0:T(8,128)(2,1)S(1)} %get-tuple-element.38), channel_id=1, source_target_pairs={{0,2},{1,3},{2,0},{3,1},{4,6},{5,7},{6,4},{7,5},{8,10},{9,11},{10,... | collective-permute-start | bytes 1179656 | tf_op jit(solution)/shard_map/ppermute | solution.py:271
  24.7 4.1 %shard_map.96 = (bf16[128,2048]{1,0:T(8,128)(2,1)S(1)}, bf16[128,2048]{1,0:T(8,128)(2,1)S(1)}) custom-call(s32[1153]{0:T(1024)S(1)} %get-tuple-element.21.slot_of, bf16[128,3072]{1,0:T(8,128)(2,1)S(1)} %copy-done, bf16[128,3072]{1,0:T(8,128)(2,1)S(1)} %collective-permute-done.other, bf16[461,128,128]{2,1,0:T(8,128)(2,1)S(1)} %get-tuple-element.22.w), custom_call_target="tpu_custom_call" | custom-call | flops 1000 | bytes 1000 | tf_op jit(solution)/shard_map/pallas_call | solution.py:221
  28.8 4.7 %shard_map.97 = (bf16[128,2304]{1,0:T(8,128)(2,1)S(1)}, bf16[128,2304]{1,0:T(8,128)(2,1)S(1)}) custom-call(s32[1153]{0:T(1024)S(1)} %get-tuple-element.21.slot_of, bf16[128,3072]{1,0:T(8,128)(2,1)S(1)} %copy-done, bf16[128,3072]{1,0:T(8,128)(2,1)S(1)} %collective-permute-done.other, bf16[461,128,128]{2,1,0:T(8,128)(2,1)S(1)} %get-tuple-element.22.w), custom_call_target="tpu_custom_call" | custom-call | flops 1000 | bytes 1000 | tf_op jit(solution)/shard_map/pallas_call | solution.py:221
  34.1 1.3 %collective-permute-start.10 = (bf16[64,1536]{1,0:T(8,128)(2,1)S(1)}, bf16[64,1536]{1,0:T(8,128)(2,1)S(1)}, u32[]{:S(2)}, u32[]{:S(2)}) collective-permute-start(bf16[64,1536]{1,0:T(8,128)(2,1)S(1)} %slice.174), channel_id=1, source_target_pairs={{0,4},{4,0},{1,5},{5,1},{2,6},{6,2},{3,7},{7,3},{8,12},{12,8},{9,1... | collective-permute-start | bytes 589832 | tf_op jit(solution)/shard_map/ppermute | solution.py:271
  35.5 1.6 %collective-permute-start.15 = (bf16[128,1536]{1,0:T(8,128)(2,1)S(1)}, bf16[128,1536]{1,0:T(8,128)(2,1)S(1)}, u32[]{:S(2)}, u32[]{:S(2)}) collective-permute-start(bf16[128,1536]{1,0:T(8,128)(2,1)S(1)} %add_convert_fusion), channel_id=1, source_target_pairs={{0,8},{8,16},{16,24},{24,0},{1,9},{9,17},{17,25},{25,1},{2,10},{10... | collective-permute-start | bytes 1179656 | tf_op jit(solution)/shard_map/ppermute | solution.py:276
  37.3 0.8 %collective-permute-start.8 = (bf16[64,1536]{1,0:T(8,128)(2,1)S(1)}, bf16[64,1536]{1,0:T(8,128)(2,1)S(1)}, u32[]{:S(2)}, u32[]{:S(2)}) collective-permute-start(bf16[64,1536]{1,0:T(8,128)(2,1)S(1)} %get-tuple-element.36), channel_id=1, source_target_pairs={{0,4},{4,0},{1,5},{5,1},{2,6},{6,2},{3,7},{7,3},{8,12},{12,8},{9,1... | collective-permute-start | bytes 589832 | tf_op jit(solution)/shard_map/ppermute | solution.py:271
  38.6 3.7 %shard_map.99 = (bf16[128,1792]{1,0:T(8,128)(2,1)S(1)}, bf16[128,1792]{1,0:T(8,128)(2,1)S(1)}) custom-call(s32[1153]{0:T(1024)S(1)} %get-tuple-element.21.slot_of, bf16[128,3072]{1,0:T(8,128)(2,1)S(1)} %copy-done, bf16[128,3072]{1,0:T(8,128)(2,1)S(1)} %collective-permute-done.other, bf16[461,128,128]{2,1,0:T(8,128)(2,1)S(1)} %get-tuple-element.22.w, ...), custom_call_target="tpu_custom_call" | custom-call | flops 1000 | bytes 1000 | tf_op jit(solution)/shard_map/pallas_call | solution.py:221
  42.6 1.6 %collective-permute-start.5 = (bf16[64,2304]{1,0:T(8,128)(2,1)S(1)}, bf16[64,2304]{1,0:T(8,128)(2,1)S(1)}, u32[]{:S(2)}, u32[]{:S(2)}) collective-permute-start(bf16[64,2304]{1,0:T(8,128)(2,1)S(1)} %get-tuple-element.31), channel_id=1, source_target_pairs={{0,2},{1,3},{2,0},{3,1},{4,6},{5,7},{6,4},{7,5},{8,10},{9,11},{10,... | collective-permute-start | bytes 884744 | tf_op jit(solution)/shard_map/ppermute | solution.py:271
  44.2 1.0 %collective-permute-done.8 = bf16[64,1536]{1,0:T(8,128)(2,1)S(1)} collective-permute-done((bf16[64,1536]{1,0:T(8,128)(2,1)S(1)}, bf16[64,1536]{1,0:T(8,128)(2,1)S(1)}, u32[]{:S(2)}, u32[]{:S(2)}) %collective-permute-start.8) | collective-permute-done | bytes 196640 | tf_op jit(solution)/shard_map/ppermute | solution.py:271
  45.3 1.6 %collective-permute-start.11 = (bf16[128,1536]{1,0:T(8,128)(2,1)S(1)}, bf16[128,1536]{1,0:T(8,128)(2,1)S(1)}, u32[]{:S(2)}, u32[]{:S(2)}) collective-permute-start(bf16[128,1536]{1,0:T(8,128)(2,1)S(1)} %pad_maximum_fusion), channel_id=1, source_target_pairs={{0,8},{8,16},{16,24},{24,0},{1,9},{9,17},{17,25},{25,1},{2,10},{10... | collective-permute-start | bytes 1179656 | tf_op jit(solution)/shard_map/ppermute | solution.py:276
  46.9 1.3 %collective-permute-done.15 = bf16[128,1536]{1,0:T(8,128)(2,1)S(1)} collective-permute-done((bf16[128,1536]{1,0:T(8,128)(2,1)S(1)}, bf16[128,1536]{1,0:T(8,128)(2,1)S(1)}, u32[]{:S(2)}, u32[]{:S(2)}) %collective-permute-start.15) | collective-permute-done | bytes 393248 | tf_op jit(solution)/shard_map/ppermute | solution.py:276
  48.9 3.6 %collective-permute-done.5 = bf16[64,2304]{1,0:T(8,128)(2,1)S(1)} collective-permute-done((bf16[64,2304]{1,0:T(8,128)(2,1)S(1)}, bf16[64,2304]{1,0:T(8,128)(2,1)S(1)}, u32[]{:S(2)}, u32[]{:S(2)}) %collective-permute-start.5) | collective-permute-done | bytes 294944 | tf_op jit(solution)/shard_map/ppermute | solution.py:271
  52.6 1.3 %collective-permute-start.13 = (bf16[32,2304]{1,0:T(8,128)(2,1)S(1)}, bf16[32,2304]{1,0:T(8,128)(2,1)S(1)}, u32[]{:S(2)}, u32[]{:S(2)}) collective-permute-start(bf16[32,2304]{1,0:T(8,128)(2,1)S(1)} %get-tuple-element.46), channel_id=1, source_target_pairs={{0,4},{4,0},{1,5},{5,1},{2,6},{6,2},{3,7},{7,3},{8,12},{12,8},{9,1... | collective-permute-start | bytes 442376 | tf_op jit(solution)/shard_map/ppermute | solution.py:271
  54.0 1.6 %collective-permute-start.7 = (bf16[64,1792]{1,0:T(8,128)(2,1)S(1)}, bf16[64,1792]{1,0:T(8,128)(2,1)S(1)}, u32[]{:S(2)}, u32[]{:S(2)}) collective-permute-start(bf16[64,1792]{1,0:T(8,128)(2,1)S(1)} %get-tuple-element.45), channel_id=1, source_target_pairs={{0,2},{1,3},{2,0},{3,1},{4,6},{5,7},{6,4},{7,5},{8,10},{9,11},{10,... | collective-permute-start | bytes 688136 | tf_op jit(solution)/shard_map/ppermute | solution.py:271
  55.6 1.1 %collective-permute-done.16 = bf16[64,1536]{1,0:T(8,128)(2,1)S(1)} collective-permute-done((bf16[64,1536]{1,0:T(8,128)(2,1)S(1)}, bf16[64,1536]{1,0:T(8,128)(2,1)S(1)}, u32[]{:S(2)}, u32[]{:S(2)}) %collective-permute-start.16) | collective-permute-done | bytes 196640 | tf_op jit(solution)/shard_map/ppermute | solution.py:271
  57.6 1.3 %collective-permute-start.12 = (bf16[32,2048]{1,0:T(8,128)(2,1)S(1)}, bf16[32,2048]{1,0:T(8,128)(2,1)S(1)}, u32[]{:S(2)}, u32[]{:S(2)}) collective-permute-start(bf16[32,2048]{1,0:T(8,128)(2,1)S(1)} %get-tuple-element.39), channel_id=1, source_target_pairs={{0,4},{4,0},{1,5},{5,1},{2,6},{6,2},{3,7},{7,3},{8,12},{12,8},{9,1... | collective-permute-start | bytes 393224 | tf_op jit(solution)/shard_map/ppermute | solution.py:271
  58.9 2.4 %collective-permute-done.7 = bf16[64,1792]{1,0:T(8,128)(2,1)S(1)} collective-permute-done((bf16[64,1792]{1,0:T(8,128)(2,1)S(1)}, bf16[64,1792]{1,0:T(8,128)(2,1)S(1)}, u32[]{:S(2)}, u32[]{:S(2)}) %collective-permute-start.7) | collective-permute-done | bytes 229408 | tf_op jit(solution)/shard_map/ppermute | solution.py:271
  61.3 1.3 %collective-permute-start.14 = (bf16[32,1792]{1,0:T(8,128)(2,1)S(1)}, bf16[32,1792]{1,0:T(8,128)(2,1)S(1)}, u32[]{:S(2)}, u32[]{:S(2)}) collective-permute-start(bf16[32,1792]{1,0:T(8,128)(2,1)S(1)} %get-tuple-element.50), channel_id=1, source_target_pairs={{0,4},{4,0},{1,5},{5,1},{2,6},{6,2},{3,7},{7,3},{8,12},{12,8},{9,1... | collective-permute-start | bytes 344072 | tf_op jit(solution)/shard_map/ppermute | solution.py:271
  62.6 1.3 %collective-permute-done.12.refs_3_ = bf16[32,2048]{1,0:T(8,128)(2,1)S(1)} collective-permute-done((bf16[32,2048]{1,0:T(8,128)(2,1)S(1)}, bf16[32,2048]{1,0:T(8,128)(2,1)S(1)}, u32[]{:S(2)}, u32[]{:S(2)}) %collective-permute-start.12) | collective-permute-done | bytes 131104 | tf_op jit(solution)/shard_map/ppermute | solution.py:271
  63.9 2.2 %collective-permute-done.14.refs_5_ = bf16[32,1792]{1,0:T(8,128)(2,1)S(1)} collective-permute-done((bf16[32,1792]{1,0:T(8,128)(2,1)S(1)}, bf16[32,1792]{1,0:T(8,128)(2,1)S(1)}, u32[]{:S(2)}, u32[]{:S(2)}) %collective-permute-start.14) | collective-permute-done | bytes 114720 | tf_op jit(solution)/shard_map/ppermute | solution.py:271
  66.2 1.9 %shard_map.100 = (bf16[32,12288]{1,0:T(8,128)(2,1)}, bf16[32,12288]{1,0:T(8,128)(2,1)}) custom-call(s32[2]{0:T(128)S(1)} %bitcast.9, bf16[32,2048]{1,0:T(8,128)(2,1)S(1)} %get-tuple-element.49.refs_0_, bf16[32,2304]{1,0:T(8,128)(2,1)S(1)} %get-tuple-element.47.refs_1_, bf16[32,1792]{1,0:T(8,128)(2,1)S(1)} %get-tuple-element.51.refs_2_, ...), custom_call_target="tpu_custom_call" | custom-call | tf_op jit(solution)/shard_map/pallas_call | solution.py:261
  (42 shorter events, 4.4 us)
Async XLA Ops:
  0.6 10.9 %copy-start.1 = (s32[1,16]{1,0:T(1,128)S(1)}, s32[1,16]{1,0:T(1,128)}, u32[]{:S(2)}) copy-start(s32[1,16]{1,0:T(1,128)} %order_hbm.1) | copy-start | bytes 196
  0.6 10.9 %copy-start.2 = (s32[1,2]{1,0:T(1,128)S(1)}, s32[1,2]{1,0:T(1,128)}, u32[]{:S(2)}) copy-start(s32[1,2]{1,0:T(1,128)} %param.14) | copy-start | bytes 28
  0.7 21.7 %collective-permute-start = (bf16[128,3072]{1,0:T(8,128)(2,1)}, bf16[128,3072]{1,0:T(8,128)(2,1)S(1)}, u32[]{:S(2)}, u32[]{:S(2)}) collective-permute-start(bf16[128,3072]{1,0:T(8,128)(2,1)} %own.5), channel_id=1, source_target_pairs={{0,4},{4,0},{1,5},{5,1},{2,6},{6,2},{3,7},{7,3},{8,12},{12,8},{9,1... | collective-permute-start | bytes 2359304 | tf_op jit(solution)/shard_map/ppermute | solution.py:271
  4.3 20.3 %copy-start = (bf16[128,3072]{1,0:T(8,128)(2,1)S(1)}, bf16[128,3072]{1,0:T(8,128)(2,1)}, u32[]{:S(2)}) copy-start(bf16[128,3072]{1,0:T(8,128)(2,1)} %own.5) | copy-start | bytes 2359300
  22.3 11.7 %collective-permute-start.9 = (bf16[128,1536]{1,0:T(8,128)(2,1)S(1)}, bf16[128,1536]{1,0:T(8,128)(2,1)S(1)}, u32[]{:S(2)}, u32[]{:S(2)}) collective-permute-start(bf16[128,1536]{1,0:T(8,128)(2,1)S(1)} %get-tuple-element.38), channel_id=1, source_target_pairs={{0,2},{1,3},{2,0},{3,1},{4,6},{5,7},{6,4},{7,5},{8,10},{9,11},{10,... | collective-permute-start | bytes 1179656 | tf_op jit(solution)/shard_map/ppermute | solution.py:271
  23.9 11.5 %collective-permute-start.4 = (bf16[128,1536]{1,0:T(8,128)(2,1)S(1)}, bf16[128,1536]{1,0:T(8,128)(2,1)S(1)}, u32[]{:S(2)}, u32[]{:S(2)}) collective-permute-start(bf16[128,1536]{1,0:T(8,128)(2,1)S(1)} %get-tuple-element.30), channel_id=1, source_target_pairs={{0,4},{4,0},{1,5},{5,1},{2,6},{6,2},{3,7},{7,3},{8,12},{12,8},{9,1... | collective-permute-start | bytes 1179656 | tf_op jit(solution)/shard_map/ppermute | solution.py:271
  28.7 8.4 %collective-permute-start.1 = (bf16[128,2048]{1,0:T(8,128)(2,1)S(1)}, bf16[128,2048]{1,0:T(8,128)(2,1)S(1)}, u32[]{:S(2)}, u32[]{:S(2)}) collective-permute-start(bf16[128,2048]{1,0:T(8,128)(2,1)S(1)} %get-tuple-element.24), channel_id=1, source_target_pairs={{0,1},{1,0},{2,3},{3,2},{4,5},{5,4},{6,7},{7,6},{8,9},{9,8},{10,11... | collective-permute-start | bytes 1572872 | tf_op jit(solution)/shard_map/ppermute | solution.py:271
  33.5 9.0 %collective-permute-start.3 = (bf16[128,2304]{1,0:T(8,128)(2,1)S(1)}, bf16[128,2304]{1,0:T(8,128)(2,1)S(1)}, u32[]{:S(2)}, u32[]{:S(2)}) collective-permute-start(bf16[128,2304]{1,0:T(8,128)(2,1)S(1)} %get-tuple-element.26), channel_id=1, source_target_pairs={{0,1},{1,0},{2,3},{3,2},{4,5},{5,4},{6,7},{7,6},{8,9},{9,8},{10,11... | collective-permute-start | bytes 1769480 | tf_op jit(solution)/shard_map/ppermute | solution.py:271
  34.1 8.2 %collective-permute-start.10 = (bf16[64,1536]{1,0:T(8,128)(2,1)S(1)}, bf16[64,1536]{1,0:T(8,128)(2,1)S(1)}, u32[]{:S(2)}, u32[]{:S(2)}) collective-permute-start(bf16[64,1536]{1,0:T(8,128)(2,1)S(1)} %slice.174), channel_id=1, source_target_pairs={{0,4},{4,0},{1,5},{5,1},{2,6},{6,2},{3,7},{7,3},{8,12},{12,8},{9,1... | collective-permute-start | bytes 589832 | tf_op jit(solution)/shard_map/ppermute | solution.py:271
  35.5 12.7 %collective-permute-start.15 = (bf16[128,1536]{1,0:T(8,128)(2,1)S(1)}, bf16[128,1536]{1,0:T(8,128)(2,1)S(1)}, u32[]{:S(2)}, u32[]{:S(2)}) collective-permute-start(bf16[128,1536]{1,0:T(8,128)(2,1)S(1)} %add_convert_fusion), channel_id=1, source_target_pairs={{0,8},{8,16},{16,24},{24,0},{1,9},{9,17},{17,25},{25,1},{2,10},{10... | collective-permute-start | bytes 1179656 | tf_op jit(solution)/shard_map/ppermute | solution.py:276
  37.3 7.9 %collective-permute-start.8 = (bf16[64,1536]{1,0:T(8,128)(2,1)S(1)}, bf16[64,1536]{1,0:T(8,128)(2,1)S(1)}, u32[]{:S(2)}, u32[]{:S(2)}) collective-permute-start(bf16[64,1536]{1,0:T(8,128)(2,1)S(1)} %get-tuple-element.36), channel_id=1, source_target_pairs={{0,4},{4,0},{1,5},{5,1},{2,6},{6,2},{3,7},{7,3},{8,12},{12,8},{9,1... | collective-permute-start | bytes 589832 | tf_op jit(solution)/shard_map/ppermute | solution.py:271
  38.1 10.7 %collective-permute-start.2 = (bf16[64,2048]{1,0:T(8,128)(2,1)S(1)}, bf16[64,2048]{1,0:T(8,128)(2,1)S(1)}, u32[]{:S(2)}, u32[]{:S(2)}) collective-permute-start(bf16[64,2048]{1,0:T(8,128)(2,1)S(1)} %get-tuple-element.43.refs_0_), channel_id=1, source_target_pairs={{0,2},{1,3},{2,0},{3,1},{4,6},{5,7},{6,4},{7,5},{8,10},{9,11},{10,... | collective-permute-start | bytes 786440 | tf_op jit(solution)/shard_map/ppermute | solution.py:271
  42.3 11.6 %collective-permute-start.6 = (bf16[128,1792]{1,0:T(8,128)(2,1)S(1)}, bf16[128,1792]{1,0:T(8,128)(2,1)S(1)}, u32[]{:S(2)}, u32[]{:S(2)}) collective-permute-start(bf16[128,1792]{1,0:T(8,128)(2,1)S(1)} %get-tuple-element.33), channel_id=1, source_target_pairs={{0,1},{1,0},{2,3},{3,2},{4,5},{5,4},{6,7},{7,6},{8,9},{9,8},{10,11... | collective-permute-start | bytes 1376264 | tf_op jit(solution)/shard_map/ppermute | solution.py:271
  42.6 9.9 %collective-permute-start.5 = (bf16[64,2304]{1,0:T(8,128)(2,1)S(1)}, bf16[64,2304]{1,0:T(8,128)(2,1)S(1)}, u32[]{:S(2)}, u32[]{:S(2)}) collective-permute-start(bf16[64,2304]{1,0:T(8,128)(2,1)S(1)} %get-tuple-element.31), channel_id=1, source_target_pairs={{0,2},{1,3},{2,0},{3,1},{4,6},{5,7},{6,4},{7,5},{8,10},{9,11},{10,... | collective-permute-start | bytes 884744 | tf_op jit(solution)/shard_map/ppermute | solution.py:271
  45.3 12.1 %collective-permute-start.11 = (bf16[128,1536]{1,0:T(8,128)(2,1)S(1)}, bf16[128,1536]{1,0:T(8,128)(2,1)S(1)}, u32[]{:S(2)}, u32[]{:S(2)}) collective-permute-start(bf16[128,1536]{1,0:T(8,128)(2,1)S(1)} %pad_maximum_fusion), channel_id=1, source_target_pairs={{0,8},{8,16},{16,24},{24,0},{1,9},{9,17},{17,25},{25,1},{2,10},{10... | collective-permute-start | bytes 1179656 | tf_op jit(solution)/shard_map/ppermute | solution.py:276
  48.2 8.5 %collective-permute-start.16 = (bf16[64,1536]{1,0:T(8,128)(2,1)S(1)}, bf16[64,1536]{1,0:T(8,128)(2,1)S(1)}, u32[]{:S(2)}, u32[]{:S(2)}) collective-permute-start(bf16[64,1536]{1,0:T(8,128)(2,1)S(1)} %slice.182), channel_id=1, source_target_pairs={{0,2},{1,3},{2,0},{3,1},{4,6},{5,7},{6,4},{7,5},{8,10},{9,11},{10,... | collective-permute-start | bytes 589832 | tf_op jit(solution)/shard_map/ppermute | solution.py:271
  52.6 10.0 %collective-permute-start.13 = (bf16[32,2304]{1,0:T(8,128)(2,1)S(1)}, bf16[32,2304]{1,0:T(8,128)(2,1)S(1)}, u32[]{:S(2)}, u32[]{:S(2)}) collective-permute-start(bf16[32,2304]{1,0:T(8,128)(2,1)S(1)} %get-tuple-element.46), channel_id=1, source_target_pairs={{0,4},{4,0},{1,5},{5,1},{2,6},{6,2},{3,7},{7,3},{8,12},{12,8},{9,1... | collective-permute-start | bytes 442376 | tf_op jit(solution)/shard_map/ppermute | solution.py:271
  54.0 7.2 %collective-permute-start.7 = (bf16[64,1792]{1,0:T(8,128)(2,1)S(1)}, bf16[64,1792]{1,0:T(8,128)(2,1)S(1)}, u32[]{:S(2)}, u32[]{:S(2)}) collective-permute-start(bf16[64,1792]{1,0:T(8,128)(2,1)S(1)} %get-tuple-element.45), channel_id=1, source_target_pairs={{0,2},{1,3},{2,0},{3,1},{4,6},{5,7},{6,4},{7,5},{8,10},{9,11},{10,... | collective-permute-start | bytes 688136 | tf_op jit(solution)/shard_map/ppermute | solution.py:271
  57.5 8.7 %collective-permute-start.17 = (bf16[32,6144]{1,0:T(8,128)(2,1)S(1)}, bf16[32,6144]{1,0:T(8,128)(2,1)S(1)}, u32[]{:S(2)}, u32[]{:S(2)}) collective-permute-start(bf16[32,6144]{1,0:T(8,128)(2,1)S(1)} %pad_maximum_fusion.1), channel_id=1, source_target_pairs={{0,1},{1,0},{2,3},{3,2},{4,5},{5,4},{6,7},{7,6},{8,9},{9,8},{10,11... | collective-permute-start | bytes 1179656 | tf_op jit(solution)/shard_map/ppermute | solution.py:271
  57.6 6.4 %collective-permute-start.12 = (bf16[32,2048]{1,0:T(8,128)(2,1)S(1)}, bf16[32,2048]{1,0:T(8,128)(2,1)S(1)}, u32[]{:S(2)}, u32[]{:S(2)}) collective-permute-start(bf16[32,2048]{1,0:T(8,128)(2,1)S(1)} %get-tuple-element.39), channel_id=1, source_target_pairs={{0,4},{4,0},{1,5},{5,1},{2,6},{6,2},{3,7},{7,3},{8,12},{12,8},{9,1... | collective-permute-start | bytes 393224 | tf_op jit(solution)/shard_map/ppermute | solution.py:271
  61.3 4.9 %collective-permute-start.14 = (bf16[32,1792]{1,0:T(8,128)(2,1)S(1)}, bf16[32,1792]{1,0:T(8,128)(2,1)S(1)}, u32[]{:S(2)}, u32[]{:S(2)}) collective-permute-start(bf16[32,1792]{1,0:T(8,128)(2,1)S(1)} %get-tuple-element.50), channel_id=1, source_target_pairs={{0,4},{4,0},{1,5},{5,1},{2,6},{6,2},{3,7},{7,3},{8,12},{12,8},{9,1... | collective-permute-start | bytes 344072 | tf_op jit(solution)/shard_map/ppermute | solution.py:271

commit v6 on v5

--- a/solution.py
+++ b/solution.py
@@ -9,14 +9,13 @@
 
 
 F_PAIRS = (6, 6)
-B_PAIRS = (8, 9, 7)
+B_PAIRS = (8, 10, 6)
 JOINT = 1
 F_FAR_FIRST = (0, 1)
 TRACE_FIRST = ()
 B_JOINED = 1
 C_SPLIT = 1
 TIES = {
-    "b0": ("x1", "z1",),
     "k2": ("c0",),
     "u1": ("d0",),
     "x1": ("y0",),

time: 68.2 us -> 68.1 us (level)
    ppermute x16, waiting for transfers between devices: 11.7 us -> 12.4 us  [swap(): lax.ppermute(x, axis, [(i, i ^ by) for i in range(lax.axis_size(axis))])]
  transfers between devices with their start and end apart: 18 -> 18, of which waited for: 8 -> 7; matrix products, arithmetic and copies ran while one was open for 1% -> 1% of each run, Pallas kernels for 45% -> 45%
where the time goes in v6:
time: 68.1 us; the launch traced here: 68 us
  Pallas kernels  32.2 us (47%)
  starting transfers between devices  19.3 us (28%)
  waiting for transfers between devices  14 us (21%)
  between operations  1.53 us (2%)
  other arithmetic  0.82 us (1%)
    ppermute x16, starting transfers between devices, swap(): lax.ppermute(x, axis, [(i, i ^ by) for i in range(lax.axis_size(axis))])  16 us
    ppermute x16, waiting for transfers between devices, swap(): lax.ppermute(x, axis, [(i, i ^ by) for i in range(lax.axis_size(axis))])  12.4 us
    pallas_call x3, Pallas kernels, backward(): pl.pallas_call(functools.partial(backward_kernel, 2 * first), out_shape=(...  12.4 us
    pallas_call x1, Pallas kernels, forward(): pl.pallas_call(functools.partial(forward_kernel, block, sum(widths) // w....  10.8 us
    pallas_call x1, Pallas kernels, prep(): pl.pallas_call(functools.partial(prep_kernel, owned, block_rows, block_co...  7.15 us
    ppermute x2, starting transfers between devices, around(): lax.ppermute(x, axis, [(i, (i + by) % length) for i in range(length)])  3.26 us
    pallas_call x1, Pallas kernels, place(): pl.pallas_call(functools.partial(place_kernel, [len(each) for each in lis...  1.9 us
    ppermute x2, waiting for transfers between devices, around(): lax.ppermute(x, axis, [(i, (i + by) % length) for i in range(length)])  1.62 us
  transfers between devices with their start and end apart: 18, of which 7 were waited for; matrix products, arithmetic and copies ran while one was open for 1% of the time, Pallas kernels for 45%

profile of v6, /device:TPU:0, one launch (start us, length us, event | category | flops | bytes accessed | tf_op | source)
XLA Modules:
  0.0 68.0 jit_solution(4232249955876725880)
XLA Ops:
  0.7 3.0 %collective-permute-start = (bf16[128,3072]{1,0:T(8,128)(2,1)}, bf16[128,3072]{1,0:T(8,128)(2,1)S(1)}, u32[]{:S(2)}, u32[]{:S(2)}) collective-permute-start(bf16[128,3072]{1,0:T(8,128)(2,1)} %own.5), channel_id=1, source_target_pairs={{0,4},{4,0},{1,5},{5,1},{2,6},{6,2},{3,7},{7,3},{8,12},{12,8},{9,1... | collective-permute-start | bytes 2359304 | tf_op jit(solution)/shard_map/ppermute | solution.py:270
  4.3 7.2 %shard_map.95 = (bf16[461,128,128]{2,1,0:T(8,128)(2,1)S(1)}, bf16[256,6144]{1,0:T(8,128)(2,1)S(1)}, s32[1153]{0:T(1024)S(1)}) custom-call(s32[1]{0:T(128)} %bitcast.6.count, s32[1,460]{1,0:T(1,128)} %bitcast.11, s32[1,460]{1,0:T(1,128)} %bitcast.12, s32[1,16]{1,0:T(1,128)} %order_hbm.1, bf16[460,128,128]{2,1,0:T(8,128)(2,1)} %bitcast.10, bf16[256,6144]{1,0:T(8,128)(2,1)} %x_hbm.1), custom_call_target="tpu_custom_call" | custom-call | tf_op jit(solution)/shard_map/pallas_call | solution.py:109
  11.5 10.8 %shard_map.98 = (bf16[128,1536]{1,0:T(8,128)(2,1)S(1)}, bf16[128,1536]{1,0:T(8,128)(2,1)S(1)}, bf16[64,1536]{1,0:T(8,128)(2,1)S(1)}, bf16[64,1536]{1,0:T(8,128)(2,1)S(1)}, bf16[128,1536]{1,0:T(8,128)(2,1)S(1)}) custom-call(s32[16]{0:T(128)S(1)} %bitcast.7, s32[2]{0:T(128)S(1)} %bitcast.8, s32[1153]{0:T(1024)S(1)} %get-tuple-element.20.slot_of, ...), custom_call_target="tpu_custom_call" | custom-call | flops 1000 | bytes 1000 | tf_op jit(solution)/shard_map/pallas_call | solution.py:177
  22.3 1.5 %collective-permute-start.13 = (bf16[128,1536]{1,0:T(8,128)(2,1)S(1)}, bf16[128,1536]{1,0:T(8,128)(2,1)S(1)}, u32[]{:S(2)}, u32[]{:S(2)}) collective-permute-start(bf16[128,1536]{1,0:T(8,128)(2,1)S(1)} %get-tuple-element.37), channel_id=1, source_target_pairs={{0,2},{1,3},{2,0},{3,1},{4,6},{5,7},{6,4},{7,5},{8,10},{9,11},{10,... | collective-permute-start | bytes 1179656 | tf_op jit(solution)/shard_map/ppermute | solution.py:270
  23.9 0.8 %collective-permute-start.4 = (bf16[128,1536]{1,0:T(8,128)(2,1)S(1)}, bf16[128,1536]{1,0:T(8,128)(2,1)S(1)}, u32[]{:S(2)}, u32[]{:S(2)}) collective-permute-start(bf16[128,1536]{1,0:T(8,128)(2,1)S(1)} %get-tuple-element.29), channel_id=1, source_target_pairs={{0,4},{4,0},{1,5},{5,1},{2,6},{6,2},{3,7},{7,3},{8,12},{12,8},{9,1... | collective-permute-start | bytes 1179656 | tf_op jit(solution)/shard_map/ppermute | solution.py:270
  24.7 4.1 %shard_map.96 = (bf16[128,2048]{1,0:T(8,128)(2,1)S(1)}, bf16[128,2048]{1,0:T(8,128)(2,1)S(1)}) custom-call(s32[1153]{0:T(1024)S(1)} %get-tuple-element.20.slot_of, bf16[128,3072]{1,0:T(8,128)(2,1)S(1)} %copy-done, bf16[128,3072]{1,0:T(8,128)(2,1)S(1)} %collective-permute-done.other, bf16[461,128,128]{2,1,0:T(8,128)(2,1)S(1)} %get-tuple-element.21.w), custom_call_target="tpu_custom_call" | custom-call | flops 1000 | bytes 1000 | tf_op jit(solution)/shard_map/pallas_call | solution.py:220
  28.8 5.1 %shard_map.97 = (bf16[128,2560]{1,0:T(8,128)(2,1)S(1)}, bf16[128,2560]{1,0:T(8,128)(2,1)S(1)}) custom-call(s32[1153]{0:T(1024)S(1)} %get-tuple-element.20.slot_of, bf16[128,3072]{1,0:T(8,128)(2,1)S(1)} %copy-done, bf16[128,3072]{1,0:T(8,128)(2,1)S(1)} %collective-permute-done.other, bf16[461,128,128]{2,1,0:T(8,128)(2,1)S(1)} %get-tuple-element.21.w), custom_call_target="tpu_custom_call" | custom-call | flops 1000 | bytes 1000 | tf_op jit(solution)/shard_map/pallas_call | solution.py:220
  34.5 1.3 %collective-permute-start.14 = (bf16[64,1536]{1,0:T(8,128)(2,1)S(1)}, bf16[64,1536]{1,0:T(8,128)(2,1)S(1)}, u32[]{:S(2)}, u32[]{:S(2)}) collective-permute-start(bf16[64,1536]{1,0:T(8,128)(2,1)S(1)} %slice.177), channel_id=1, source_target_pairs={{0,4},{4,0},{1,5},{5,1},{2,6},{6,2},{3,7},{7,3},{8,12},{12,8},{9,1... | collective-permute-start | bytes 589832 | tf_op jit(solution)/shard_map/ppermute | solution.py:270
  35.9 1.6 %collective-permute-start.11 = (bf16[128,1536]{1,0:T(8,128)(2,1)S(1)}, bf16[128,1536]{1,0:T(8,128)(2,1)S(1)}, u32[]{:S(2)}, u32[]{:S(2)}) collective-permute-start(bf16[128,1536]{1,0:T(8,128)(2,1)S(1)} %add_convert_fusion), channel_id=1, source_target_pairs={{0,8},{8,16},{16,24},{24,0},{1,9},{9,17},{17,25},{25,1},{2,10},{10... | collective-permute-start | bytes 1179656 | tf_op jit(solution)/shard_map/ppermute | solution.py:275
  37.7 0.8 %collective-permute-start.12 = (bf16[64,1536]{1,0:T(8,128)(2,1)S(1)}, bf16[64,1536]{1,0:T(8,128)(2,1)S(1)}, u32[]{:S(2)}, u32[]{:S(2)}) collective-permute-start(bf16[64,1536]{1,0:T(8,128)(2,1)S(1)} %get-tuple-element.35), channel_id=1, source_target_pairs={{0,4},{4,0},{1,5},{5,1},{2,6},{6,2},{3,7},{7,3},{8,12},{12,8},{9,1... | collective-permute-start | bytes 589832 | tf_op jit(solution)/shard_map/ppermute | solution.py:270
  39.0 3.3 %shard_map.99 = (bf16[128,1536]{1,0:T(8,128)(2,1)S(1)}, bf16[128,1536]{1,0:T(8,128)(2,1)S(1)}) custom-call(s32[1153]{0:T(1024)S(1)} %get-tuple-element.20.slot_of, bf16[128,3072]{1,0:T(8,128)(2,1)S(1)} %copy-done, bf16[128,3072]{1,0:T(8,128)(2,1)S(1)} %collective-permute-done.other, bf16[461,128,128]{2,1,0:T(8,128)(2,1)S(1)} %get-tuple-element.21.w, ...), custom_call_target="tpu_custom_call" | custom-call | flops 1000 | bytes 1000 | tf_op jit(solution)/shard_map/pallas_call | solution.py:220
  42.6 1.6 %collective-permute-start.5 = (bf16[64,2560]{1,0:T(8,128)(2,1)S(1)}, bf16[64,2560]{1,0:T(8,128)(2,1)S(1)}, u32[]{:S(2)}, u32[]{:S(2)}) collective-permute-start(bf16[64,2560]{1,0:T(8,128)(2,1)S(1)} %get-tuple-element.30), channel_id=1, source_target_pairs={{0,2},{1,3},{2,0},{3,1},{4,6},{5,7},{6,4},{7,5},{8,10},{9,11},{10,... | collective-permute-start | bytes 983048 | tf_op jit(solution)/shard_map/ppermute | solution.py:270
  44.2 1.4 %collective-permute-done.12 = bf16[64,1536]{1,0:T(8,128)(2,1)S(1)} collective-permute-done((bf16[64,1536]{1,0:T(8,128)(2,1)S(1)}, bf16[64,1536]{1,0:T(8,128)(2,1)S(1)}, u32[]{:S(2)}, u32[]{:S(2)}) %collective-permute-start.12) | collective-permute-done | bytes 196640 | tf_op jit(solution)/shard_map/ppermute | solution.py:270
  45.7 1.6 %collective-permute-start.15 = (bf16[128,1536]{1,0:T(8,128)(2,1)S(1)}, bf16[128,1536]{1,0:T(8,128)(2,1)S(1)}, u32[]{:S(2)}, u32[]{:S(2)}) collective-permute-start(bf16[128,1536]{1,0:T(8,128)(2,1)S(1)} %pad_maximum_fusion), channel_id=1, source_target_pairs={{0,8},{8,16},{16,24},{24,0},{1,9},{9,17},{17,25},{25,1},{2,10},{10... | collective-permute-start | bytes 1179656 | tf_op jit(solution)/shard_map/ppermute | solution.py:275
  47.3 1.3 %collective-permute-done.11 = bf16[128,1536]{1,0:T(8,128)(2,1)S(1)} collective-permute-done((bf16[128,1536]{1,0:T(8,128)(2,1)S(1)}, bf16[128,1536]{1,0:T(8,128)(2,1)S(1)}, u32[]{:S(2)}, u32[]{:S(2)}) %collective-permute-start.11) | collective-permute-done | bytes 393248 | tf_op jit(solution)/shard_map/ppermute | solution.py:275
  49.3 0.8 %collective-permute-start.8 = (bf16[32,2048]{1,0:T(8,128)(2,1)S(1)}, bf16[32,2048]{1,0:T(8,128)(2,1)S(1)}, u32[]{:S(2)}, u32[]{:S(2)}) collective-permute-start(bf16[32,2048]{1,0:T(8,128)(2,1)S(1)} %get-tuple-element.46), channel_id=1, source_target_pairs={{0,4},{4,0},{1,5},{5,1},{2,6},{6,2},{3,7},{7,3},{8,12},{12,8},{9,1... | collective-permute-start | bytes 393224 | tf_op jit(solution)/shard_map/ppermute | solution.py:270
  50.2 1.6 %collective-permute-start.7 = (bf16[64,1536]{1,0:T(8,128)(2,1)S(1)}, bf16[64,1536]{1,0:T(8,128)(2,1)S(1)}, u32[]{:S(2)}, u32[]{:S(2)}) collective-permute-start(bf16[64,1536]{1,0:T(8,128)(2,1)S(1)} %get-tuple-element.43), channel_id=1, source_target_pairs={{0,2},{1,3},{2,0},{3,1},{4,6},{5,7},{6,4},{7,5},{8,10},{9,11},{10,... | collective-permute-start | bytes 589832 | tf_op jit(solution)/shard_map/ppermute | solution.py:270
  51.8 1.4 %collective-permute-done.5 = bf16[64,2560]{1,0:T(8,128)(2,1)S(1)} collective-permute-done((bf16[64,2560]{1,0:T(8,128)(2,1)S(1)}, bf16[64,2560]{1,0:T(8,128)(2,1)S(1)}, u32[]{:S(2)}, u32[]{:S(2)}) %collective-permute-start.5) | collective-permute-done | bytes 327712 | tf_op jit(solution)/shard_map/ppermute | solution.py:270
  53.3 1.3 %collective-permute-start.9 = (bf16[32,2560]{1,0:T(8,128)(2,1)S(1)}, bf16[32,2560]{1,0:T(8,128)(2,1)S(1)}, u32[]{:S(2)}, u32[]{:S(2)}) collective-permute-start(bf16[32,2560]{1,0:T(8,128)(2,1)S(1)} %get-tuple-element.44), channel_id=1, source_target_pairs={{0,4},{4,0},{1,5},{5,1},{2,6},{6,2},{3,7},{7,3},{8,12},{12,8},{9,1... | collective-permute-start | bytes 491528 | tf_op jit(solution)/shard_map/ppermute | solution.py:270
  54.6 2.8 %collective-permute-done.16 = bf16[64,1536]{1,0:T(8,128)(2,1)S(1)} collective-permute-done((bf16[64,1536]{1,0:T(8,128)(2,1)S(1)}, bf16[64,1536]{1,0:T(8,128)(2,1)S(1)}, u32[]{:S(2)}, u32[]{:S(2)}) %collective-permute-start.16) | collective-permute-done | bytes 196640 | tf_op jit(solution)/shard_map/ppermute | solution.py:270
  58.0 3.4 %collective-permute-done.7 = bf16[64,1536]{1,0:T(8,128)(2,1)S(1)} collective-permute-done((bf16[64,1536]{1,0:T(8,128)(2,1)S(1)}, bf16[64,1536]{1,0:T(8,128)(2,1)S(1)}, u32[]{:S(2)}, u32[]{:S(2)}) %collective-permute-start.7) | collective-permute-done | bytes 196640 | tf_op jit(solution)/shard_map/ppermute | solution.py:270
  61.4 1.3 %collective-permute-start.10 = (bf16[32,1536]{1,0:T(8,128)(2,1)S(1)}, bf16[32,1536]{1,0:T(8,128)(2,1)S(1)}, u32[]{:S(2)}, u32[]{:S(2)}) collective-permute-start(bf16[32,1536]{1,0:T(8,128)(2,1)S(1)} %get-tuple-element.54), channel_id=1, source_target_pairs={{0,4},{4,0},{1,5},{5,1},{2,6},{6,2},{3,7},{7,3},{8,12},{12,8},{9,1... | collective-permute-start | bytes 294920 | tf_op jit(solution)/shard_map/ppermute | solution.py:270
  62.7 3.4 %collective-permute-done.10.refs_5_ = bf16[32,1536]{1,0:T(8,128)(2,1)S(1)} collective-permute-done((bf16[32,1536]{1,0:T(8,128)(2,1)S(1)}, bf16[32,1536]{1,0:T(8,128)(2,1)S(1)}, u32[]{:S(2)}, u32[]{:S(2)}) %collective-permute-start.10) | collective-permute-done | bytes 98336 | tf_op jit(solution)/shard_map/ppermute | solution.py:270
  66.1 1.9 %shard_map.100 = (bf16[32,12288]{1,0:T(8,128)(2,1)}, bf16[32,12288]{1,0:T(8,128)(2,1)}) custom-call(s32[2]{0:T(128)S(1)} %bitcast.9, bf16[32,2048]{1,0:T(8,128)(2,1)S(1)} %get-tuple-element.47.refs_0_, bf16[32,2560]{1,0:T(8,128)(2,1)S(1)} %get-tuple-element.45.refs_1_, bf16[32,1536]{1,0:T(8,128)(2,1)S(1)} %get-tuple-element.55.refs_2_, ...), custom_call_target="tpu_custom_call" | custom-call | tf_op jit(solution)/shard_map/pallas_call | solution.py:260
  (42 shorter events, 3.2 us)
Async XLA Ops:
  0.6 10.9 %copy-start.1 = (s32[1,16]{1,0:T(1,128)S(1)}, s32[1,16]{1,0:T(1,128)}, u32[]{:S(2)}) copy-start(s32[1,16]{1,0:T(1,128)} %order_hbm.1) | copy-start | bytes 196
  0.6 10.9 %copy-start.2 = (s32[1,2]{1,0:T(1,128)S(1)}, s32[1,2]{1,0:T(1,128)}, u32[]{:S(2)}) copy-start(s32[1,2]{1,0:T(1,128)} %param.14) | copy-start | bytes 28
  0.7 21.7 %collective-permute-start = (bf16[128,3072]{1,0:T(8,128)(2,1)}, bf16[128,3072]{1,0:T(8,128)(2,1)S(1)}, u32[]{:S(2)}, u32[]{:S(2)}) collective-permute-start(bf16[128,3072]{1,0:T(8,128)(2,1)} %own.5), channel_id=1, source_target_pairs={{0,4},{4,0},{1,5},{5,1},{2,6},{6,2},{3,7},{7,3},{8,12},{12,8},{9,1... | collective-permute-start | bytes 2359304 | tf_op jit(solution)/shard_map/ppermute | solution.py:270
  4.3 20.3 %copy-start = (bf16[128,3072]{1,0:T(8,128)(2,1)S(1)}, bf16[128,3072]{1,0:T(8,128)(2,1)}, u32[]{:S(2)}) copy-start(bf16[128,3072]{1,0:T(8,128)(2,1)} %own.5) | copy-start | bytes 2359300
  22.3 12.1 %collective-permute-start.13 = (bf16[128,1536]{1,0:T(8,128)(2,1)S(1)}, bf16[128,1536]{1,0:T(8,128)(2,1)S(1)}, u32[]{:S(2)}, u32[]{:S(2)}) collective-permute-start(bf16[128,1536]{1,0:T(8,128)(2,1)S(1)} %get-tuple-element.37), channel_id=1, source_target_pairs={{0,2},{1,3},{2,0},{3,1},{4,6},{5,7},{6,4},{7,5},{8,10},{9,11},{10,... | collective-permute-start | bytes 1179656 | tf_op jit(solution)/shard_map/ppermute | solution.py:270
  23.9 11.9 %collective-permute-start.4 = (bf16[128,1536]{1,0:T(8,128)(2,1)S(1)}, bf16[128,1536]{1,0:T(8,128)(2,1)S(1)}, u32[]{:S(2)}, u32[]{:S(2)}) collective-permute-start(bf16[128,1536]{1,0:T(8,128)(2,1)S(1)} %get-tuple-element.29), channel_id=1, source_target_pairs={{0,4},{4,0},{1,5},{5,1},{2,6},{6,2},{3,7},{7,3},{8,12},{12,8},{9,1... | collective-permute-start | bytes 1179656 | tf_op jit(solution)/shard_map/ppermute | solution.py:270
  28.7 8.8 %collective-permute-start.1 = (bf16[128,2048]{1,0:T(8,128)(2,1)S(1)}, bf16[128,2048]{1,0:T(8,128)(2,1)S(1)}, u32[]{:S(2)}, u32[]{:S(2)}) collective-permute-start(bf16[128,2048]{1,0:T(8,128)(2,1)S(1)} %get-tuple-element.23), channel_id=1, source_target_pairs={{0,1},{1,0},{2,3},{3,2},{4,5},{5,4},{6,7},{7,6},{8,9},{9,8},{10,11... | collective-permute-start | bytes 1572872 | tf_op jit(solution)/shard_map/ppermute | solution.py:270
  33.9 8.6 %collective-permute-start.3 = (bf16[128,2560]{1,0:T(8,128)(2,1)S(1)}, bf16[128,2560]{1,0:T(8,128)(2,1)S(1)}, u32[]{:S(2)}, u32[]{:S(2)}) collective-permute-start(bf16[128,2560]{1,0:T(8,128)(2,1)S(1)} %get-tuple-element.25), channel_id=1, source_target_pairs={{0,1},{1,0},{2,3},{3,2},{4,5},{5,4},{6,7},{7,6},{8,9},{9,8},{10,11... | collective-permute-start | bytes 1966088 | tf_op jit(solution)/shard_map/ppermute | solution.py:270
  34.5 7.8 %collective-permute-start.14 = (bf16[64,1536]{1,0:T(8,128)(2,1)S(1)}, bf16[64,1536]{1,0:T(8,128)(2,1)S(1)}, u32[]{:S(2)}, u32[]{:S(2)}) collective-permute-start(bf16[64,1536]{1,0:T(8,128)(2,1)S(1)} %slice.177), channel_id=1, source_target_pairs={{0,4},{4,0},{1,5},{5,1},{2,6},{6,2},{3,7},{7,3},{8,12},{12,8},{9,1... | collective-permute-start | bytes 589832 | tf_op jit(solution)/shard_map/ppermute | solution.py:270
  35.9 12.7 %collective-permute-start.11 = (bf16[128,1536]{1,0:T(8,128)(2,1)S(1)}, bf16[128,1536]{1,0:T(8,128)(2,1)S(1)}, u32[]{:S(2)}, u32[]{:S(2)}) collective-permute-start(bf16[128,1536]{1,0:T(8,128)(2,1)S(1)} %add_convert_fusion), channel_id=1, source_target_pairs={{0,8},{8,16},{16,24},{24,0},{1,9},{9,17},{17,25},{25,1},{2,10},{10... | collective-permute-start | bytes 1179656 | tf_op jit(solution)/shard_map/ppermute | solution.py:275
  37.7 7.9 %collective-permute-start.12 = (bf16[64,1536]{1,0:T(8,128)(2,1)S(1)}, bf16[64,1536]{1,0:T(8,128)(2,1)S(1)}, u32[]{:S(2)}, u32[]{:S(2)}) collective-permute-start(bf16[64,1536]{1,0:T(8,128)(2,1)S(1)} %get-tuple-element.35), channel_id=1, source_target_pairs={{0,4},{4,0},{1,5},{5,1},{2,6},{6,2},{3,7},{7,3},{8,12},{12,8},{9,1... | collective-permute-start | bytes 589832 | tf_op jit(solution)/shard_map/ppermute | solution.py:270
  38.5 10.7 %collective-permute-start.2 = (bf16[64,2048]{1,0:T(8,128)(2,1)S(1)}, bf16[64,2048]{1,0:T(8,128)(2,1)S(1)}, u32[]{:S(2)}, u32[]{:S(2)}) collective-permute-start(bf16[64,2048]{1,0:T(8,128)(2,1)S(1)} %get-tuple-element.41.refs_0_), channel_id=1, source_target_pairs={{0,2},{1,3},{2,0},{3,1},{4,6},{5,7},{6,4},{7,5},{8,10},{9,11},{10,... | collective-permute-start | bytes 786440 | tf_op jit(solution)/shard_map/ppermute | solution.py:270
  42.3 7.8 %collective-permute-start.6 = (bf16[128,1536]{1,0:T(8,128)(2,1)S(1)}, bf16[128,1536]{1,0:T(8,128)(2,1)S(1)}, u32[]{:S(2)}, u32[]{:S(2)}) collective-permute-start(bf16[128,1536]{1,0:T(8,128)(2,1)S(1)} %get-tuple-element.32), channel_id=1, source_target_pairs={{0,1},{1,0},{2,3},{3,2},{4,5},{5,4},{6,7},{7,6},{8,9},{9,8},{10,11... | collective-permute-start | bytes 1179656 | tf_op jit(solution)/shard_map/ppermute | solution.py:270
  42.6 10.6 %collective-permute-start.5 = (bf16[64,2560]{1,0:T(8,128)(2,1)S(1)}, bf16[64,2560]{1,0:T(8,128)(2,1)S(1)}, u32[]{:S(2)}, u32[]{:S(2)}) collective-permute-start(bf16[64,2560]{1,0:T(8,128)(2,1)S(1)} %get-tuple-element.30), channel_id=1, source_target_pairs={{0,2},{1,3},{2,0},{3,1},{4,6},{5,7},{6,4},{7,5},{8,10},{9,11},{10,... | collective-permute-start | bytes 983048 | tf_op jit(solution)/shard_map/ppermute | solution.py:270
  45.7 12.1 %collective-permute-start.15 = (bf16[128,1536]{1,0:T(8,128)(2,1)S(1)}, bf16[128,1536]{1,0:T(8,128)(2,1)S(1)}, u32[]{:S(2)}, u32[]{:S(2)}) collective-permute-start(bf16[128,1536]{1,0:T(8,128)(2,1)S(1)} %pad_maximum_fusion), channel_id=1, source_target_pairs={{0,8},{8,16},{16,24},{24,0},{1,9},{9,17},{17,25},{25,1},{2,10},{10... | collective-permute-start | bytes 1179656 | tf_op jit(solution)/shard_map/ppermute | solution.py:275
  48.6 8.8 %collective-permute-start.16 = (bf16[64,1536]{1,0:T(8,128)(2,1)S(1)}, bf16[64,1536]{1,0:T(8,128)(2,1)S(1)}, u32[]{:S(2)}, u32[]{:S(2)}) collective-permute-start(bf16[64,1536]{1,0:T(8,128)(2,1)S(1)} %slice.182), channel_id=1, source_target_pairs={{0,2},{1,3},{2,0},{3,1},{4,6},{5,7},{6,4},{7,5},{8,10},{9,11},{10,... | collective-permute-start | bytes 589832 | tf_op jit(solution)/shard_map/ppermute | solution.py:270
  49.3 13.5 %collective-permute-start.8 = (bf16[32,2048]{1,0:T(8,128)(2,1)S(1)}, bf16[32,2048]{1,0:T(8,128)(2,1)S(1)}, u32[]{:S(2)}, u32[]{:S(2)}) collective-permute-start(bf16[32,2048]{1,0:T(8,128)(2,1)S(1)} %get-tuple-element.46), channel_id=1, source_target_pairs={{0,4},{4,0},{1,5},{5,1},{2,6},{6,2},{3,7},{7,3},{8,12},{12,8},{9,1... | collective-permute-start | bytes 393224 | tf_op jit(solution)/shard_map/ppermute | solution.py:270
  50.2 11.1 %collective-permute-start.7 = (bf16[64,1536]{1,0:T(8,128)(2,1)S(1)}, bf16[64,1536]{1,0:T(8,128)(2,1)S(1)}, u32[]{:S(2)}, u32[]{:S(2)}) collective-permute-start(bf16[64,1536]{1,0:T(8,128)(2,1)S(1)} %get-tuple-element.43), channel_id=1, source_target_pairs={{0,2},{1,3},{2,0},{3,1},{4,6},{5,7},{6,4},{7,5},{8,10},{9,11},{10,... | collective-permute-start | bytes 589832 | tf_op jit(solution)/shard_map/ppermute | solution.py:270
  53.3 9.4 %collective-permute-start.9 = (bf16[32,2560]{1,0:T(8,128)(2,1)S(1)}, bf16[32,2560]{1,0:T(8,128)(2,1)S(1)}, u32[]{:S(2)}, u32[]{:S(2)}) collective-permute-start(bf16[32,2560]{1,0:T(8,128)(2,1)S(1)} %get-tuple-element.44), channel_id=1, source_target_pairs={{0,4},{4,0},{1,5},{5,1},{2,6},{6,2},{3,7},{7,3},{8,12},{12,8},{9,1... | collective-permute-start | bytes 491528 | tf_op jit(solution)/shard_map/ppermute | solution.py:270
  57.9 8.2 %collective-permute-start.17 = (bf16[32,6144]{1,0:T(8,128)(2,1)S(1)}, bf16[32,6144]{1,0:T(8,128)(2,1)S(1)}, u32[]{:S(2)}, u32[]{:S(2)}) collective-permute-start(bf16[32,6144]{1,0:T(8,128)(2,1)S(1)} %pad_maximum_fusion.1), channel_id=1, source_target_pairs={{0,1},{1,0},{2,3},{3,2},{4,5},{5,4},{6,7},{7,6},{8,9},{9,8},{10,11... | collective-permute-start | bytes 1179656 | tf_op jit(solution)/shard_map/ppermute | solution.py:270
  61.4 4.7 %collective-permute-start.10 = (bf16[32,1536]{1,0:T(8,128)(2,1)S(1)}, bf16[32,1536]{1,0:T(8,128)(2,1)S(1)}, u32[]{:S(2)}, u32[]{:S(2)}) collective-permute-start(bf16[32,1536]{1,0:T(8,128)(2,1)S(1)} %get-tuple-element.54), channel_id=1, source_target_pairs={{0,4},{4,0},{1,5},{5,1},{2,6},{6,2},{3,7},{7,3},{8,12},{12,8},{9,1... | collective-permute-start | bytes 294920 | tf_op jit(solution)/shard_map/ppermute | solution.py:270
